TPU v7x, 32 devices: a whole 2x2x4 slice. The times are simulated.
32 devices in a mesh: ctx: 8 (over z, x), shard: 4 (over y, core).
Axes of the slice: x: 2, y: 2, z: 4, core: 2. Of those that a mesh axis runs over, the one named last changes fastest.
Arguments:
- block_input: bfloat16 [4, 1024, 576], P('shard', 'ctx'), may hold values from -6 to 6
- out_grad: bfloat16 [4, 1024, 576], P('shard', 'ctx'), may hold values from -6 to 6
- positions: int32 [1024], P('ctx'), may hold values from 0 to 1023, as said below
- norm_gains: bfloat16 [2, 576], P(None, 'shard'), may hold values from 0.25 to 1.75
- w_query: bfloat16 [576, 576], P('shard'), may hold values from -0.25 to 0.25
- w_kv: bfloat16 [2, 576, 192], P(None, 'shard'), may hold values from -0.25 to 0.25
- w_out: bfloat16 [576, 576], P('shard'), may hold values from -2 to 2
- w_gate_up: bfloat16 [2, 576, 1536], P(None, 'shard'), may hold values from -0.25 to 0.25
- w_down: bfloat16 [1536, 576], P('shard'), may hold values from -0.15625 to 0.15625
- mom_gains: float32 [2, 576], P(None, 'shard')
- mom_query: float32 [576, 576], P('shard')
- mom_kv: float32 [2, 576, 192], P(None, 'shard')
- mom_out: float32 [576, 576], P('shard')
- mom_gate_up: float32 [2, 576, 1536], P(None, 'shard')
- mom_down: float32 [1536, 576], P('shard')
Outputs:
- block_output: float32 [4, 1024, 576], P('shard', 'ctx')
- input_grad: float32 [4, 1024, 576], P('shard', 'ctx')
- grad_gains: float32 [2, 576], P(None, 'shard')
- grad_query: float32 [576, 576], P('shard')
- grad_kv: float32 [2, 576, 192], P(None, 'shard')
- grad_out: float32 [576, 576], P('shard')
- grad_gate_up: float32 [2, 576, 1536], P(None, 'shard')
- grad_down: float32 [1536, 576], P('shard')
- moment_gains: float32 [2, 576], P(None, 'shard')
- moment_query: float32 [576, 576], P('shard')
- moment_kv: float32 [2, 576, 192], P(None, 'shard')
- moment_out: float32 [576, 576], P('shard')
- moment_gate_up: float32 [2, 576, 1536], P(None, 'shard')
- moment_down: float32 [1536, 576], P('shard')
- momentum_norms: float32 [7], replicated
- new_gains: float32 [2, 576], P(None, 'shard')
- new_query: float32 [576, 576], P('shard')
- new_kv: float32 [2, 576, 192], P(None, 'shard')
- new_out: float32 [576, 576], P('shard')
- new_gate_up: float32 [2, 576, 1536], P(None, 'shard')
- new_down: float32 [1536, 576], P('shard')
Inputs may be any that keep to these rules, and one draw needn't show every extreme that they name: Each device's 128 entries are consecutive positions in rising order; all entries together are 0 to 1023, each once.
All inputs are finite; a program needn't handle non-finite values.
Results may differ from a plain program's by a relative error of at most 0.023.
Values may be sent and summed in bfloat16 or wider, within the bound.
No kernel may reach another device: no remote copies, remote signals or barrier semaphores. Data moves between devices by JAX's collectives and lax.ppermute only.
A program may use at most 192 MiB of HBM per device.

v0:
```python
import functools
import math

import jax
import jax.numpy as jnp
from jax import lax
from jax.experimental import pallas as pl
from jax.experimental.pallas import tpu as pltpu
from jax.sharding import Mesh
from jax.sharding import PartitionSpec as P

D = 576
FF = 1536
HEAD_DIM = 64
HEADS = 9
KV_HEADS = 3
GROUPS = 3
KV_WIDTH = 192
NS_STEPS = 5
NS_A = 3.4445
NS_B = -4.775
NS_C = 2.0315
NORM_EPS = 1e-05
MOMENTUM = 0.95
RATE = 0.2
SHAPE_SCALE = 0.2
GAIN_RATE = 0.02
NEG_LARGE = -1e30

bf16 = jnp.bfloat16
f32 = jnp.float32
SHARD = ("y", "core")
LO = ("lh", "lx")
OWNER = ("lx", "core")
CTX = ("hi", "lh", "lx")
ALL = ("hi", "lh", "lx", "y", "core")
TRADE = ((0, 1), (1, 0))


def dot(left, right):
    return jnp.dot(left, right, preferred_element_type=f32)


def dot_cols(left, right):
    return lax.dot_general(left, right, (((1,), (1,)), ((), ())), preferred_element_type=f32)


def dot_rows(left, right):
    return lax.dot_general(left, right, (((0,), (0,)), ((), ())), preferred_element_type=f32)


def call(body, outs, args, scratch=(), smem=(), hold=(), limit=64):
    count = len(args)
    spaces = [pltpu.SMEM if i in smem else pltpu.VMEM for i in range(count)]
    spaces += [pl.ANY] * len(hold)

    def run(*refs):
        body(*refs[:count], *refs[count + len(hold) :])

    return pl.pallas_call(
        run,
        name=getattr(body, "func", body).__name__,
        out_shape=[jax.ShapeDtypeStruct(s, d) for s, d in outs],
        in_specs=[pl.BlockSpec(memory_space=space) for space in spaces],
        out_specs=[pl.BlockSpec(memory_space=pltpu.VMEM) for _ in outs],
        scratch_shapes=list(scratch),
        compiler_params=pltpu.CompilerParams(vmem_limit_bytes=limit * 2**20),
        cost_estimate=pl.CostEstimate(flops=0, bytes_accessed=1024, transcendentals=0),
    )(*args, *hold)


def after(x, *hold):
    return pl.pallas_call(
        lambda *refs: None,
        name="after",
        out_shape=jax.ShapeDtypeStruct(x.shape, x.dtype),
        in_specs=[pl.BlockSpec(memory_space=pl.ANY)] * (1 + len(hold)),
        out_specs=pl.BlockSpec(memory_space=pl.ANY),
        input_output_aliases={0: 0},
        cost_estimate=pl.CostEstimate(flops=0, bytes_accessed=1024, transcendentals=0),
    )(x, *hold)


def turn(chunk, cosine, sine):
    lane = lax.broadcasted_iota(jnp.int32, chunk.shape, 1)
    other = jnp.where(lane % 64 < 32, pltpu.roll(chunk, 96, 1), pltpu.roll(chunk, 32, 1))
    return chunk * cosine + other * sine


def turn_wide(rows, cosine, sine):
    width = rows.shape[1]
    parts = []
    for at in range(0, width, 128):
        if at + 128 <= width:
            parts.append(turn(rows[:, at : at + 128], cosine, sine))
        else:
            tail = rows[:, at:]
            parts.append(turn(jnp.concatenate([tail, tail], axis=1), cosine, sine)[:, :64])
    return jnp.concatenate(parts, axis=1)


def inverse_rms(rows):
    return lax.rsqrt(jnp.mean(rows * rows, axis=1, keepdims=True) + NORM_EPS)


def pack_body(tok, pos_ref, x_ref, gains_ref, wq_ref, wkv_ref, xs_ref, packed_ref):
    rows = wq_ref.shape[0]
    xs_ref[0:tok, :] = x_ref[...].T
    base = (pos_ref[0] // tok).astype(f32)
    xs_ref[tok:, :] = jnp.full((8, D), base, f32).astype(bf16)
    packed_ref[0:rows, 0:KV_WIDTH] = wkv_ref[0]
    packed_ref[0:rows, KV_WIDTH : 2 * KV_WIDTH] = wkv_ref[1]
    packed_ref[0:rows, 2 * KV_WIDTH :] = wq_ref[...]
    packed_ref[rows:, :] = jnp.zeros((8, packed_ref.shape[1]), bf16)
    packed_ref[rows : rows + 2, 0:rows] = gains_ref[...]


def pack_wide_body(me_ref, wgu_ref, *out_refs):
    me = me_ref[0]
    part = wgu_ref.shape[2] // len(out_refs)
    for j, out_ref in enumerate(out_refs):
        at = pl.multiple_of((me ^ j) * part, 128)
        out_ref[:, 0:part] = wgu_ref[0, :, pl.ds(at, part)]
        out_ref[:, part : 2 * part] = wgu_ref[1, :, pl.ds(at, part)]


def project_body(
    tok, me_ref, xs_ref, p0, p1, p2, p3, cos_ref, sin_ref,
    attn_in_ref, q_ref, kv_ref, w_ref, gains_ref, pieces,
):
    me = me_ref[0]
    rows = p0.shape[0] - 8
    for j, piece in enumerate((p0, p1, p2, p3)):
        at = me ^ j
        w_ref[pl.ds(pl.multiple_of(at * rows, 16), rows), :] = piece[0:rows, :]
        pieces[at] = piece[rows:, 0:256].astype(f32)
    gains = jnp.concatenate([pieces[t, :, 0:rows] for t in range(4)], axis=1)
    gains_ref[...] = gains
    x = xs_ref[0:tok, :].astype(f32)
    attn_in = (x * inverse_rms(x) * gains[0:1, :]).astype(bf16)
    attn_in_ref[...] = attn_in
    cosine, sine = cos_ref[...], sin_ref[...]
    keys_values = dot(attn_in, w_ref[:, 0 : 2 * KV_WIDTH])
    key = turn_wide(keys_values[:, 0:KV_WIDTH], cosine, sine).astype(bf16)
    value = keys_values[:, KV_WIDTH:].astype(bf16)
    for t in range(kv_ref.shape[0]):
        kv_ref[t, 0:tok, 0:KV_WIDTH] = key
        kv_ref[t, 0:tok, KV_WIDTH:] = value
        kv_ref[t, tok:, :] = xs_ref[tok:, 0 : 2 * KV_WIDTH]
    query = dot(attn_in, w_ref[:, 2 * KV_WIDTH :])
    q_ref[...] = turn_wide(query, cosine, sine).astype(bf16) * jnp.asarray(0.125, bf16)


def group_rows(rows, group):
    return jnp.concatenate(
        [
            rows[:, (GROUPS * group + i) * HEAD_DIM : (GROUPS * group + i + 1) * HEAD_DIM]
            for i in range(GROUPS)
        ],
        axis=0,
    )


def ungroup(groups, tok):
    return jnp.concatenate(
        [g[i * tok : (i + 1) * tok, :] for g in groups for i in range(GROUPS)], axis=1
    )


def each_block(count, visit):
    if count <= 8:
        for j in range(count):
            visit(j)
    else:
        lax.fori_loop(0, count, lambda j, c: (visit(j), c)[1], 0)


def attend_body(
    tok, blocks, me_ref, xg_ref, q_ref, kv_ref, p0, p1, p2, p3, gains_ref,
    wo_ref, attn_f_ref, ffn_ref, rows_ref, middle_ref, lse_ref, scores_ref, peak_ref, total_ref, mixed_ref,
):
    wide = GROUPS * tok
    for j, piece in enumerate((p0, p1, p2, p3)):
        rows = piece.shape[0]
        wo_ref[pl.ds(pl.multiple_of((me_ref[0] ^ j) * rows, 16), rows), :] = piece[...]
    x = xg_ref[0:tok, :].astype(f32)
    query_base = xg_ref[tok : tok + 1, 0:1].astype(f32) * tok
    row = lax.broadcasted_iota(jnp.int32, (tok, wide), 0)
    col = lax.broadcasted_iota(jnp.int32, (tok, wide), 1) % tok
    ahead = (row - col).astype(f32)
    q = q_ref[...]
    queries = [group_rows(q, g) for g in range(KV_HEADS)]
    peak_ref[...] = jnp.full(peak_ref.shape, NEG_LARGE, f32)
    total_ref[...] = jnp.zeros(total_ref.shape, f32)
    mixed_ref[...] = jnp.zeros(mixed_ref.shape, f32)

    def first(j):
        allowed = ahead <= query_base - kv_ref[j, tok : tok + 1, 0:1].astype(f32) * tok
        for g in range(KV_HEADS):
            s = dot_cols(kv_ref[j, 0:tok, g * HEAD_DIM : (g + 1) * HEAD_DIM], queries[g])
            s = jnp.where(allowed, s, NEG_LARGE)
            scores_ref[g, j] = s
            peak_ref[g : g + 1, :] = jnp.maximum(
                peak_ref[g : g + 1, :], jnp.max(s, axis=0, keepdims=True)
            )

    each_block(blocks, first)

    def second(j):
        for g in range(KV_HEADS):
            p = jnp.exp(scores_ref[g, j] - peak_ref[g : g + 1, :])
            total_ref[g : g + 1, :] += jnp.sum(p, axis=0, keepdims=True)
            at = KV_WIDTH + g * HEAD_DIM
            mixed_ref[g] += dot_rows(kv_ref[j, 0:tok, at : at + HEAD_DIM], p.astype(bf16))

    each_block(blocks, second)
    lse_ref[...] = peak_ref[...] + jnp.log(total_ref[...])
    attn_f = ungroup(
        [(mixed_ref[g] / total_ref[g : g + 1, :]).T for g in range(KV_HEADS)], tok
    )
    attn_f_ref[...] = attn_f
    attn_rows = attn_f.astype(bf16)
    middle = x + dot(attn_rows, wo_ref[...])
    middle_ref[...] = middle
    ffn_ref[...] = (middle * inverse_rms(middle) * gains_ref[1:2, :]).astype(bf16)
    rows_ref[...] = attn_rows


def feed_body(
    me_ref, lo_ref, ffn_ref, g0, g1, g2, g3, p0, p1, p2, p3, wd_ref, in_ref, rows_ref,
    m0, m1, m2, m3, dffn_ref, *rest,
):
    grad_refs, (cot_ref, wgu_ref, whole_ref, out_ref) = rest[:-4], rest[-4:]
    part = wd_ref.shape[1]
    tok = g0.shape[1]
    me, lo = me_ref[0], lo_ref[0]
    for j, piece in enumerate((g0, g1, g2, g3)):
        cot_ref[:, pl.ds(pl.multiple_of((me ^ j) * tok, 128), tok)] = piece[...]
    for j, piece in enumerate((p0, p1, p2, p3)):
        rows = piece.shape[0]
        wgu_ref[pl.ds(pl.multiple_of((me ^ j) * rows, 16), rows), :] = piece[...]
    ffn_in = ffn_ref[...]
    cotangent = cot_ref[...]
    wgu = wgu_ref[...]
    wd = wd_ref[...]
    gate_up = dot(ffn_in, wgu)
    gate, up = gate_up[:, :part], gate_up[:, part:]
    sigma = jax.nn.sigmoid(gate)
    swish = gate * sigma
    hidden = (swish * up).astype(bf16)
    d_hidden = dot_rows(cotangent, wd)
    d_gate = (d_hidden * up * sigma * (1.0 + gate * (1.0 - sigma))).astype(bf16)
    d_up = (d_hidden * swish).astype(bf16)
    both = jnp.concatenate([d_gate, d_up], axis=1)
    dffn = dot_cols(both, wgu).astype(bf16)
    out = dot_cols(hidden, wd).astype(bf16)
    for s in range(4):
        dffn_ref[s, 0:tok, :] = dffn[s * tok : (s + 1) * tok, :]
        out_ref[s] = out[s * tok : (s + 1) * tok, :]
    for j, send in enumerate((m0, m1, m2, m3)):
        send[0:tok, :] = out_ref[me ^ j]
        send[tok:, :] = jnp.where((me ^ j) == 2, rows_ref[...], in_ref[...])
    gu_grad = dot_rows(ffn_in, both).astype(bf16)
    down_grad = dot(cotangent, hidden).astype(bf16)
    height = whole_ref.shape[1]
    for t in range(whole_ref.shape[0]):
        whole_ref[t, :, 0 : 2 * part] = gu_grad[t * height : (t + 1) * height, :]
        whole_ref[t, :, 2 * part :] = down_grad[t * height : (t + 1) * height, :]
    for k, grad_ref in enumerate(grad_refs):
        grad_ref[...] = whole_ref[lo ^ k]


def old_body(
    me_ref, flags_ref, mq_ref, mkv_ref, mo_ref, mgu_ref, md_ref, q0, q1, q2, q3, same_ref, other_ref
):
    me, lx, core = me_ref[0], flags_ref[0], flags_ref[1]
    rows = mq_ref.shape[0]
    blank = jnp.zeros((rows, D - KV_WIDTH), f32)
    key = jnp.concatenate([mkv_ref[0], blank], axis=1).astype(bf16)
    value = jnp.concatenate([mkv_ref[1], blank], axis=1).astype(bf16)
    query, out = mq_ref[...].astype(bf16), mo_ref[...].astype(bf16)
    for j, old in enumerate((q0, q1, q2, q3)):
        to = me ^ j
        old[...] = jnp.where(
            to == 0, query, jnp.where(to == 1, key, jnp.where(to == 2, out, value))
        )
    part = md_ref.shape[1]

    @pl.when(lx == 0)
    def _():
        for b in range(4):
            at = slice(b * part, (b + 1) * part)
            gate, up = mgu_ref[0, :, at].astype(bf16), mgu_ref[1, :, at].astype(bf16)
            same_ref[b * rows : (b + 1) * rows, :] = jnp.where(core == 0, gate, up)
            other_ref[b * rows : (b + 1) * rows, :] = jnp.where(core == 0, up, gate)

    @pl.when(lx != 0)
    def _():
        down = md_ref[...].astype(bf16)
        up = jnp.concatenate(
            [mgu_ref[1, :, b * part : (b + 1) * part].astype(bf16) for b in range(4)], axis=0
        )
        same_ref[...] = jnp.where(core == 0, down, up)
        other_ref[...] = jnp.where(core == 0, up, down)


def add_pieces_body(*refs):
    total = refs[0][...].astype(f32)
    for piece in refs[1:-1]:
        total = total + piece[...].astype(f32)
    refs[-1][...] = total.astype(bf16)


def add_slots_body(part, total_ref, got_ref, slots_ref):
    total = (total_ref[...].astype(f32) + got_ref[...].astype(f32)).astype(bf16)
    for lx in range(2):
        for core in range(2):
            number = 1 if core == 1 else 2 * lx
            piece = total[:, number * part : (number + 1) * part]
            for lh in range(slots_ref.shape[0]):
                slots_ref[lh, lx, core] = piece


def back_body(
    tok, blocks, dffn_ref, xg_ref, g_ref, middle_ref, gains_ref, wo_ref, attn_f_ref, q_ref, kv_ref,
    lse_ref, cos_ref, sin_ref,
    dmid_ref, dq_ref, dbranch_ref, dkv_ref, gain_ref, dq_acc,
):
    wide = GROUPS * tok
    query_base = xg_ref[tok : tok + 1, 0:1].astype(f32) * tok
    middle = middle_ref[...]
    inverse = inverse_rms(middle)
    normed = middle * inverse
    d_in = dffn_ref[0, 0:tok, :].astype(f32)
    for i in range(1, dffn_ref.shape[0]):
        d_in = d_in + dffn_ref[i, 0:tok, :].astype(f32)
    gain_ref[...] = jnp.sum(d_in * normed, axis=0, keepdims=True)
    scaled = d_in * gains_ref[1:2, :]
    d_middle = g_ref[...].astype(f32).T + inverse * (
        scaled - normed * jnp.mean(scaled * normed, axis=1, keepdims=True)
    )
    dmid_ref[...] = d_middle
    d_branch = d_middle.astype(bf16)
    dbranch_ref[...] = d_branch
    d_attn = dot_cols(d_branch, wo_ref[...]).astype(bf16)
    attn_f = attn_f_ref[...]
    row = lax.broadcasted_iota(jnp.int32, (tok, wide), 0)
    col = lax.broadcasted_iota(jnp.int32, (tok, wide), 1) % tok
    ahead = (row - col).astype(f32)
    q = q_ref[...]
    queries = [group_rows(q, g) for g in range(KV_HEADS)]
    outs = [group_rows(d_attn, g) for g in range(KV_HEADS)]
    product = d_attn.astype(f32) * attn_f
    deltas = [
        jnp.sum(group_rows(product, g).T, axis=0, keepdims=True) for g in range(KV_HEADS)
    ]
    dq_acc[...] = jnp.zeros(dq_acc.shape, f32)

    def visit(j):
        allowed = ahead <= query_base - kv_ref[j, tok : tok + 1, 0:1].astype(f32) * tok
        d_keys, d_values = [], []
        for g in range(KV_HEADS):
            at = KV_WIDTH + g * HEAD_DIM
            key = kv_ref[j, 0:tok, g * HEAD_DIM : (g + 1) * HEAD_DIM]
            value = kv_ref[j, 0:tok, at : at + HEAD_DIM]
            s = dot_cols(key, queries[g])
            p = jnp.where(allowed, jnp.exp(s - lse_ref[g : g + 1, :]), 0.0)
            d_weight = dot_cols(value, outs[g])
            ds = (p * (d_weight - deltas[g])).astype(bf16)
            d_values.append(dot(p.astype(bf16), outs[g]))
            d_keys.append(dot(ds, queries[g]))
            dq_acc[g] += dot_rows(key, ds)
        dkv_ref[j] = jnp.concatenate(d_keys + d_values, axis=1).astype(bf16)

    each_block(blocks, visit)
    d_query = ungroup([dq_acc[g].T * 0.125 for g in range(KV_HEADS)], tok)
    dq_ref[...] = turn_wide(d_query, cos_ref[...], -sin_ref[...]).astype(bf16)


def input_body(
    tok, rows, me_ref, dkv_ref, xg_ref, dmid_ref, gains_ref, w_ref, dq_ref, dbranch_ref, gain_two_ref,
    cos_ref, sin_ref, dx_ref, s0, s1, s2, s3, send_ref,
):
    total = dkv_ref[0].astype(f32)
    for i in range(1, dkv_ref.shape[0]):
        total = total + dkv_ref[i].astype(f32)
    d_key = turn_wide(total[:, :KV_WIDTH], cos_ref[...], -sin_ref[...]).astype(bf16)
    d_value = total[:, KV_WIDTH:].astype(bf16)
    cat = jnp.concatenate([d_key, d_value, dq_ref[...]], axis=1)
    d_in = dot_cols(cat, w_ref[...])
    x = xg_ref[0:tok, :].astype(f32)
    inverse = inverse_rms(x)
    normed = x * inverse
    gain_one = jnp.sum(d_in * normed, axis=0, keepdims=True)
    scaled = d_in * gains_ref[0:1, :]
    dx_ref[...] = dmid_ref[...] + inverse * (
        scaled - normed * jnp.mean(scaled * normed, axis=1, keepdims=True)
    )
    gain_two = gain_two_ref[...]
    blank = jnp.zeros((tok, D - KV_WIDTH), bf16)
    columns = (
        dq_ref[...], jnp.concatenate([d_key, blank], axis=1), dbranch_ref[...],
        jnp.concatenate([d_value, blank], axis=1),
    )
    for s, column in enumerate(columns):
        send_ref[s, 0:tok, :] = column
        pair = jnp.concatenate(
            [
                gain_one[:, s * rows : (s + 1) * rows],
                gain_two[:, s * rows : (s + 1) * rows],
                jnp.zeros((6, rows), f32),
            ],
            axis=0,
        )
        send_ref[s, tok:, :] = jnp.concatenate(
            [pair, jnp.zeros((8, D - rows), f32)], axis=1
        ).astype(bf16)
    for j, out_ref in enumerate((s0, s1, s2, s3)):
        out_ref[...] = send_ref[me_ref[0] ^ j]


def finish_body(tok, middle_ref, dx_ref, m0, m1, m2, m3, out_ref):
    output = middle_ref[...]
    for piece in (m0, m1, m2, m3):
        output = output + piece[0:tok, :].astype(f32)
    out_ref[0] = output.T.astype(bf16)
    out_ref[1] = dx_ref[...].T.astype(bf16)


def attn_grad_body(tok, me_ref, lo_ref, r0, r1, r2, r3, m0, m1, m2, m3, *rest):
    out_refs, (rows_ref, cols_ref, whole_ref) = rest[:-3], rest[-3:]
    me, lo = me_ref[0], lo_ref[0]
    gain = jnp.zeros((8, D), f32)
    for j, (cols, piece) in enumerate(((r0, m0), (r1, m1), (r2, m2), (r3, m3))):
        rows_ref[j * tok : (j + 1) * tok, :] = piece[tok:, :]
        cols_ref[j * tok : (j + 1) * tok, :] = cols[0:tok, :]
        gain = gain + cols[tok:, :].astype(f32)
    grad = dot_rows(cols_ref[...], rows_ref[...]).astype(bf16)
    gain = gain.astype(bf16)
    height = whole_ref.shape[1] - 8
    for t in range(whole_ref.shape[0]):
        whole_ref[t, 0:height, :] = grad[t * height : (t + 1) * height, :]
        whole_ref[t, height:, :] = gain
    for k, out_ref in enumerate(out_refs):
        out_ref[...] = whole_ref[lo ^ k]


def add_second_body(total_ref, got_ref, slots_ref, gain_ref):
    total = total_ref[...].astype(f32) + got_ref[...].astype(f32)
    height = slots_ref.shape[1]
    piece = total[0:height, :].astype(bf16)
    for t in range(slots_ref.shape[0]):
        slots_ref[t] = piece
    gain_ref[...] = total[height:, :]


def each_rows(n, block, visit, carry):
    def step(i, value):
        at = pl.multiple_of(i * block, 16)
        return visit(at, pl.ds(at, block), value)

    return lax.fori_loop(0, n // block, step, carry)


def sum_all(rows):
    return jnp.sum(jnp.sum(rows, axis=0, keepdims=True), axis=1, keepdims=True)


def sweeps(z_ref, zb_ref, rest_ref, rest_b_ref, poly_ref, squares, count, block, steps):
    n = z_ref.shape[0]
    row = lax.broadcasted_iota(jnp.int32, (block, n), 0)
    col = lax.broadcasted_iota(jnp.int32, (block, n), 1)

    def sweep(_, squares):
        center = squares / count
        slope = NS_B + 2.0 * NS_C * center
        lead = NS_A + NS_B * center + NS_C * center * center

        def first(at, here):
            gram = dot_cols(zb_ref[here, :], zb_ref[...])
            mine = jnp.logical_and(row + at == col, (row + at).astype(f32) < count)
            rest = jnp.where(mine, gram - center, gram)
            rest_ref[here, :] = rest
            rest_b_ref[here, :] = rest.astype(bf16)

        def second(at, here):
            square = dot(rest_b_ref[here, :], rest_b_ref[...])
            poly_ref[here, :] = (NS_C * square + slope * rest_ref[here, :]).astype(bf16)

        def third(at, here, total):
            z = lead * z_ref[here, :] + dot(poly_ref[here, :], zb_ref[...])
            z_ref[here, :] = z
            return total + sum_all(z * z)

        for at in range(0, n, block):
            first(at, slice(at, at + block))
        for at in range(0, n, block):
            second(at, slice(at, at + block))
        total = jnp.zeros((1, 1), f32)
        for at in range(0, n, block):
            total = third(at, slice(at, at + block), total)
        zb_ref[...] = z_ref[...].astype(bf16)
        return total

    return lax.fori_loop(0, steps, sweep, squares)


def normalize(z_ref, zb_ref):
    n = z_ref.shape[0]
    total = each_rows(
        n, 48, lambda at, here, total: total + sum_all(z_ref[here, :] * z_ref[here, :]),
        jnp.zeros((1, 1), f32),
    )
    scale = 1.0 / (jnp.sqrt(total) + 1e-07)

    def visit(at, here, carry):
        z = z_ref[here, :] * scale
        z_ref[here, :] = z
        zb_ref[here, :] = z.astype(bf16)
        return carry

    each_rows(n, 48, visit, 0)
    return total, total * scale * scale


def norm_rows(total, entries, shape):
    value = jnp.broadcast_to(jnp.sqrt(total / entries), shape)
    high = value.astype(bf16).astype(f32)
    row = lax.broadcasted_iota(jnp.int32, shape, 0)
    return jnp.where(row == 0, high, value - high).astype(bf16)


def feed_ns_body(
    flags_ref, near_ref, far_ref, o0, o1, o2, o3, same_ref, other_ref,
    z_ref, g_ref, zb_ref, rest_ref, rest_b_ref, poly_ref,
):
    core, y, rowwise, me = flags_ref[1], flags_ref[2], flags_ref[3] == 1, flags_ref[4]
    n_lo, _, height, part = near_ref.shape
    parts = 4
    rows = D // parts
    for t in range(n_lo):
        for c in range(2):
            here = slice(t * height, (t + 1) * height)
            near = pl.ds(pl.multiple_of((2 * y + c) * part, 128), part)
            far = pl.ds(pl.multiple_of((2 * (1 - y) + c) * part, 128), part)
            g_ref[here, near] = near_ref[t, c]
            g_ref[here, far] = far_ref[t, c]
    for j, old_ref in enumerate((o0, o1, o2, o3)):
        s = me ^ j

        @pl.when(rowwise)
        def _():
            for b in range(parts):
                z_ref[pl.ds(pl.multiple_of(s * rows, 16), rows), b * part : (b + 1) * part] = (
                    MOMENTUM * old_ref[b * rows : (b + 1) * rows, :].astype(f32)
                )

        @pl.when(jnp.logical_not(rowwise))
        def _():
            z_ref[:, pl.ds(pl.multiple_of(s * part, 128), part)] = MOMENTUM * old_ref[...].astype(f32)


    def add(at, here, carry):
        z_ref[here, :] += g_ref[here, :].astype(f32)
        return carry

    each_rows(D, 48, add, 0)
    total, squares = normalize(z_ref, zb_ref)
    sweeps(
        z_ref, zb_ref, rest_ref, rest_b_ref, poly_ref, squares, jnp.float32(D), D // 2, NS_STEPS
    )
    norm = norm_rows(total, jnp.float32(D * parts * part), (8, part))
    for out_ref, to in ((same_ref, core), (other_ref, 1 - core)):
        s = 2 * y + to
        out_ref[D : D + 8, :] = norm
        for first, source in ((0, zb_ref), (D + 8, g_ref)):

            @pl.when(rowwise)
            def _():
                for b in range(parts):
                    out_ref[first + b * rows : first + (b + 1) * rows, :] = source[
                        pl.ds(pl.multiple_of(s * rows, 16), rows), b * part : (b + 1) * part
                    ]

            @pl.when(jnp.logical_not(rowwise))
            def _():
                out_ref[first : first + D, :] = source[
                    :, pl.ds(pl.multiple_of(s * part, 128), part)
                ]


def attn_old_body(me_ref, m0, m1, m2, m3, out_ref, old_ref):
    rows = m0.shape[0]
    for j, piece in enumerate((m0, m1, m2, m3)):
        old_ref[pl.ds(pl.multiple_of((me_ref[0] ^ j) * rows, 16), rows), :] = piece[...]
    out_ref[...] = MOMENTUM * old_ref[...].T.astype(f32)


def attn_ns_body(
    me_ref, grad_ref, old_ref, out_ref, z_ref, zb_ref, rest_ref, rest_b_ref, poly_ref
):
    n_lo, height, _ = grad_ref.shape
    rows = D // 4
    for t in range(n_lo):
        zb_ref[t * height : (t + 1) * height, :] = grad_ref[t]
    count = jnp.where(me_ref[0] % 2 == 0, float(D), float(KV_WIDTH))
    grad_rows = zb_ref[...].T
    for s in range(4):
        out_ref[s, rows : 2 * rows, :] = grad_rows[s * rows : (s + 1) * rows, :]
    z_ref[...] = old_ref[...] + zb_ref[...].astype(f32)
    total, squares = normalize(z_ref, zb_ref)
    sweeps(z_ref, zb_ref, rest_ref, rest_b_ref, poly_ref, squares, count, D, NS_STEPS)
    ortho = zb_ref[...].T
    norm = norm_rows(total, count * D, (8, D))
    for s in range(4):
        out_ref[s, 0:rows, :] = ortho[s * rows : (s + 1) * rows, :]
        out_ref[s, 2 * rows :, :] = norm


def feed_new_body(
    flags_ref, own, core_ref, even, odd, mgu_ref, md_ref, wgu_ref, wd_ref,
    ggu_ref, gd_ref, ngu_ref, nd_ref, ugu_ref, ud_ref, norm_ref,
):
    lx, core = flags_ref[0], flags_ref[1]
    rate = -RATE * SHAPE_SCALE * math.sqrt(FF)
    rows = mgu_ref.shape[1]
    part = md_ref.shape[1]

    def pick(number, piece):
        if number == 1:
            return jnp.where(core == 1, own[piece, :], core_ref[piece, :]).astype(f32)
        near = jnp.where(core == 0, own[piece, :], core_ref[piece, :])
        far = jnp.where(core == 0, even[piece, :], odd[piece, :])
        return jnp.where(lx == number // 2, near, far).astype(f32)

    for number in range(2):
        for b in range(4):
            at = slice(b * part, (b + 1) * part)
            ortho = pick(number, slice(b * rows, (b + 1) * rows))
            grad = pick(number, slice(D + 8 + b * rows, D + 8 + (b + 1) * rows))
            ggu_ref[number, :, at] = grad
            ngu_ref[number, :, at] = MOMENTUM * mgu_ref[number, :, at] + grad
            ugu_ref[number, :, at] = wgu_ref[number, :, at].astype(f32) + rate * ortho
    grad = pick(2, slice(D + 8, 2 * D + 8))
    gd_ref[...] = grad
    nd_ref[...] = MOMENTUM * md_ref[...] + grad
    ud_ref[...] = wd_ref[...].astype(f32) + rate * pick(2, slice(0, D))
    for number in range(3):
        norm_ref[number] = pick(number, slice(D, D + 8))


def attn_new_body(
    back_ref, feed_norm_ref, wq_ref, wkv_ref, wo_ref, mq_ref, mkv_ref, mo_ref,
    gq, gkv, go, nq, nkv, no, uq, ukv, uo, norm_ref,
):
    rate = -RATE * SHAPE_SCALE * math.sqrt(D)
    rows = wq_ref.shape[0]

    def update(number, width, weight, old):
        ortho = back_ref[number, 0:rows, 0:width].astype(f32)
        grad = back_ref[number, rows : 2 * rows, 0:width].astype(f32)
        return grad, MOMENTUM * old + grad, weight.astype(f32) + rate * ortho

    gq[...], nq[...], uq[...] = update(0, D, wq_ref[...], mq_ref[...])
    go[...], no[...], uo[...] = update(2, D, wo_ref[...], mo_ref[...])
    for i, number in enumerate((1, 3)):
        gkv[i], nkv[i], ukv[i] = update(number, KV_WIDTH, wkv_ref[i], mkv_ref[i])
    lane = lax.broadcasted_iota(jnp.int32, (1, 128), 1)
    norms = jnp.zeros((1, 128), f32)
    for i, number in enumerate((0, 1, 3, 2)):
        pair = back_ref[number, 2 * rows :, 0:1].astype(f32)
        norms = jnp.where(lane == i, pair[0:1] + pair[1:2], norms)
    for i in range(3):
        pair = feed_norm_ref[i, :, 0:1]
        norms = jnp.where(lane == 4 + i, pair[0:1] + pair[1:2], norms)
    norm_ref[...] = norms


def trade(x, axis):
    return lax.ppermute(x, axis, TRADE)


def pass_on(x, axis, size, j):
    return lax.ppermute(x, axis, [(i, i ^ j) for i in range(size)])


def spread(x, axis, size):
    return deal(jnp.broadcast_to(x[None], (size,) + x.shape), axis)


def deal(x, axis):
    return lax.all_to_all(x, axis, 0, 0, tiled=True)


def on_device(
    n_hi, n_lo, block_input, out_grad, positions, norm_gains, w_query, w_kv, w_out, w_gate_up,
    w_down, mom_gains, mom_query, mom_kv, mom_out, mom_gate_up, mom_down,
):
    tok = block_input.shape[1]
    rows = w_query.shape[0]
    part = w_down.shape[0]
    n_shard = 4
    n_ctx = n_hi * n_lo
    blocks = 2 * n_lo
    wide = GROUPS * tok
    height = D // n_lo
    at_lx, at_y, at_core = lax.axis_index("lx"), lax.axis_index("y"), lax.axis_index("core")
    me = (at_y * 2 + at_core).astype(jnp.int32)
    lo = lax.axis_index(LO).astype(jnp.int32)[None]
    rowwise = jnp.where(jnp.logical_and(at_lx == 1, at_core == 0), 0, 1)
    flags = jnp.stack([at_lx, at_core, at_y, rowwise, me]).astype(jnp.int32)
    me = me[None]

    moves = []
    for hi in range(2):
        for at in range(n_lo):
            for y in range(2):
                for core in range(2):
                    moves.append(
                        (
                            ((hi * n_lo + at) * 2 + y) * 2 + core,
                            ((core * n_lo + at) * 2 + y) * 2 + hi,
                        )
                    )

    xs, packed = call(
        functools.partial(pack_body, tok),
        [((tok + 8, D), bf16), ((rows + 8, 2 * KV_WIDTH + D), bf16)],
        (positions, block_input[0].T, norm_gains, w_query, w_kv),
        smem=(0,),
    )
    xs = lax.ppermute(xs, ALL, moves)

    def gathered(x):
        far = trade(x, "y")
        return (x, trade(x, "core"), far, trade(far, "core"))

    def pass_shard(pieces):
        return (pieces[0],) + tuple(pass_on(pieces[j], SHARD, n_shard, j) for j in (1, 2, 3))

    attn_weights = gathered(packed)
    wide_parts = call(
        pack_wide_body, [((rows, 2 * part), bf16)] * n_shard, (me, w_gate_up), smem=(0,)
    )
    out_weights = gathered(w_out)
    wide_pieces = pass_shard(wide_parts)
    cot = lax.ppermute(out_grad[0].T, ALL, moves)
    cots = pass_shard((cot,) * n_shard)

    pos = xs[tok, 0].astype(f32) * tok + jnp.arange(tok, dtype=f32)
    half = HEAD_DIM // 2
    lane = jnp.arange(128)
    inverse = 1.0 / 10000.0 ** ((lane % half).astype(f32) * 2.0 / HEAD_DIM)
    angles = pos[:, None] * inverse[None, :]
    cosine = jnp.cos(angles)
    sine = jnp.sin(angles) * jnp.where(lane % HEAD_DIM < half, -1.0, 1.0)[None, :]

    attn_in, query, kv, w_kvq, gains = call(
        functools.partial(project_body, tok),
        [
            ((tok, D), bf16), ((tok, D), bf16), ((blocks, tok + 8, 2 * KV_WIDTH), bf16),
            ((D, 2 * KV_WIDTH + D), bf16), ((8, D), f32),
        ],
        (me, xs) + attn_weights + (cosine, sine),
        scratch=(pltpu.VMEM((n_shard, 8, 256), f32),),
        smem=(0,),
        hold=(wide_parts[0],) + out_weights[1:],
    )
    kv = deal(kv, LO + ("core",))
    *attn_old, old_same, old_other = call(
        old_body,
        [((rows, D), bf16)] * n_shard + [((D, part), bf16)] * 2,
        (me, flags, mom_query, mom_kv, mom_out, mom_gate_up, mom_down.T),
        smem=(0, 1),
    )
    w_o, attn_f, ffn_in, attn_rows, middle, lse = call(
        functools.partial(attend_body, tok, blocks),
        [
            ((D, D), bf16), ((tok, D), f32), ((tok, D), bf16), ((tok, D), bf16),
            ((tok, D), f32), ((KV_HEADS, wide), f32),
        ],
        (me, xs, query, kv) + out_weights + (gains,),
        scratch=(
            pltpu.VMEM((KV_HEADS, blocks, tok, wide), f32),
            pltpu.VMEM((KV_HEADS, wide), f32),
            pltpu.VMEM((KV_HEADS, wide), f32),
            pltpu.VMEM((KV_HEADS, HEAD_DIM, wide), f32),
        ),
        smem=(0,),
        hold=wide_pieces[1:] + (old_same,),
        limit=64,
    )
    ffn_all = lax.all_gather(ffn_in, SHARD, axis=0, tiled=True)
    old_same, old_other = after(old_same, ffn_all), after(old_other, ffn_all)
    attn_olds = pass_shard([attn_old[0]] + [after(old, ffn_all) for old in attn_old[1:]])
    olds = pass_shard((old_same, old_other, old_same, old_other))
    misc_0, misc_1, misc_2, misc_3, dffn_part, *feed_grads = call(
        feed_body,
        [((2 * tok, D), bf16)] * n_shard + [((n_shard, tok + 8, D), bf16)]
        + [((height, 3 * part), bf16)] * n_lo,
        (me, lo, ffn_all) + cots + wide_pieces + (w_down.T, attn_in, attn_rows),
        scratch=(
            pltpu.VMEM((D, n_shard * tok), bf16), pltpu.VMEM((D, 2 * part), bf16),
            pltpu.VMEM((n_lo, height, 3 * part), bf16), pltpu.VMEM((n_shard, tok, D), bf16),
        ),
        smem=(0, 1),
    )
    dffn = deal(dffn_part, SHARD)
    feed_got = [feed_grads[0]] + [pass_on(feed_grads[k], LO, n_lo, k) for k in range(1, n_lo)]

    misc = pass_shard((misc_0, misc_1, misc_2, misc_3))

    d_middle, d_query, d_branch, dkv, gain_two = call(
        functools.partial(back_body, tok, blocks),
        [
            ((tok, D), f32), ((tok, D), bf16), ((tok, D), bf16),
            ((blocks, tok, 2 * KV_WIDTH), bf16), ((1, D), f32),
        ],
        (dffn, xs, cot, middle, gains, w_o, attn_f, query, kv, lse, cosine, sine),
        scratch=(pltpu.VMEM((KV_HEADS, HEAD_DIM, wide), f32),),
    )
    (feed_sum,) = call(
        add_pieces_body, [((height, 3 * part), bf16)], tuple(feed_got), hold=(gain_two,)
    )
    dkv = deal(after(dkv, *feed_got[1:], *olds[1:3], *attn_olds[1:]), LO + ("core",))
    feed_other = trade(feed_sum, "hi")
    d_input, *sends = call(
        functools.partial(input_body, tok, rows),
        [((tok, D), f32)] + [((tok + 8, D), bf16)] * n_shard,
        (me, dkv, xs, d_middle, gains, w_kvq, d_query, d_branch, gain_two, cosine, sine),
        scratch=(pltpu.VMEM((n_shard, tok + 8, D), bf16),),
        smem=(0,),
        hold=misc[1:],
    )
    sends = pass_shard(sends)
    (feed_slots,) = call(
        functools.partial(add_slots_body, part),
        [((n_lo // 2, 2, 2, height, part), bf16)],
        (feed_sum, feed_other),
        hold=(d_input,),
    )
    feed_near = deal(feed_slots.reshape(n_lo * 2, height, part), LO + ("core",))
    feed_near = feed_near.reshape(n_lo, 2, height, part)
    (finished,) = call(
        functools.partial(finish_body, tok),
        [((2, D, tok), bf16)],
        (middle, d_input) + misc,
    )

    attn_chunks = call(
        functools.partial(attn_grad_body, tok),
        [((height + 8, D), bf16)] * n_lo,
        (me, lo) + sends + misc,
        scratch=(
            pltpu.VMEM((n_shard * tok, D), bf16), pltpu.VMEM((n_shard * tok, D), bf16),
            pltpu.VMEM((n_lo, height + 8, D), bf16),
        ),
        smem=(0, 1),
    )
    feed_near = after(feed_near, attn_chunks[0])
    feed_far = trade(feed_near, "y")
    attn_got = [attn_chunks[0]] + [pass_on(attn_chunks[k], LO, n_lo, k) for k in range(1, n_lo)]
    (attn_sum,) = call(
        add_pieces_body, [((height + 8, D), bf16)], tuple(attn_got), hold=(finished,)
    )
    attn_other = trade(attn_sum, "hi")
    results = lax.ppermute(finished, ALL, moves)
    (attn_old_rows,) = call(
        attn_old_body,
        [((D, D), f32)],
        (me,) + attn_olds,
        scratch=(pltpu.VMEM((D, D), bf16),),
        smem=(0,),
        hold=(attn_sum,),
    )
    attn_slots, gain_rows = call(
        add_second_body,
        [((n_lo, height, D), bf16), ((8, D), f32)],
        (attn_sum, attn_other),
        hold=(attn_old_rows,),
    )
    feed_same, feed_other = call(
        feed_ns_body,
        [((2 * D + 8, part), bf16)] * 2,
        (flags, feed_near, feed_far) + olds,
        scratch=(
            pltpu.VMEM((D, FF), f32), pltpu.VMEM((D, FF), bf16), pltpu.VMEM((D, FF), bf16),
            pltpu.VMEM((D, D), f32), pltpu.VMEM((D, D), bf16), pltpu.VMEM((D, D), bf16),
        ),
        smem=(0,),
        hold=(attn_slots, results),
    )
    feed_back = (
        feed_same, trade(feed_other, "core"),
        lax.ppermute(feed_same, OWNER, [(0, 2), (2, 0)]),
        lax.ppermute(feed_other, OWNER, [(0, 3), (2, 1)]),
    )
    attn_full = deal(attn_slots, LO)
    (attn_ortho,) = call(
        attn_ns_body,
        [((n_shard, 2 * rows + 8, D), bf16)],
        (me, attn_full, attn_old_rows),
        scratch=(
            pltpu.VMEM((D, D), f32), pltpu.VMEM((D, D), bf16), pltpu.VMEM((D, D), f32),
            pltpu.VMEM((D, D), bf16), pltpu.VMEM((D, D), bf16),
        ),
        smem=(0,),
        hold=(feed_same,),
    )
    attn_ortho = after(attn_ortho, *feed_back[2:])
    attn_back = deal(attn_ortho, SHARD)
    two = [((2, rows, FF), f32), ((D, part), f32)]
    grad_gate_up, grad_down, moment_gate_up, moment_down, new_gate_up, new_down, feed_norm = call(
        feed_new_body,
        two * 3 + [((3, 8, part), f32)],
        (flags,) + feed_back + (mom_gate_up, mom_down.T, w_gate_up, w_down.T),
        smem=(0,),
        hold=(attn_ortho,),
    )
    three = [((rows, D), f32), ((2, rows, KV_WIDTH), f32), ((rows, D), f32)]
    (
        grad_query, grad_kv, grad_out, moment_query, moment_kv, moment_out,
        new_query, new_kv, new_out, norms,
    ) = call(
        attn_new_body,
        three * 3 + [((1, 128), f32)],
        (attn_back, feed_norm, w_query, w_kv, w_out, mom_query, mom_kv, mom_out),
    )
    momentum_norms = norms[0, :7]
    grad_gains = gain_rows[:2, :rows]
    moment_gains = MOMENTUM * mom_gains + grad_gains
    all_tokens = tok * n_ctx * n_shard
    new_gains = norm_gains.astype(f32) + -GAIN_RATE / math.sqrt(all_tokens) * moment_gains
    results = jnp.transpose(results, (0, 2, 1)).astype(f32)
    return (
        results[0][None], results[1][None],
        grad_gains, grad_query, grad_kv, grad_out, grad_gate_up, grad_down.T,
        moment_gains, moment_query, moment_kv, moment_out, moment_gate_up, moment_down.T,
        momentum_norms,
        new_gains, new_query, new_kv, new_out, new_gate_up, new_down.T,
    )


def solution(mesh):
    n_ctx = mesh.shape["ctx"]
    split = Mesh(mesh.devices.reshape(2, n_ctx // 4, 2, 2, 2), ALL)
    tokens = P(SHARD, CTX, None)
    first, second, gains = P(SHARD, None), P(None, SHARD, None), P(None, SHARD)
    weights = (gains, first, second, first, second, first)
    return jax.shard_map(
        functools.partial(on_device, 2, n_ctx // 2),
        mesh=split,
        in_specs=(tokens, tokens, P(CTX)) + weights + weights,
        out_specs=(tokens, tokens) + weights + weights + (P(),) + weights,
        check_vma=False,
    )
```

profile of v0, /device:TPU:0, one launch (start us, length us, event | category | flops | bytes accessed | tf_op | source)
XLA Modules:
  0.0 252.8 jit_solution(397013829859878463)
XLA Ops:
  0.7 2.0 pack_body.1
  2.7 3.0 %collective-permute-start.2 = (bf16[152,960]{1,0:T(8,128)(2,1)}, bf16[152,960]{1,0:T(8,128)(2,1)}, u32[]{:S(2)}, u32[]{:S(2)}) collective-permute-start(bf16[152,960]{1,0:T(8,128)(2,1)} %get-tuple-element.89.refs_2_), channel_id=1, source_target_pairs={{0,2},{2,0},{1,3},{3,1},{4,6},{6,4},{5,7},{7,5},{8,10},{10,8},{9,1... | collective-permute-start | bytes 875528 | tf_op jit(solution)/shard_map/ppermute | solution.py:680
  5.6 2.9 %collective-permute-start = (bf16[136,576]{1,0:T(8,128)(2,1)}, bf16[136,576]{1,0:T(8,128)(2,1)}, u32[]{:S(2)}, u32[]{:S(2)}) collective-permute-start(bf16[136,576]{1,0:T(8,128)(2,1)} %get-tuple-element.88), channel_id=1, source_target_pairs={{0,0},{1,16},{2,2},{3,18},{4,4},{5,20},{6,6},{7,22},{8,8},{9,24},{... | collective-permute-start | bytes 470024 | tf_op jit(solution)/shard_map/ppermute | solution.py:732
  8.5 1.8 collective-permute-start.1
  11.3 2.1 pack_wide_body.1
  15.3 2.1 collective-permute-start.3
  19.3 3.1 %project_body.1 = (bf16[128,576]{1,0:T(8,128)(2,1)}, bf16[128,576]{1,0:T(8,128)(2,1)}, bf16[8,136,384]{2,1,0:T(8,128)(2,1)}, bf16[576,960]{1,0:T(8,128)(2,1)}, f32[8,576]{1,0:T(8,128)}) custom-call(s32[1]{0:T(128)} %bitcast.refs_0_, bf16[136,576]{1,0:T(8,128)(2,1)} %collective-permute-done.refs_1_.refs_2_, bf16[152,960]{1,0:T(8,128)(2,1)} %get-tuple-element.89.refs_2_, ...), custom_call_target="tpu_custom_call" | custom-call | bytes 1024 | tf_op jit(solution)/shard_map/project_body/pallas_call | solution.py:60
  22.3 4.2 %all-to-all-start = ((bf16[8,136,384]{2,1,0:T(8,128)(2,1)}), bf16[8,136,384]{2,1,0:T(8,128)(2,1)}, u32[]{:S(2)}, u32[]{:S(2)}) async-start(bf16[8,136,384]{2,1,0:T(8,128)(2,1)} %get-tuple-element.92), calls=%async_computation | async-start | bytes 1671168 | tf_op jit(solution)/shard_map/all_to_all | solution.py:692
  28.5 2.8 %collective-permute-start.10 = (bf16[576,128]{1,0:T(8,128)(2,1)}, bf16[576,128]{1,0:T(8,128)(2,1)}, u32[]{:S(2)}, u32[]{:S(2)}) collective-permute-start(bf16[576,128]{1,0:T(8,128)(2,1)} %bitcast.11), channel_id=1, source_target_pairs={{0,0},{1,16},{2,2},{3,18},{4,4},{5,20},{6,6},{7,22},{8,8},{9,24},{... | collective-permute-start | bytes 442376 | tf_op jit(solution)/shard_map/ppermute | solution.py:747
  32.0 3.4 %old_body.1 = (bf16[144,576]{1,0:T(8,128)(2,1)}, bf16[144,576]{1,0:T(8,128)(2,1)}, bf16[144,576]{1,0:T(8,128)(2,1)}, bf16[144,576]{1,0:T(8,128)(2,1)}, bf16[576,...) custom-call(s32[1]{0:T(128)} %bitcast.refs_0_, s32[5]{0:T(128)} %stack.20.refs_1_.refs_0_, f32[144,576]{1,0:T(8,128)} %refs_5_.5, ...), custom_call_target="tpu_custom_call" | custom-call | bytes 1024 | tf_op jit(solution)/shard_map/old_body/pallas_call | solution.py:60
  35.5 2.9 %collective-permute-start.11 = (bf16[576,128]{1,0:T(8,128)(2,1)}, bf16[576,128]{1,0:T(8,128)(2,1)}, u32[]{:S(2)}, u32[]{:S(2)}) collective-permute-start(bf16[576,128]{1,0:T(8,128)(2,1)} %collective-permute-done.10.refs_3_.refs_2_), channel_id=1, source_target_pairs={{0,1},{1,0},{2,3},{3,2},{4,5},{5,4},{6,7},{7,6},{8,9},{9,8},{10,11... | collective-permute-start | bytes 442376 | tf_op jit(solution)/shard_map/ppermute | solution.py:684
  40.3 5.1 %attend_body.1 = (bf16[576,576]{1,0:T(8,128)(2,1)}, f32[128,576]{1,0:T(8,128)}, bf16[128,576]{1,0:T(8,128)(2,1)}, bf16[128,576]{1,0:T(8,128)(2,1)}, f32[128,576]{1,0:T(8,128)}, /*index=5*/f32[3,384]{1,0:T(4,128)}) custom-call(s32[1]{0:T(128)} %bitcast.refs_0_, bf16[136,576]{1,0:T(8,128)(2,1)} %collective-permute-done.refs_1_.refs_2_, ...), custom_call_target="tpu_custom_call" | custom-call | bytes 1024 | tf_op jit(solution)/shard_map/attend_body/pallas_call | solution.py:60
  45.5 9.8 %all_gather.3.refs_2_.refs_1_ = bf16[512,576]{1,0:T(8,128)(2,1)} all-gather(bf16[128,576]{1,0:T(8,128)(2,1)} %get-tuple-element.99), channel_id=1, replica_groups=mesh['hi'=2,'lh'=2,'lx'=2,'y'=2,'core'=2] {'y','core'}, dimensions={0}, use_global_device_ids=true | all-gather | bytes 737280 | tf_op jit(solution)/shard_map/all_gather | solution.py:793
  57.1 6.7 %feed_body.1 = (bf16[256,576]{1,0:T(8,128)(2,1)}, bf16[256,576]{1,0:T(8,128)(2,1)}, bf16[256,576]{1,0:T(8,128)(2,1)}, bf16[256,576]{1,0:T(8,128)(2,1)}, bf16[4,1...) custom-call(s32[1]{0:T(128)} %bitcast.refs_0_, ...), custom_call_target="tpu_custom_call" | custom-call | bytes 1024 | tf_op jit(solution)/shard_map/feed_body/pallas_call | solution.py:60
  63.9 4.4 %all-to-all-start.1 = ((bf16[4,136,576]{2,1,0:T(8,128)(2,1)}), bf16[4,136,576]{2,1,0:T(8,128)(2,1)}, u32[]{:S(2)}, u32[]{:S(2)}) async-start(bf16[4,136,576]{2,1,0:T(8,128)(2,1)} %get-tuple-element.102), calls=%async_computation.1 | async-start | bytes 1392640 | tf_op jit(solution)/shard_map/all_to_all | solution.py:692
  71.8 4.0 %collective-permute-start.15 = (bf16[144,1152]{1,0:T(8,128)(2,1)}, bf16[144,1152]{1,0:T(8,128)(2,1)}, u32[]{:S(2)}, u32[]{:S(2)}) collective-permute-start(bf16[144,1152]{1,0:T(8,128)(2,1)} %get-tuple-element.108), channel_id=1, source_target_pairs={{0,8},{4,12},{8,0},{12,4},{1,9},{5,13},{9,1},{13,5},{2,10},{6,14},... | collective-permute-start | bytes 995336 | tf_op jit(solution)/shard_map/ppermute | solution.py:684
  76.0 3.4 %all-to-all-done.1.refs_0_ = bf16[4,136,576]{2,1,0:T(8,128)(2,1)} async-done(((bf16[4,136,576]{2,1,0:T(8,128)(2,1)}), bf16[4,136,576]{2,1,0:T(8,128)(2,1)}, u32[]{:S(2)}, u32[]{:S(2)}) %all-to-all-start.1) | async-done | bytes 626720 | tf_op jit(solution)/shard_map/all_to_all | solution.py:692
  79.3 9.8 %back_body.1 = (f32[128,576]{1,0:T(8,128)}, bf16[128,576]{1,0:T(8,128)(2,1)}, bf16[128,576]{1,0:T(8,128)(2,1)}, bf16[8,128,384]{2,1,0:T(8,128)(2,1)}, f32[1,576]{1,0:T(1,128)}) custom-call(bf16[4,136,576]{2,1,0:T(8,128)(2,1)} %all-to-all-done.1.refs_0_, bf16[136,576]{1,0:T(8,128)(2,1)} %collective-permute-done.refs_1_.refs_2_, ...), custom_call_target="tpu_custom_call" | custom-call | bytes 1024 | tf_op jit(solution)/shard_map/back_body/pallas_call | solution.py:60
  89.1 1.9 collective-permute-done.16.refs_3_
  91.1 4.5 %all-to-all-start.2 = ((bf16[8,128,384]{2,1,0:T(8,128)(2,1)}), bf16[8,128,384]{2,1,0:T(8,128)(2,1)}, u32[]{:S(2)}, u32[]{:S(2)}) async-start(bf16[8,128,384]{2,1,0:T(8,128)(2,1)} %after.13), calls=%async_computation.2 | async-start | bytes 1572864 | tf_op jit(solution)/shard_map/all_to_all | solution.py:692
  95.6 2.2 add_pieces_body.3.refs_0_
  100.8 8.9 %collective-permute-done.23.refs_12_.refs_4_.refs_8_ = bf16[256,576]{1,0:T(8,128)(2,1)} collective-permute-done((bf16[256,576]{1,0:T(8,128)(2,1)}, bf16[256,576]{1,0:T(8,128)(2,1)}, u32[]{:S(2)}, u32[]{:S(2)}) %collective-permute-start.23) | collective-permute-done | bytes 294944 | tf_op jit(solution)/shard_map/ppermute | solution.py:684
  109.8 6.1 %collective-permute-done.24.refs_13_.refs_5_.refs_9_ = bf16[256,576]{1,0:T(8,128)(2,1)} collective-permute-done((bf16[256,576]{1,0:T(8,128)(2,1)}, bf16[256,576]{1,0:T(8,128)(2,1)}, u32[]{:S(2)}, u32[]{:S(2)}) %collective-permute-start.24) | collective-permute-done | bytes 294944 | tf_op jit(solution)/shard_map/ppermute | solution.py:684
  115.9 3.5 %input_body.1 = (f32[128,576]{1,0:T(8,128)}, bf16[136,576]{1,0:T(8,128)(2,1)}, bf16[136,576]{1,0:T(8,128)(2,1)}, bf16[136,576]{1,0:T(8,128)(2,1)}, bf16[136,576]{1,0:T(8,128)(2,1)}) custom-call(s32[1]{0:T(128)} %bitcast.refs_0_, bf16[8,128,384]{2,1,0:T(8,128)(2,1)} %all-to-all-done.2.refs_1_, bf16[136,576]{1,0:T(8,128)(2,1)} %collective-permute-done.refs_1_.refs_2_, ...), custom_call_target="tpu_custom_call" | custom-call | bytes 1024 | tf_op jit(solution)/shard_map/input_body/pallas_call | solution.py:60
  119.3 2.1 add_slots_body.1
  121.4 4.3 %all-to-all-start.4 = ((bf16[8,144,384]{2,1,0:T(8,128)(2,1)}), bf16[8,144,384]{2,1,0:T(8,128)(2,1)}, u32[]{:S(2)}, u32[]{:S(2)}) async-start(bf16[8,144,384]{2,1,0:T(8,128)(2,1)} %bitcast.26), calls=%async_computation.4 | async-start | bytes 1769472 | tf_op jit(solution)/shard_map/all_to_all | solution.py:692
  127.8 5.9 %collective-permute-done.27.refs_4_ = bf16[136,576]{1,0:T(8,128)(2,1)} collective-permute-done((bf16[136,576]{1,0:T(8,128)(2,1)S(1)}, bf16[136,576]{1,0:T(8,128)(2,1)}, u32[]{:S(2)}, u32[]{:S(2)}) %collective-permute-start.27) | collective-permute-done | bytes 156704 | tf_op jit(solution)/shard_map/ppermute | solution.py:684
  133.8 2.0 collective-permute-done.28.refs_5_
  135.8 3.1 %attn_grad_body.1 = (bf16[152,576]{1,0:T(8,128)(2,1)}, bf16[152,576]{1,0:T(8,128)(2,1)}, bf16[152,576]{1,0:T(8,128)(2,1)}, bf16[152,576]{1,0:T(8,128)(2,1)}) custom-call(s32[1]{0:T(128)} %bitcast.refs_0_, s32[1]{0:T(128)} %bitcast.9.refs_1_, bf16[136,576]{1,0:T(8,128)(2,1)} %get-tuple-element.124.refs_2_, bf16[136,576]{1,0:T(8,128)(2,1)} %collective-permute-done.26.refs_3_, ...), custom_call_target="tpu_custom_call" | custom-call | bytes 1024 | tf_op jit(solution)/shard_map/attn_grad_body/pallas_call | solution.py:60
  139.3 2.0 collective-permute-start.29
  144.0 2.4 finish_body.1.refs_4_
  147.2 3.7 %collective-permute-start.25 = (bf16[2,576,128]{2,1,0:T(8,128)(2,1)}, bf16[2,576,128]{2,1,0:T(8,128)(2,1)}, u32[]{:S(2)}, u32[]{:S(2)}) collective-permute-start(bf16[2,576,128]{2,1,0:T(8,128)(2,1)} %finish_body.1.refs_4_), channel_id=1, source_target_pairs={{0,0},{1,16},{2,2},{3,18},{4,4},{5,20},{6,6},{7,22},{8,8},{9,24},{... | collective-permute-start | bytes 884744 | tf_op jit(solution)/shard_map/ppermute | solution.py:867
  150.9 1.7 collective-permute-done.31.refs_3_
  152.6 2.0 add_pieces_body.2.refs_5_.refs_0_
  154.6 1.9 collective-permute-start.32
  156.5 2.6 %attn_old_body.1.refs_2_ = f32[576,576]{1,0:T(8,128)} custom-call(s32[1]{0:T(128)} %bitcast.refs_0_, bf16[144,576]{1,0:T(8,128)(2,1)} %get-tuple-element.132.refs_1_, bf16[144,576]{1,0:T(8,128)(2,1)} %collective-permute-done.19.refs_6_.refs_2_, bf16[144,576]{1,0:T(8,128)(2,1)} %collective-permute-done.20.refs_7_.refs_3_, ...), custom_call_target="tpu_custom_call" | custom-call | bytes 1024 | tf_op jit(solution)/shard_map/attn_old_body/pallas_call | solution.py:60
  159.1 8.9 %collective-permute-done.32.refs_1_ = bf16[152,576]{1,0:T(8,128)(2,1)} collective-permute-done((bf16[152,576]{1,0:T(8,128)(2,1)}, bf16[152,576]{1,0:T(8,128)(2,1)}, u32[]{:S(2)}, u32[]{:S(2)}) %collective-permute-start.32) | collective-permute-done | bytes 175136 | tf_op jit(solution)/shard_map/ppermute | solution.py:680
  168.0 1.9 add_second_body.1
  170.0 4.2 %all-to-all-start.3 = ((bf16[4,144,576]{2,1,0:T(8,128)(2,1)}), bf16[4,144,576]{2,1,0:T(8,128)(2,1)}, u32[]{:S(2)}, u32[]{:S(2)}) async-start(bf16[4,144,576]{2,1,0:T(8,128)(2,1)} %get-tuple-element.134.refs_7_), calls=%async_computation.3 | async-start | bytes 1474560 | tf_op jit(solution)/shard_map/all_to_all | solution.py:692
  174.2 25.6 %feed_ns_body.1 = (bf16[1160,384]{1,0:T(8,128)(2,1)}, bf16[1160,384]{1,0:T(8,128)(2,1)}) custom-call(s32[5]{0:T(128)} %stack.20.refs_1_.refs_0_, bf16[4,2,144,384]{3,2,1,0:T(8,128)(2,1)} %after.14.refs_1_, bf16[4,2,144,384]{3,2,1,0:T(8,128)(2,1)} %collective-permute-done.34.refs_2_, bf16[576,384]{1,0:T(8,128)(2,1)} %after.9.refs_3_, ...), custom_call_target="tpu_custom_call" | custom-call | bytes 1024 | tf_op jit(solution)/shard_map/feed_ns_body/pallas_call | solution.py:60
  199.8 3.9 %collective-permute-start.36 = (bf16[1160,384]{1,0:T(8,128)(2,1)}, bf16[1160,384]{1,0:T(8,128)(2,1)}, u32[]{:S(2)}, u32[]{:S(2)}) collective-permute-start(bf16[1160,384]{1,0:T(8,128)(2,1)} %get-tuple-element.136.refs_3_.refs_1_), channel_id=1, source_target_pairs={{0,4},{4,0},{2,6},{6,2},{8,12},{12,8},{10,14},{14,10},{16,20},{20,... | collective-permute-start | bytes 2672648 | tf_op jit(solution)/shard_map/ppermute | solution.py:895
  203.6 2.2 collective-permute-start.37
  205.9 16.0 %attn_ns_body.1.refs_0_ = bf16[4,296,576]{2,1,0:T(8,128)(2,1)} custom-call(s32[1]{0:T(128)} %bitcast.refs_0_, bf16[4,144,576]{2,1,0:T(8,128)(2,1)} %all-to-all-done.3.refs_1_, f32[576,576]{1,0:T(8,128)} %attn_old_body.1.refs_2_, bf16[1160,384]{1,0:T(8,128)(2,1)} %get-tuple-element.136.refs_3_.refs_1_), custom_call_target="tpu_custom_call" | custom-call | bytes 1024 | tf_op jit(solution)/shard_map/attn_ns_body/pallas_call | solution.py:60
  221.8 2.3 collective-permute-done.37.refs_2_.refs_4_
  224.1 4.5 %all-to-all-start.5 = ((bf16[4,296,576]{2,1,0:T(8,128)(2,1)}), bf16[4,296,576]{2,1,0:T(8,128)(2,1)}, u32[]{:S(2)}, u32[]{:S(2)}) async-start(bf16[4,296,576]{2,1,0:T(8,128)(2,1)} %after.15.refs_9_), calls=%async_computation.5 | async-start | bytes 3031040 | tf_op jit(solution)/shard_map/all_to_all | solution.py:692
  232.3 6.5 %feed_new_body.1 = (f32[2,144,1536]{2,1,0:T(8,128)}, f32[576,384]{1,0:T(8,128)}, f32[2,144,1536]{2,1,0:T(8,128)}, f32[576,384]{1,0:T(8,128)}, f32[2,144,1536]{2,...) custom-call(s32[5]{0:T(128)} %stack.20.refs_1_.refs_0_, bf16[1160,384]{1,0:T(8,128)(2,1)} %get-tuple-element.136.refs_3_.refs_1_, ...), custom_call_target="tpu_custom_call" | custom-call | bytes 1024 | tf_op jit(solution)/shard_map/feed_new_body/pallas_call | solution.py:60
  238.8 9.3 %all-to-all-done.5.refs_0_ = bf16[4,296,576]{2,1,0:T(8,128)(2,1)} async-done(((bf16[4,296,576]{2,1,0:T(8,128)(2,1)}), bf16[4,296,576]{2,1,0:T(8,128)(2,1)}, u32[]{:S(2)}, u32[]{:S(2)}) %all-to-all-start.5) | async-done | bytes 1364000 | tf_op jit(solution)/shard_map/all_to_all | solution.py:692
  248.1 3.5 %attn_new_body.1 = (f32[144,576]{1,0:T(8,128)}, f32[2,144,192]{2,1,0:T(8,128)}, f32[144,576]{1,0:T(8,128)}, f32[144,576]{1,0:T(8,128)}, f32[2,144,192]{2,1,0:T(8...) custom-call(bf16[4,296,576]{2,1,0:T(8,128)(2,1)} %all-to-all-done.5., ...), custom_call_target="tpu_custom_call" | custom-call | bytes 1024 | tf_op jit(solution)/shard_map/attn_new_body/pallas_call | solution.py:60
  (91 shorter events, 28.1 us)
Async XLA Ops:
  2.7 12.7 %collective-permute-start.2 = (bf16[152,960]{1,0:T(8,128)(2,1)}, bf16[152,960]{1,0:T(8,128)(2,1)}, u32[]{:S(2)}, u32[]{:S(2)}) collective-permute-start(bf16[152,960]{1,0:T(8,128)(2,1)} %get-tuple-element.89.refs_2_), channel_id=1, source_target_pairs={{0,2},{2,0},{1,3},{3,1},{4,6},{6,4},{5,7},{7,5},{8,10},{10,8},{9,1... | collective-permute-start | bytes 875528 | tf_op jit(solution)/shard_map/ppermute | solution.py:680
  5.6 7.9 %collective-permute-start = (bf16[136,576]{1,0:T(8,128)(2,1)}, bf16[136,576]{1,0:T(8,128)(2,1)}, u32[]{:S(2)}, u32[]{:S(2)}) collective-permute-start(bf16[136,576]{1,0:T(8,128)(2,1)} %get-tuple-element.88), channel_id=1, source_target_pairs={{0,0},{1,16},{2,2},{3,18},{4,4},{5,20},{6,6},{7,22},{8,8},{9,24},{... | collective-permute-start | bytes 470024 | tf_op jit(solution)/shard_map/ppermute | solution.py:732
  8.5 10.7 %collective-permute-start.1 = (bf16[152,960]{1,0:T(8,128)(2,1)}, bf16[152,960]{1,0:T(8,128)(2,1)}, u32[]{:S(2)}, u32[]{:S(2)}) collective-permute-start(bf16[152,960]{1,0:T(8,128)(2,1)} %get-tuple-element.89.refs_2_), channel_id=1, source_target_pairs={{0,1},{1,0},{2,3},{3,2},{4,5},{5,4},{6,7},{7,6},{8,9},{9,8},{10,11... | collective-permute-start | bytes 875528 | tf_op jit(solution)/shard_map/ppermute | solution.py:680
  10.3 7.1 %collective-permute-start.5 = (bf16[144,576]{1,0:T(8,128)(2,1)}, bf16[144,576]{1,0:T(8,128)(2,1)}, u32[]{:S(2)}, u32[]{:S(2)}) collective-permute-start(bf16[144,576]{1,0:T(8,128)(2,1)} %refs_4_.7), channel_id=1, source_target_pairs={{0,2},{2,0},{1,3},{3,1},{4,6},{6,4},{5,7},{7,5},{8,10},{10,8},{9,1... | collective-permute-start | bytes 497672 | tf_op jit(solution)/shard_map/ppermute | solution.py:680
  10.8 8.4 %collective-permute-start.4 = (bf16[144,576]{1,0:T(8,128)(2,1)}, bf16[144,576]{1,0:T(8,128)(2,1)}, u32[]{:S(2)}, u32[]{:S(2)}) collective-permute-start(bf16[144,576]{1,0:T(8,128)(2,1)} %refs_4_.7), channel_id=1, source_target_pairs={{0,1},{1,0},{2,3},{3,2},{4,5},{5,4},{6,7},{7,6},{8,9},{9,8},{10,11... | collective-permute-start | bytes 497672 | tf_op jit(solution)/shard_map/ppermute | solution.py:680
  15.3 3.9 %collective-permute-start.3 = (bf16[152,960]{1,0:T(8,128)(2,1)}, bf16[152,960]{1,0:T(8,128)(2,1)}, u32[]{:S(2)}, u32[]{:S(2)}) collective-permute-start(bf16[152,960]{1,0:T(8,128)(2,1)} %collective-permute-done.2.refs_4_), channel_id=1, source_target_pairs={{0,1},{1,0},{2,3},{3,2},{4,5},{5,4},{6,7},{7,6},{8,9},{9,8},{10,11... | collective-permute-start | bytes 875528 | tf_op jit(solution)/shard_map/ppermute | solution.py:680
  17.4 1.8 collective-permute-start.6
  22.3 18.0 %all-to-all-start = ((bf16[8,136,384]{2,1,0:T(8,128)(2,1)}), bf16[8,136,384]{2,1,0:T(8,128)(2,1)}, u32[]{:S(2)}, u32[]{:S(2)}) async-start(bf16[8,136,384]{2,1,0:T(8,128)(2,1)} %get-tuple-element.92), calls=%async_computation | async-start | bytes 1671168 | tf_op jit(solution)/shard_map/all_to_all | solution.py:692
  26.6 13.3 %collective-permute-start.7 = (bf16[144,768]{1,0:T(8,128)(2,1)}, bf16[144,768]{1,0:T(8,128)(2,1)}, u32[]{:S(2)}, u32[]{:S(2)}) collective-permute-start(bf16[144,768]{1,0:T(8,128)(2,1)} %get-tuple-element.94), channel_id=1, source_target_pairs={{0,1},{1,0},{2,3},{3,2},{4,5},{5,4},{6,7},{7,6},{8,9},{9,8},{10,11... | collective-permute-start | bytes 663560 | tf_op jit(solution)/shard_map/ppermute | solution.py:684
  27.0 12.8 %collective-permute-start.8 = (bf16[144,768]{1,0:T(8,128)(2,1)}, bf16[144,768]{1,0:T(8,128)(2,1)}, u32[]{:S(2)}, u32[]{:S(2)}) collective-permute-start(bf16[144,768]{1,0:T(8,128)(2,1)} %get-tuple-element.95), channel_id=1, source_target_pairs={{0,2},{1,3},{2,0},{3,1},{4,6},{5,7},{6,4},{7,5},{8,10},{9,11},{10,... | collective-permute-start | bytes 663560 | tf_op jit(solution)/shard_map/ppermute | solution.py:684
  28.5 11.4 %collective-permute-start.9 = (bf16[144,768]{1,0:T(8,128)(2,1)}, bf16[144,768]{1,0:T(8,128)(2,1)}, u32[]{:S(2)}, u32[]{:S(2)}) collective-permute-start(bf16[144,768]{1,0:T(8,128)(2,1)} %get-tuple-element.96), channel_id=1, source_target_pairs={{0,3},{1,2},{2,1},{3,0},{4,7},{5,6},{6,5},{7,4},{8,11},{9,10},{10,... | collective-permute-start | bytes 663560 | tf_op jit(solution)/shard_map/ppermute | solution.py:684
  28.5 6.9 %collective-permute-start.10 = (bf16[576,128]{1,0:T(8,128)(2,1)}, bf16[576,128]{1,0:T(8,128)(2,1)}, u32[]{:S(2)}, u32[]{:S(2)}) collective-permute-start(bf16[576,128]{1,0:T(8,128)(2,1)} %bitcast.11), channel_id=1, source_target_pairs={{0,0},{1,16},{2,2},{3,18},{4,4},{5,20},{6,6},{7,22},{8,8},{9,24},{... | collective-permute-start | bytes 442376 | tf_op jit(solution)/shard_map/ppermute | solution.py:747
  35.5 20.7 %collective-permute-start.11 = (bf16[576,128]{1,0:T(8,128)(2,1)}, bf16[576,128]{1,0:T(8,128)(2,1)}, u32[]{:S(2)}, u32[]{:S(2)}) collective-permute-start(bf16[576,128]{1,0:T(8,128)(2,1)} %collective-permute-done.10.refs_3_.refs_2_), channel_id=1, source_target_pairs={{0,1},{1,0},{2,3},{3,2},{4,5},{5,4},{6,7},{7,6},{8,9},{9,8},{10,11... | collective-permute-start | bytes 442376 | tf_op jit(solution)/shard_map/ppermute | solution.py:684
  38.4 18.8 %collective-permute-start.12 = (bf16[576,128]{1,0:T(8,128)(2,1)}, bf16[576,128]{1,0:T(8,128)(2,1)}, u32[]{:S(2)}, u32[]{:S(2)}) collective-permute-start(bf16[576,128]{1,0:T(8,128)(2,1)} %collective-permute-done.10.refs_3_.refs_2_), channel_id=1, source_target_pairs={{0,2},{1,3},{2,0},{3,1},{4,6},{5,7},{6,4},{7,5},{8,10},{9,11},{10,... | collective-permute-start | bytes 442376 | tf_op jit(solution)/shard_map/ppermute | solution.py:684
  39.8 17.3 %collective-permute-start.13 = (bf16[576,128]{1,0:T(8,128)(2,1)}, bf16[576,128]{1,0:T(8,128)(2,1)}, u32[]{:S(2)}, u32[]{:S(2)}) collective-permute-start(bf16[576,128]{1,0:T(8,128)(2,1)} %collective-permute-done.10.refs_3_.refs_2_), channel_id=1, source_target_pairs={{0,3},{1,2},{2,1},{3,0},{4,7},{5,6},{6,5},{7,4},{8,11},{9,10},{10,... | collective-permute-start | bytes 442376 | tf_op jit(solution)/shard_map/ppermute | solution.py:684
  55.3 15.0 %collective-permute-start.19 = (bf16[144,576]{1,0:T(8,128)(2,1)}, bf16[144,576]{1,0:T(8,128)(2,1)}, u32[]{:S(2)}, u32[]{:S(2)}) collective-permute-start(bf16[144,576]{1,0:T(8,128)(2,1)} %after.10), channel_id=1, source_target_pairs={{0,1},{1,0},{2,3},{3,2},{4,5},{5,4},{6,7},{7,6},{8,9},{9,8},{10,11... | collective-permute-start | bytes 497672 | tf_op jit(solution)/shard_map/ppermute | solution.py:684
  55.6 16.2 %collective-permute-start.20 = (bf16[144,576]{1,0:T(8,128)(2,1)}, bf16[144,576]{1,0:T(8,128)(2,1)}, u32[]{:S(2)}, u32[]{:S(2)}) collective-permute-start(bf16[144,576]{1,0:T(8,128)(2,1)} %after.11), channel_id=1, source_target_pairs={{0,2},{1,3},{2,0},{3,1},{4,6},{5,7},{6,4},{7,5},{8,10},{9,11},{10,... | collective-permute-start | bytes 497672 | tf_op jit(solution)/shard_map/ppermute | solution.py:684
  56.2 19.7 %collective-permute-start.21 = (bf16[144,576]{1,0:T(8,128)(2,1)}, bf16[144,576]{1,0:T(8,128)(2,1)}, u32[]{:S(2)}, u32[]{:S(2)}) collective-permute-start(bf16[144,576]{1,0:T(8,128)(2,1)} %after.12), channel_id=1, source_target_pairs={{0,3},{1,2},{2,1},{3,0},{4,7},{5,6},{6,5},{7,4},{8,11},{9,10},{10,... | collective-permute-start | bytes 497672 | tf_op jit(solution)/shard_map/ppermute | solution.py:684
  63.9 15.4 %all-to-all-start.1 = ((bf16[4,136,576]{2,1,0:T(8,128)(2,1)}), bf16[4,136,576]{2,1,0:T(8,128)(2,1)}, u32[]{:S(2)}, u32[]{:S(2)}) async-start(bf16[4,136,576]{2,1,0:T(8,128)(2,1)} %get-tuple-element.102), calls=%async_computation.1 | async-start | bytes 1392640 | tf_op jit(solution)/shard_map/all_to_all | solution.py:692
  68.3 22.8 %collective-permute-start.17 = (bf16[576,384]{1,0:T(8,128)(2,1)}, bf16[576,384]{1,0:T(8,128)(2,1)}, u32[]{:S(2)}, u32[]{:S(2)}) collective-permute-start(bf16[576,384]{1,0:T(8,128)(2,1)} %after.8), channel_id=1, source_target_pairs={{0,1},{1,0},{2,3},{3,2},{4,5},{5,4},{6,7},{7,6},{8,9},{9,8},{10,11... | collective-permute-start | bytes 1327112 | tf_op jit(solution)/shard_map/ppermute | solution.py:684
  69.0 22.1 %collective-permute-start.18 = (bf16[576,384]{1,0:T(8,128)(2,1)}, bf16[576,384]{1,0:T(8,128)(2,1)}, u32[]{:S(2)}, u32[]{:S(2)}) collective-permute-start(bf16[576,384]{1,0:T(8,128)(2,1)} %after.9.refs_3_), channel_id=1, source_target_pairs={{0,2},{1,3},{2,0},{3,1},{4,6},{5,7},{6,4},{7,5},{8,10},{9,11},{10,... | collective-permute-start | bytes 1327112 | tf_op jit(solution)/shard_map/ppermute | solution.py:684
  70.2 18.9 %collective-permute-start.14 = (bf16[144,1152]{1,0:T(8,128)(2,1)}, bf16[144,1152]{1,0:T(8,128)(2,1)}, u32[]{:S(2)}, u32[]{:S(2)}) collective-permute-start(bf16[144,1152]{1,0:T(8,128)(2,1)} %get-tuple-element.107), channel_id=1, source_target_pairs={{0,4},{4,0},{8,12},{12,8},{1,5},{5,1},{9,13},{13,9},{2,6},{6,2},{1... | collective-permute-start | bytes 995336 | tf_op jit(solution)/shard_map/ppermute | solution.py:684
  71.8 17.3 %collective-permute-start.15 = (bf16[144,1152]{1,0:T(8,128)(2,1)}, bf16[144,1152]{1,0:T(8,128)(2,1)}, u32[]{:S(2)}, u32[]{:S(2)}) collective-permute-start(bf16[144,1152]{1,0:T(8,128)(2,1)} %get-tuple-element.108), channel_id=1, source_target_pairs={{0,8},{4,12},{8,0},{12,4},{1,9},{5,13},{9,1},{13,5},{2,10},{6,14},... | collective-permute-start | bytes 995336 | tf_op jit(solution)/shard_map/ppermute | solution.py:684
  75.9 15.2 %collective-permute-start.16 = (bf16[144,1152]{1,0:T(8,128)(2,1)}, bf16[144,1152]{1,0:T(8,128)(2,1)}, u32[]{:S(2)}, u32[]{:S(2)}) collective-permute-start(bf16[144,1152]{1,0:T(8,128)(2,1)} %get-tuple-element.109), channel_id=1, source_target_pairs={{0,12},{4,8},{8,4},{12,0},{1,13},{5,9},{9,5},{13,1},{2,14},{6,10},... | collective-permute-start | bytes 995336 | tf_op jit(solution)/shard_map/ppermute | solution.py:684
  91.1 24.8 %all-to-all-start.2 = ((bf16[8,128,384]{2,1,0:T(8,128)(2,1)}), bf16[8,128,384]{2,1,0:T(8,128)(2,1)}, u32[]{:S(2)}, u32[]{:S(2)}) async-start(bf16[8,128,384]{2,1,0:T(8,128)(2,1)} %after.13), calls=%async_computation.2 | async-start | bytes 1572864 | tf_op jit(solution)/shard_map/all_to_all | solution.py:692
  97.7 21.6 %collective-permute-start.33 = (bf16[144,1152]{1,0:T(8,128)(2,1)}, bf16[144,1152]{1,0:T(8,128)(2,1)}, u32[]{:S(2)}, u32[]{:S(2)}) collective-permute-start(bf16[144,1152]{1,0:T(8,128)(2,1)} %add_pieces_body.3.refs_0_), channel_id=1, source_target_pairs={{0,16},{16,0},{1,17},{17,1},{2,18},{18,2},{3,19},{19,3},{4,20},{20... | collective-permute-start | bytes 995336 | tf_op jit(solution)/shard_map/ppermute | solution.py:680
  98.8 2.0 collective-permute-start.22
  98.9 10.8 %collective-permute-start.23 = (bf16[256,576]{1,0:T(8,128)(2,1)}, bf16[256,576]{1,0:T(8,128)(2,1)}, u32[]{:S(2)}, u32[]{:S(2)}) collective-permute-start(bf16[256,576]{1,0:T(8,128)(2,1)} %get-tuple-element.120), channel_id=1, source_target_pairs={{0,2},{1,3},{2,0},{3,1},{4,6},{5,7},{6,4},{7,5},{8,10},{9,11},{10,... | collective-permute-start | bytes 884744 | tf_op jit(solution)/shard_map/ppermute | solution.py:684
  99.2 16.6 %collective-permute-start.24 = (bf16[256,576]{1,0:T(8,128)(2,1)}, bf16[256,576]{1,0:T(8,128)(2,1)}, u32[]{:S(2)}, u32[]{:S(2)}) collective-permute-start(bf16[256,576]{1,0:T(8,128)(2,1)} %get-tuple-element.121), channel_id=1, source_target_pairs={{0,3},{1,2},{2,1},{3,0},{4,7},{5,6},{6,5},{7,4},{8,11},{9,10},{10,... | collective-permute-start | bytes 884744 | tf_op jit(solution)/shard_map/ppermute | solution.py:684
  121.4 5.0 %copy-start.4 = (bf16[136,576]{1,0:T(8,128)(2,1)S(1)}, bf16[136,576]{1,0:T(8,128)(2,1)}, u32[]{:S(2)}) copy-start(bf16[136,576]{1,0:T(8,128)(2,1)} %get-tuple-element.126) | copy-start | bytes 470020
  121.4 5.2 %copy-start.3 = (bf16[136,576]{1,0:T(8,128)(2,1)S(1)}, bf16[136,576]{1,0:T(8,128)(2,1)}, u32[]{:S(2)}) copy-start(bf16[136,576]{1,0:T(8,128)(2,1)} %get-tuple-element.127) | copy-start | bytes 470020
  121.4 17.5 %all-to-all-start.4 = ((bf16[8,144,384]{2,1,0:T(8,128)(2,1)}), bf16[8,144,384]{2,1,0:T(8,128)(2,1)}, u32[]{:S(2)}, u32[]{:S(2)}) async-start(bf16[8,144,384]{2,1,0:T(8,128)(2,1)} %bitcast.26), calls=%async_computation.4 | async-start | bytes 1769472 | tf_op jit(solution)/shard_map/all_to_all | solution.py:692
  125.8 2.0 collective-permute-start.26
  126.4 7.4 %collective-permute-start.27 = (bf16[136,576]{1,0:T(8,128)(2,1)S(1)}, bf16[136,576]{1,0:T(8,128)(2,1)}, u32[]{:S(2)}, u32[]{:S(2)}) collective-permute-start(bf16[136,576]{1,0:T(8,128)(2,1)S(1)} %copy-done.4), channel_id=1, source_target_pairs={{0,2},{1,3},{2,0},{3,1},{4,6},{5,7},{6,4},{7,5},{8,10},{9,11},{10,... | collective-permute-start | bytes 470024 | tf_op jit(solution)/shard_map/ppermute | solution.py:684
  126.7 9.1 %collective-permute-start.28 = (bf16[136,576]{1,0:T(8,128)(2,1)S(1)}, bf16[136,576]{1,0:T(8,128)(2,1)}, u32[]{:S(2)}, u32[]{:S(2)}) collective-permute-start(bf16[136,576]{1,0:T(8,128)(2,1)S(1)} %copy-done.3), channel_id=1, source_target_pairs={{0,3},{1,2},{2,1},{3,0},{4,7},{5,6},{6,5},{7,4},{8,11},{9,10},{10,... | collective-permute-start | bytes 470024 | tf_op jit(solution)/shard_map/ppermute | solution.py:684
  138.9 35.3 %collective-permute-start.34 = (bf16[4,2,144,384]{3,2,1,0:T(8,128)(2,1)}, bf16[4,2,144,384]{3,2,1,0:T(8,128)(2,1)}, u32[]{:S(2)}, u32[]{:S(2)}) collective-permute-start(bf16[4,2,144,384]{3,2,1,0:T(8,128)(2,1)} %after.14.refs_1_), channel_id=1, source_target_pairs={{0,2},{2,0},{1,3},{3,1},{4,6},{6,4},{5,7},{7,5},{8,10},{10,8},{9,1... | collective-permute-start | bytes 2654216 | tf_op jit(solution)/shard_map/ppermute | solution.py:680
  139.3 7.9 %collective-permute-start.29 = (bf16[152,576]{1,0:T(8,128)(2,1)}, bf16[152,576]{1,0:T(8,128)(2,1)}, u32[]{:S(2)}, u32[]{:S(2)}) collective-permute-start(bf16[152,576]{1,0:T(8,128)(2,1)} %get-tuple-element.129), channel_id=1, source_target_pairs={{0,4},{4,0},{8,12},{12,8},{1,5},{5,1},{9,13},{13,9},{2,6},{6,2},{1... | collective-permute-start | bytes 525320 | tf_op jit(solution)/shard_map/ppermute | solution.py:684
  141.2 9.7 %collective-permute-start.30 = (bf16[152,576]{1,0:T(8,128)(2,1)}, bf16[152,576]{1,0:T(8,128)(2,1)}, u32[]{:S(2)}, u32[]{:S(2)}) collective-permute-start(bf16[152,576]{1,0:T(8,128)(2,1)} %get-tuple-element.130), channel_id=1, source_target_pairs={{0,8},{4,12},{8,0},{12,4},{1,9},{5,13},{9,1},{13,5},{2,10},{6,14},... | collective-permute-start | bytes 525320 | tf_op jit(solution)/shard_map/ppermute | solution.py:684
  142.8 9.8 %collective-permute-start.31 = (bf16[152,576]{1,0:T(8,128)(2,1)}, bf16[152,576]{1,0:T(8,128)(2,1)}, u32[]{:S(2)}, u32[]{:S(2)}) collective-permute-start(bf16[152,576]{1,0:T(8,128)(2,1)} %get-tuple-element.131), channel_id=1, source_target_pairs={{0,12},{4,8},{8,4},{12,0},{1,13},{5,9},{9,5},{13,1},{2,14},{6,10},... | collective-permute-start | bytes 525320 | tf_op jit(solution)/shard_map/ppermute | solution.py:684
  142.8 31.4 %collective-permute-start.35 = (bf16[576,384]{1,0:T(8,128)(2,1)}, bf16[576,384]{1,0:T(8,128)(2,1)}, u32[]{:S(2)}, u32[]{:S(2)}) collective-permute-start(bf16[576,384]{1,0:T(8,128)(2,1)} %after.8), channel_id=1, source_target_pairs={{0,3},{1,2},{2,1},{3,0},{4,7},{5,6},{6,5},{7,4},{8,11},{9,10},{10,... | collective-permute-start | bytes 1327112 | tf_op jit(solution)/shard_map/ppermute | solution.py:684
  147.2 27.0 %collective-permute-start.25 = (bf16[2,576,128]{2,1,0:T(8,128)(2,1)}, bf16[2,576,128]{2,1,0:T(8,128)(2,1)}, u32[]{:S(2)}, u32[]{:S(2)}) collective-permute-start(bf16[2,576,128]{2,1,0:T(8,128)(2,1)} %finish_body.1.refs_4_), channel_id=1, source_target_pairs={{0,0},{1,16},{2,2},{3,18},{4,4},{5,20},{6,6},{7,22},{8,8},{9,24},{... | collective-permute-start | bytes 884744 | tf_op jit(solution)/shard_map/ppermute | solution.py:867
  154.6 13.5 %collective-permute-start.32 = (bf16[152,576]{1,0:T(8,128)(2,1)}, bf16[152,576]{1,0:T(8,128)(2,1)}, u32[]{:S(2)}, u32[]{:S(2)}) collective-permute-start(bf16[152,576]{1,0:T(8,128)(2,1)} %add_pieces_body.2.refs_5_.refs_0_), channel_id=1, source_target_pairs={{0,16},{16,0},{1,17},{17,1},{2,18},{18,2},{3,19},{19,3},{4,20},{20... | collective-permute-start | bytes 525320 | tf_op jit(solution)/shard_map/ppermute | solution.py:680
  170.0 35.9 %all-to-all-start.3 = ((bf16[4,144,576]{2,1,0:T(8,128)(2,1)}), bf16[4,144,576]{2,1,0:T(8,128)(2,1)}, u32[]{:S(2)}, u32[]{:S(2)}) async-start(bf16[4,144,576]{2,1,0:T(8,128)(2,1)} %get-tuple-element.134.refs_7_), calls=%async_computation.3 | async-start | bytes 1474560 | tf_op jit(solution)/shard_map/all_to_all | solution.py:692
  199.8 22.1 %collective-permute-start.36 = (bf16[1160,384]{1,0:T(8,128)(2,1)}, bf16[1160,384]{1,0:T(8,128)(2,1)}, u32[]{:S(2)}, u32[]{:S(2)}) collective-permute-start(bf16[1160,384]{1,0:T(8,128)(2,1)} %get-tuple-element.136.refs_3_.refs_1_), channel_id=1, source_target_pairs={{0,4},{4,0},{2,6},{6,2},{8,12},{12,8},{10,14},{14,10},{16,20},{20,... | collective-permute-start | bytes 2672648 | tf_op jit(solution)/shard_map/ppermute | solution.py:895
  203.6 20.5 %collective-permute-start.37 = (bf16[1160,384]{1,0:T(8,128)(2,1)}, bf16[1160,384]{1,0:T(8,128)(2,1)}, u32[]{:S(2)}, u32[]{:S(2)}) collective-permute-start(bf16[1160,384]{1,0:T(8,128)(2,1)} %get-tuple-element.137), channel_id=1, source_target_pairs={{0,5},{4,1},{2,7},{6,3},{8,13},{12,9},{10,15},{14,11},{16,21},{20,... | collective-permute-start | bytes 2672648 | tf_op jit(solution)/shard_map/ppermute | solution.py:896
  224.1 4.5 %copy-start.2 = (bf16[1160,384]{1,0:T(8,128)(2,1)S(1)}, bf16[1160,384]{1,0:T(8,128)(2,1)}, u32[]{:S(2)}) copy-start(bf16[1160,384]{1,0:T(8,128)(2,1)} %get-tuple-element.137) | copy-start | bytes 2672644
  224.1 24.0 %all-to-all-start.5 = ((bf16[4,296,576]{2,1,0:T(8,128)(2,1)}), bf16[4,296,576]{2,1,0:T(8,128)(2,1)}, u32[]{:S(2)}, u32[]{:S(2)}) async-start(bf16[4,296,576]{2,1,0:T(8,128)(2,1)} %after.15.refs_9_), calls=%async_computation.5 | async-start | bytes 3031040 | tf_op jit(solution)/shard_map/all_to_all | solution.py:692
  228.6 3.6 %collective-permute-start.38 = (bf16[1160,384]{1,0:T(8,128)(2,1)S(1)}, bf16[1160,384]{1,0:T(8,128)(2,1)}, u32[]{:S(2)}, u32[]{:S(2)}) collective-permute-start(bf16[1160,384]{1,0:T(8,128)(2,1)S(1)} %copy-done.2), channel_id=1, source_target_pairs={{0,1},{1,0},{2,3},{3,2},{4,5},{5,4},{6,7},{7,6},{8,9},{9,8},{10,11... | collective-permute-start | bytes 2672648 | tf_op jit(solution)/shard_map/ppermute | solution.py:680
  (3 other events, 9.1 us)
where the time goes:
time: 254 us; the launch traced here: 253 us
  Pallas kernels  104 us (41%)
  starting transfers between devices  77.5 us (31%)
  waiting for transfers between devices  51.9 us (20%)
  blocking collectives  9.81 us (4%)
  other arithmetic  4.46 us (2%)
  local copies, waits for them, and re-layouts  3.92 us (2%)
    pallas_call x19, Pallas kernels, call(): pl.pallas_call(run, name=getattr(body, 'func', body).__name__, out_shape=...  104 us
    ppermute x24, waiting for transfers between devices, pass_on(): return lax.ppermute(x, axis, [(i, i ^ j) for i in range(size)])  27.5 us
    all_to_all x6, starting transfers between devices, deal(): return lax.all_to_all(x, axis, 0, 0, tiled=True)  26.1 us
    ppermute x24, starting transfers between devices, pass_on(): return lax.ppermute(x, axis, [(i, i ^ j) for i in range(size)])  24.5 us
    all_to_all x6, waiting for transfers between devices, deal(): return lax.all_to_all(x, axis, 0, 0, tiled=True)  13.2 us
    ppermute x10, starting transfers between devices, trade(): return lax.ppermute(x, axis, TRADE)  11.4 us
    all_gather x1, blocking collectives, on_device(): ffn_all = lax.all_gather(ffn_in, SHARD, axis=0, tiled=True)  9.81 us
    ppermute x10, waiting for transfers between devices, trade(): return lax.ppermute(x, axis, TRADE)  9.01 us
  transfers between devices with their start and end apart: 45, of which 14 were waited for; matrix products, arithmetic and copies ran while one was open for 3% of the time, Pallas kernels for 37%

commit v1 on v0

--- a/solution.py
+++ b/solution.py
@@ -62,7 +62,9 @@
         name=getattr(body, "func", body).__name__,
         out_shape=[jax.ShapeDtypeStruct(s, d) for s, d in outs],
         in_specs=[pl.BlockSpec(memory_space=space) for space in spaces],
-        out_specs=[pl.BlockSpec(memory_space=pltpu.VMEM) for _ in outs],
+        out_specs=[
+            pl.BlockSpec(memory_space=pltpu.SMEM if len(s) == 1 else pltpu.VMEM) for s, _ in outs
+        ],
         scratch_shapes=list(scratch),
         compiler_params=pltpu.CompilerParams(vmem_limit_bytes=limit * 2**20),
         cost_estimate=pl.CostEstimate(flops=0, bytes_accessed=1024, transcendentals=0),
@@ -167,19 +169,30 @@
     )
 
 
-def each_block(count, visit):
-    if count <= 8:
-        for j in range(count):
-            visit(j)
-    else:
-        lax.fori_loop(0, count, lambda j, c: (visit(j), c)[1], 0)
+def kv_block(kv_refs, j):
+    half = kv_refs[0].shape[0]
+    return kv_refs[j // half].at[j % half]
+
+
+def head_rows(kv_refs, tok, first, count, group):
+    return tuple(
+        jnp.concatenate(
+            [
+                kv_block(kv_refs, j)[0:tok, at : at + HEAD_DIM]
+                for j in range(first, first + count)
+            ],
+            axis=0,
+        )
+        for at in (group * HEAD_DIM, KV_WIDTH + group * HEAD_DIM)
+    )
 
 
 def attend_body(
-    tok, blocks, me_ref, xg_ref, q_ref, kv_ref, p0, p1, p2, p3, gains_ref,
+    tok, blocks, me_ref, xg_ref, q_ref, near_ref, far_ref, p0, p1, p2, p3, gains_ref,
     wo_ref, attn_f_ref, ffn_ref, rows_ref, middle_ref, lse_ref, scores_ref, peak_ref, total_ref, mixed_ref,
 ):
     wide = GROUPS * tok
+    kv_refs = (near_ref, far_ref)
     for j, piece in enumerate((p0, p1, p2, p3)):
         rows = piece.shape[0]
         wo_ref[pl.ds(pl.multiple_of((me_ref[0] ^ j) * rows, 16), rows), :] = piece[...]
@@ -194,26 +207,25 @@
     total_ref[...] = jnp.zeros(total_ref.shape, f32)
     mixed_ref[...] = jnp.zeros(mixed_ref.shape, f32)
 
-    def first(j):
-        allowed = ahead <= query_base - kv_ref[j, tok : tok + 1, 0:1].astype(f32) * tok
+    for j in range(blocks):
+        block_ref = kv_block(kv_refs, j)
+        allowed = ahead <= query_base - block_ref[tok : tok + 1, 0:1].astype(f32) * tok
         for g in range(KV_HEADS):
-            s = dot_cols(kv_ref[j, 0:tok, g * HEAD_DIM : (g + 1) * HEAD_DIM], queries[g])
+            s = dot_cols(block_ref[0:tok, g * HEAD_DIM : (g + 1) * HEAD_DIM], queries[g])
             s = jnp.where(allowed, s, NEG_LARGE)
             scores_ref[g, j] = s
             peak_ref[g : g + 1, :] = jnp.maximum(
                 peak_ref[g : g + 1, :], jnp.max(s, axis=0, keepdims=True)
             )
 
-    each_block(blocks, first)
-
-    def second(j):
+    for j in range(blocks):
+        block_ref = kv_block(kv_refs, j)
         for g in range(KV_HEADS):
             p = jnp.exp(scores_ref[g, j] - peak_ref[g : g + 1, :])
             total_ref[g : g + 1, :] += jnp.sum(p, axis=0, keepdims=True)
             at = KV_WIDTH + g * HEAD_DIM
-            mixed_ref[g] += dot_rows(kv_ref[j, 0:tok, at : at + HEAD_DIM], p.astype(bf16))
-
-    each_block(blocks, second)
+            mixed_ref[g] += dot_rows(block_ref[0:tok, at : at + HEAD_DIM], p.astype(bf16))
+
     lse_ref[...] = peak_ref[...] + jnp.log(total_ref[...])
     attn_f = ungroup(
         [(mixed_ref[g] / total_ref[g : g + 1, :]).T for g in range(KV_HEADS)], tok
@@ -322,11 +334,12 @@
 
 
 def back_body(
-    tok, blocks, dffn_ref, xg_ref, g_ref, middle_ref, gains_ref, wo_ref, attn_f_ref, q_ref, kv_ref,
-    lse_ref, cos_ref, sin_ref,
+    tok, blocks, flags_ref, dffn_ref, xg_ref, g_ref, middle_ref, gains_ref, wo_ref, attn_f_ref, q_ref, near_ref,
+    far_ref, lse_ref, cos_ref, sin_ref,
     dmid_ref, dq_ref, dbranch_ref, dkv_ref, gain_ref, dq_acc,
 ):
     wide = GROUPS * tok
+    core, kv_refs = flags_ref[1], (near_ref, far_ref)
     query_base = xg_ref[tok : tok + 1, 0:1].astype(f32) * tok
     middle = middle_ref[...]
     inverse = inverse_rms(middle)
@@ -355,24 +368,32 @@
         jnp.sum(group_rows(product, g).T, axis=0, keepdims=True) for g in range(KV_HEADS)
     ]
     dq_acc[...] = jnp.zeros(dq_acc.shape, f32)
-
-    def visit(j):
-        allowed = ahead <= query_base - kv_ref[j, tok : tok + 1, 0:1].astype(f32) * tok
+    count = min(blocks, 8)
+    for first in range(0, blocks, count):
+        masked = jnp.concatenate(
+            [
+                jnp.where(
+                    ahead
+                    <= query_base - kv_block(kv_refs, j)[tok : tok + 1, 0:1].astype(f32) * tok,
+                    0.0,
+                    NEG_LARGE,
+                )
+                for j in range(first, first + count)
+            ],
+            axis=0,
+        )
         d_keys, d_values = [], []
         for g in range(KV_HEADS):
-            at = KV_WIDTH + g * HEAD_DIM
-            key = kv_ref[j, 0:tok, g * HEAD_DIM : (g + 1) * HEAD_DIM]
-            value = kv_ref[j, 0:tok, at : at + HEAD_DIM]
-            s = dot_cols(key, queries[g])
-            p = jnp.where(allowed, jnp.exp(s - lse_ref[g : g + 1, :]), 0.0)
+            key, value = head_rows(kv_refs, tok, first, count, g)
+            p = jnp.exp(dot_cols(key, queries[g]) + (masked - lse_ref[g : g + 1, :]))
             d_weight = dot_cols(value, outs[g])
             ds = (p * (d_weight - deltas[g])).astype(bf16)
-            d_values.append(dot(p.astype(bf16), outs[g]))
-            d_keys.append(dot(ds, queries[g]))
+            d_values.append(dot(p.astype(bf16), outs[g]).astype(bf16))
+            d_keys.append(dot(ds, queries[g]).astype(bf16))
             dq_acc[g] += dot_rows(key, ds)
-        dkv_ref[j] = jnp.concatenate(d_keys + d_values, axis=1).astype(bf16)
-
-    each_block(blocks, visit)
+        both = jnp.concatenate(d_keys + d_values, axis=1)
+        for j in range(count):
+            dkv_ref[(core * (blocks // 2) + first + j) % blocks] = both[j * tok : (j + 1) * tok, :]
     d_query = ungroup([dq_acc[g].T * 0.125 for g in range(KV_HEADS)], tok)
     dq_ref[...] = turn_wide(d_query, cos_ref[...], -sin_ref[...]).astype(bf16)
 
@@ -435,7 +456,7 @@
         rows_ref[j * tok : (j + 1) * tok, :] = piece[tok:, :]
         cols_ref[j * tok : (j + 1) * tok, :] = cols[0:tok, :]
         gain = gain + cols[tok:, :].astype(f32)
-    grad = dot_rows(cols_ref[...], rows_ref[...]).astype(bf16)
+    grad = dot_rows(rows_ref[...], cols_ref[...]).astype(bf16)
     gain = gain.astype(bf16)
     height = whole_ref.shape[1] - 8
     for t in range(whole_ref.shape[0]):
@@ -466,20 +487,19 @@
     return jnp.sum(jnp.sum(rows, axis=0, keepdims=True), axis=1, keepdims=True)
 
 
-def sweeps(z_ref, zb_ref, rest_ref, rest_b_ref, poly_ref, squares, count, block, steps):
+def sweeps(z_ref, zb_ref, rest_ref, rest_b_ref, poly_ref, squares, block, steps):
     n = z_ref.shape[0]
     row = lax.broadcasted_iota(jnp.int32, (block, n), 0)
     col = lax.broadcasted_iota(jnp.int32, (block, n), 1)
 
     def sweep(_, squares):
-        center = squares / count
+        center = squares / float(n)
         slope = NS_B + 2.0 * NS_C * center
         lead = NS_A + NS_B * center + NS_C * center * center
 
         def first(at, here):
             gram = dot_cols(zb_ref[here, :], zb_ref[...])
-            mine = jnp.logical_and(row + at == col, (row + at).astype(f32) < count)
-            rest = jnp.where(mine, gram - center, gram)
+            rest = jnp.where(row + at == col, gram - center, gram)
             rest_ref[here, :] = rest
             rest_b_ref[here, :] = rest.astype(bf16)
 
@@ -567,7 +587,7 @@
     each_rows(D, 48, add, 0)
     total, squares = normalize(z_ref, zb_ref)
     sweeps(
-        z_ref, zb_ref, rest_ref, rest_b_ref, poly_ref, squares, jnp.float32(D), D // 2, NS_STEPS
+        z_ref, zb_ref, rest_ref, rest_b_ref, poly_ref, squares, D // 2, NS_STEPS
     )
     norm = norm_rows(total, jnp.float32(D * parts * part), (8, part))
     for out_ref, to in ((same_ref, core), (other_ref, 1 - core)):
@@ -589,32 +609,38 @@
                 ]
 
 
-def attn_old_body(me_ref, m0, m1, m2, m3, out_ref, old_ref):
-    rows = m0.shape[0]
-    for j, piece in enumerate((m0, m1, m2, m3)):
-        old_ref[pl.ds(pl.multiple_of((me_ref[0] ^ j) * rows, 16), rows), :] = piece[...]
-    out_ref[...] = MOMENTUM * old_ref[...].T.astype(f32)
-
-
 def attn_ns_body(
-    me_ref, grad_ref, old_ref, out_ref, z_ref, zb_ref, rest_ref, rest_b_ref, poly_ref
-):
+    me_ref, grad_ref, m0, m1, m2, m3, out_ref, z_ref, zb_ref, rest_ref, rest_b_ref, poly_ref,
+    *narrow_refs,
+):
+    me = me_ref[0]
+    narrow = me % 2 == 1
     n_lo, height, _ = grad_ref.shape
     rows = D // 4
     for t in range(n_lo):
-        zb_ref[t * height : (t + 1) * height, :] = grad_ref[t]
-    count = jnp.where(me_ref[0] % 2 == 0, float(D), float(KV_WIDTH))
-    grad_rows = zb_ref[...].T
-    for s in range(4):
-        out_ref[s, rows : 2 * rows, :] = grad_rows[s * rows : (s + 1) * rows, :]
-    z_ref[...] = old_ref[...] + zb_ref[...].astype(f32)
+        z_ref[t * height : (t + 1) * height, :] = grad_ref[t].astype(f32)
+    for j, piece in enumerate((m0, m1, m2, m3)):
+        here = pl.ds(pl.multiple_of((me ^ j) * rows, 16), rows)
+        z_ref[here, :] += MOMENTUM * piece[...].astype(f32)
     total, squares = normalize(z_ref, zb_ref)
-    sweeps(z_ref, zb_ref, rest_ref, rest_b_ref, poly_ref, squares, count, D, NS_STEPS)
-    ortho = zb_ref[...].T
+
+    @pl.when(narrow)
+    def _():
+        z_ref[...] = z_ref[...].T
+        zb_ref[...] = zb_ref[...].T
+        part = slice(0, KV_WIDTH)
+        sweeps(z_ref.at[part], zb_ref.at[part], *narrow_refs, squares, KV_WIDTH, NS_STEPS)
+        zb_ref[...] = zb_ref[...].T
+
+    @pl.when(jnp.logical_not(narrow))
+    def _():
+        sweeps(z_ref, zb_ref, rest_ref, rest_b_ref, poly_ref, squares, D, NS_STEPS)
+
+    count = jnp.where(narrow, float(KV_WIDTH), float(D))
     norm = norm_rows(total, count * D, (8, D))
     for s in range(4):
-        out_ref[s, 0:rows, :] = ortho[s * rows : (s + 1) * rows, :]
-        out_ref[s, 2 * rows :, :] = norm
+        out_ref[s, 0:rows, :] = zb_ref[s * rows : (s + 1) * rows, :]
+        out_ref[s, rows:, :] = norm
 
 
 def feed_new_body(
@@ -650,7 +676,7 @@
 
 
 def attn_new_body(
-    back_ref, feed_norm_ref, wq_ref, wkv_ref, wo_ref, mq_ref, mkv_ref, mo_ref,
+    back_ref, grad_ref, feed_norm_ref, wq_ref, wkv_ref, wo_ref, mq_ref, mkv_ref, mo_ref,
     gq, gkv, go, nq, nkv, no, uq, ukv, uo, norm_ref,
 ):
     rate = -RATE * SHAPE_SCALE * math.sqrt(D)
@@ -658,22 +684,17 @@
 
     def update(number, width, weight, old):
         ortho = back_ref[number, 0:rows, 0:width].astype(f32)
-        grad = back_ref[number, rows : 2 * rows, 0:width].astype(f32)
+        grad = grad_ref[number, :, 0:width].astype(f32)
         return grad, MOMENTUM * old + grad, weight.astype(f32) + rate * ortho
 
     gq[...], nq[...], uq[...] = update(0, D, wq_ref[...], mq_ref[...])
     go[...], no[...], uo[...] = update(2, D, wo_ref[...], mo_ref[...])
     for i, number in enumerate((1, 3)):
         gkv[i], nkv[i], ukv[i] = update(number, KV_WIDTH, wkv_ref[i], mkv_ref[i])
-    lane = lax.broadcasted_iota(jnp.int32, (1, 128), 1)
-    norms = jnp.zeros((1, 128), f32)
     for i, number in enumerate((0, 1, 3, 2)):
-        pair = back_ref[number, 2 * rows :, 0:1].astype(f32)
-        norms = jnp.where(lane == i, pair[0:1] + pair[1:2], norms)
+        norm_ref[i] = jnp.sum(back_ref[number, rows : rows + 2, 0:1].astype(f32))
     for i in range(3):
-        pair = feed_norm_ref[i, :, 0:1]
-        norms = jnp.where(lane == 4 + i, pair[0:1] + pair[1:2], norms)
-    norm_ref[...] = norms
+        norm_ref[4 + i] = jnp.sum(feed_norm_ref[i, 0:2, 0:1])
 
 
 def trade(x, axis):
@@ -758,7 +779,7 @@
     attn_in, query, kv, w_kvq, gains = call(
         functools.partial(project_body, tok),
         [
-            ((tok, D), bf16), ((tok, D), bf16), ((blocks, tok + 8, 2 * KV_WIDTH), bf16),
+            ((tok, D), bf16), ((tok, D), bf16), ((n_lo, tok + 8, 2 * KV_WIDTH), bf16),
             ((D, 2 * KV_WIDTH + D), bf16), ((8, D), f32),
         ],
         (me, xs) + attn_weights + (cosine, sine),
@@ -766,20 +787,22 @@
         smem=(0,),
         hold=(wide_parts[0],) + out_weights[1:],
     )
-    kv = deal(kv, LO + ("core",))
+    kv = deal(kv, LO)
     *attn_old, old_same, old_other = call(
         old_body,
         [((rows, D), bf16)] * n_shard + [((D, part), bf16)] * 2,
         (me, flags, mom_query, mom_kv, mom_out, mom_gate_up, mom_down.T),
         smem=(0, 1),
     )
+    kv = after(kv, old_same, cot, *wide_pieces[1:3])
+    kv_pair = (kv, trade(kv, "core"))
     w_o, attn_f, ffn_in, attn_rows, middle, lse = call(
         functools.partial(attend_body, tok, blocks),
         [
             ((D, D), bf16), ((tok, D), f32), ((tok, D), bf16), ((tok, D), bf16),
             ((tok, D), f32), ((KV_HEADS, wide), f32),
         ],
-        (me, xs, query, kv) + out_weights + (gains,),
+        (me, xs, query) + kv_pair + out_weights + (gains,),
         scratch=(
             pltpu.VMEM((KV_HEADS, blocks, tok, wide), f32),
             pltpu.VMEM((KV_HEADS, wide), f32),
@@ -787,10 +810,9 @@
             pltpu.VMEM((KV_HEADS, HEAD_DIM, wide), f32),
         ),
         smem=(0,),
-        hold=wide_pieces[1:] + (old_same,),
         limit=64,
     )
-    ffn_all = lax.all_gather(ffn_in, SHARD, axis=0, tiled=True)
+    ffn_all = lax.all_gather(after(ffn_in, wide_pieces[3]), SHARD, axis=0, tiled=True)
     old_same, old_other = after(old_same, ffn_all), after(old_other, ffn_all)
     attn_olds = pass_shard([attn_old[0]] + [after(old, ffn_all) for old in attn_old[1:]])
     olds = pass_shard((old_same, old_other, old_same, old_other))
@@ -816,13 +838,14 @@
             ((tok, D), f32), ((tok, D), bf16), ((tok, D), bf16),
             ((blocks, tok, 2 * KV_WIDTH), bf16), ((1, D), f32),
         ],
-        (dffn, xs, cot, middle, gains, w_o, attn_f, query, kv, lse, cosine, sine),
+        (flags, dffn, xs, cot, middle, gains, w_o, attn_f, query) + kv_pair + (lse, cosine, sine),
         scratch=(pltpu.VMEM((KV_HEADS, HEAD_DIM, wide), f32),),
+        smem=(0,),
     )
     (feed_sum,) = call(
         add_pieces_body, [((height, 3 * part), bf16)], tuple(feed_got), hold=(gain_two,)
     )
-    dkv = deal(after(dkv, *feed_got[1:], *olds[1:3], *attn_olds[1:]), LO + ("core",))
+    dkv = deal(after(dkv, *feed_got[1:], *olds[1:3], *attn_olds[1:]), ("core",) + LO)
     feed_other = trade(feed_sum, "hi")
     d_input, *sends = call(
         functools.partial(input_body, tok, rows),
@@ -865,19 +888,11 @@
     )
     attn_other = trade(attn_sum, "hi")
     results = lax.ppermute(finished, ALL, moves)
-    (attn_old_rows,) = call(
-        attn_old_body,
-        [((D, D), f32)],
-        (me,) + attn_olds,
-        scratch=(pltpu.VMEM((D, D), bf16),),
-        smem=(0,),
-        hold=(attn_sum,),
-    )
     attn_slots, gain_rows = call(
         add_second_body,
         [((n_lo, height, D), bf16), ((8, D), f32)],
         (attn_sum, attn_other),
-        hold=(attn_old_rows,),
+        hold=(results, olds[3]),
     )
     feed_same, feed_other = call(
         feed_ns_body,
@@ -888,7 +903,7 @@
             pltpu.VMEM((D, D), f32), pltpu.VMEM((D, D), bf16), pltpu.VMEM((D, D), bf16),
         ),
         smem=(0,),
-        hold=(attn_slots, results),
+        hold=(attn_slots,),
     )
     feed_back = (
         feed_same, trade(feed_other, "core"),
@@ -896,18 +911,17 @@
         lax.ppermute(feed_other, OWNER, [(0, 3), (2, 1)]),
     )
     attn_full = deal(attn_slots, LO)
+    attn_rows_back = deal(attn_full.reshape(n_shard, rows, D), SHARD)
     (attn_ortho,) = call(
         attn_ns_body,
-        [((n_shard, 2 * rows + 8, D), bf16)],
-        (me, attn_full, attn_old_rows),
-        scratch=(
-            pltpu.VMEM((D, D), f32), pltpu.VMEM((D, D), bf16), pltpu.VMEM((D, D), f32),
-            pltpu.VMEM((D, D), bf16), pltpu.VMEM((D, D), bf16),
-        ),
+        [((n_shard, rows + 8, D), bf16)],
+        (me, attn_full) + attn_olds,
+        scratch=[pltpu.VMEM((D, D), kind) for kind in (f32, bf16, f32, bf16, bf16)]
+        + [pltpu.VMEM((KV_WIDTH, KV_WIDTH), kind) for kind in (f32, bf16, bf16)],
         smem=(0,),
         hold=(feed_same,),
     )
-    attn_ortho = after(attn_ortho, *feed_back[2:])
+    attn_ortho = after(attn_ortho, feed_back[2])
     attn_back = deal(attn_ortho, SHARD)
     two = [((2, rows, FF), f32), ((D, part), f32)]
     grad_gate_up, grad_down, moment_gate_up, moment_down, new_gate_up, new_down, feed_norm = call(
@@ -920,13 +934,12 @@
     three = [((rows, D), f32), ((2, rows, KV_WIDTH), f32), ((rows, D), f32)]
     (
         grad_query, grad_kv, grad_out, moment_query, moment_kv, moment_out,
-        new_query, new_kv, new_out, norms,
+        new_query, new_kv, new_out, momentum_norms,
     ) = call(
         attn_new_body,
-        three * 3 + [((1, 128), f32)],
-        (attn_back, feed_norm, w_query, w_kv, w_out, mom_query, mom_kv, mom_out),
-    )
-    momentum_norms = norms[0, :7]
+        three * 3 + [((7,), f32)],
+        (attn_back, attn_rows_back, feed_norm, w_query, w_kv, w_out, mom_query, mom_kv, mom_out),
+    )
     grad_gains = gain_rows[:2, :rows]
     moment_gains = MOMENTUM * mom_gains + grad_gains
     all_tokens = tok * n_ctx * n_shard

time: 254 us -> 246 us (0.969)
  Pallas kernels: 104 us -> 97.5 us
  waiting for transfers between devices: 51.9 us -> 45.8 us
  starting transfers between devices: 77.5 us -> 81.3 us
    pallas_call x19 -> x18, Pallas kernels: 104 us -> 97.5 us  [call(): pl.pallas_call(run, name=getattr(body, 'func', body).__name__, out_shape=...]
    all_to_all x6 -> x7, waiting for transfers between devices: 13.2 us -> 7.24 us  [deal(): return lax.all_to_all(x, axis, 0, 0, tiled=True)]
    ppermute x24, starting transfers between devices: 24.5 us -> 20.1 us  [pass_on(): return lax.ppermute(x, axis, [(i, i ^ j) for i in range(size)])]
    ppermute x10 -> x11, starting transfers between devices: 11.4 us -> 15.3 us  [trade(): return lax.ppermute(x, axis, TRADE)]
    all_to_all x6 -> x7, starting transfers between devices: 26.1 us -> 29.8 us  [deal(): return lax.all_to_all(x, axis, 0, 0, tiled=True)]
    ppermute x10 -> x11, waiting for transfers between devices: 9.01 us -> 10.3 us  [trade(): return lax.ppermute(x, axis, TRADE)]
  transfers between devices with their start and end apart: 45 -> 47, of which waited for: 14 -> 13; matrix products, arithmetic and copies ran while one was open for 3% -> 3% of each run, Pallas kernels for 37% -> 35%
where the time goes in v1:
time: 246 us; the launch traced here: 245 us
  Pallas kernels  97.5 us (40%)
  starting transfers between devices  81.3 us (33%)
  waiting for transfers between devices  45.8 us (19%)
  blocking collectives  11.3 us (5%)
  other arithmetic  4.46 us (2%)
  local copies, waits for them, and re-layouts  2.66 us (1%)
    pallas_call x18, Pallas kernels, call(): pl.pallas_call(run, name=getattr(body, 'func', body).__name__, out_shape=...  97.5 us
    all_to_all x7, starting transfers between devices, deal(): return lax.all_to_all(x, axis, 0, 0, tiled=True)  29.8 us
    ppermute x24, waiting for transfers between devices, pass_on(): return lax.ppermute(x, axis, [(i, i ^ j) for i in range(size)])  28.2 us
    ppermute x24, starting transfers between devices, pass_on(): return lax.ppermute(x, axis, [(i, i ^ j) for i in range(size)])  20.1 us
    ppermute x11, starting transfers between devices, trade(): return lax.ppermute(x, axis, TRADE)  15.3 us
    all_gather x1, blocking collectives, on_device(): lax.all_gather(after(ffn_in, wide_pieces[3]), SHARD, axis=0, tiled=True)  11.3 us
    ppermute x11, waiting for transfers between devices, trade(): return lax.ppermute(x, axis, TRADE)  10.3 us
    all_to_all x7, waiting for transfers between devices, deal(): return lax.all_to_all(x, axis, 0, 0, tiled=True)  7.24 us
  transfers between devices with their start and end apart: 47, of which 13 were waited for; matrix products, arithmetic and copies ran while one was open for 3% of the time, Pallas kernels for 35%

profile of v1, /device:TPU:0, one launch (start us, length us, event | category | flops | bytes accessed | tf_op | source)
XLA Modules:
  0.0 244.6 jit_solution(431954558717122926)
XLA Ops:
  0.7 2.0 pack_body.1
  2.7 3.0 %collective-permute-start.2 = (bf16[152,960]{1,0:T(8,128)(2,1)}, bf16[152,960]{1,0:T(8,128)(2,1)}, u32[]{:S(2)}, u32[]{:S(2)}) collective-permute-start(bf16[152,960]{1,0:T(8,128)(2,1)} %get-tuple-element.89.refs_2_), channel_id=1, source_target_pairs={{0,2},{2,0},{1,3},{3,1},{4,6},{6,4},{5,7},{7,5},{8,10},{10,8},{9,1... | collective-permute-start | bytes 875528 | tf_op jit(solution)/shard_map/ppermute | solution.py:701
  5.6 2.9 %collective-permute-start = (bf16[136,576]{1,0:T(8,128)(2,1)}, bf16[136,576]{1,0:T(8,128)(2,1)}, u32[]{:S(2)}, u32[]{:S(2)}) collective-permute-start(bf16[136,576]{1,0:T(8,128)(2,1)} %get-tuple-element.88), channel_id=1, source_target_pairs={{0,0},{1,16},{2,2},{3,18},{4,4},{5,20},{6,6},{7,22},{8,8},{9,24},{... | collective-permute-start | bytes 470024 | tf_op jit(solution)/shard_map/ppermute | solution.py:753
  8.5 1.8 collective-permute-start.1
  11.3 2.1 pack_wide_body.1
  15.3 2.1 collective-permute-start.3
  17.5 1.6 fusion
  19.3 2.9 %project_body.1 = (bf16[128,576]{1,0:T(8,128)(2,1)}, bf16[128,576]{1,0:T(8,128)(2,1)}, bf16[4,136,384]{2,1,0:T(8,128)(2,1)}, bf16[576,960]{1,0:T(8,128)(2,1)}, f32[8,576]{1,0:T(8,128)}) custom-call(s32[1]{0:T(128)} %bitcast.refs_0_, bf16[136,576]{1,0:T(8,128)(2,1)} %collective-permute-done.refs_1_.refs_2_, bf16[152,960]{1,0:T(8,128)(2,1)} %get-tuple-element.89.refs_2_, ...), custom_call_target="tpu_custom_call" | custom-call | bytes 1024 | tf_op jit(solution)/shard_map/project_body/pallas_call | solution.py:60
  22.2 4.1 %all-to-all-start = ((bf16[4,136,384]{2,1,0:T(8,128)(2,1)}), bf16[4,136,384]{2,1,0:T(8,128)(2,1)}, u32[]{:S(2)}, u32[]{:S(2)}) async-start(bf16[4,136,384]{2,1,0:T(8,128)(2,1)} %get-tuple-element.92), calls=%async_computation | async-start | bytes 835584 | tf_op jit(solution)/shard_map/all_to_all | solution.py:713
  28.3 2.8 %collective-permute-start.7 = (bf16[576,128]{1,0:T(8,128)(2,1)}, bf16[576,128]{1,0:T(8,128)(2,1)}, u32[]{:S(2)}, u32[]{:S(2)}) collective-permute-start(bf16[576,128]{1,0:T(8,128)(2,1)} %bitcast.31), channel_id=1, source_target_pairs={{0,0},{1,16},{2,2},{3,18},{4,4},{5,20},{6,6},{7,22},{8,8},{9,24},{... | collective-permute-start | bytes 442376 | tf_op jit(solution)/shard_map/ppermute | solution.py:768
  31.7 3.4 %old_body.1 = (bf16[144,576]{1,0:T(8,128)(2,1)}, bf16[144,576]{1,0:T(8,128)(2,1)}, bf16[144,576]{1,0:T(8,128)(2,1)}, bf16[144,576]{1,0:T(8,128)(2,1)}, bf16[576,...) custom-call(s32[1]{0:T(128)} %bitcast.refs_0_, s32[5]{0:T(128)} %stack.20.refs_1_.refs_0_, f32[144,576]{1,0:T(8,128)} %refs_6_.1, ...), custom_call_target="tpu_custom_call" | custom-call | bytes 1024 | tf_op jit(solution)/shard_map/old_body/pallas_call | solution.py:60
  35.2 1.9 collective-permute-start.10
  39.2 5.1 %attend_body.1 = (bf16[576,576]{1,0:T(8,128)(2,1)}, f32[128,576]{1,0:T(8,128)}, bf16[128,576]{1,0:T(8,128)(2,1)}, bf16[128,576]{1,0:T(8,128)(2,1)}, f32[128,576]{1,0:T(8,128)}, /*index=5*/f32[3,384]{1,0:T(4,128)}) custom-call(s32[1]{0:T(128)} %bitcast.refs_0_, bf16[136,576]{1,0:T(8,128)(2,1)} %collective-permute-done.refs_1_.refs_2_, ...), custom_call_target="tpu_custom_call" | custom-call | bytes 1024 | tf_op jit(solution)/shard_map/attend_body/pallas_call | solution.py:60
  44.9 11.3 %all_gather.3.refs_2_.refs_1_ = bf16[512,576]{1,0:T(8,128)(2,1)} all-gather(bf16[128,576]{1,0:T(8,128)(2,1)} %after.11), channel_id=1, replica_groups=mesh['hi'=2,'lh'=2,'lx'=2,'y'=2,'core'=2] {'y','core'}, dimensions={0}, use_global_device_ids=true | all-gather | bytes 737280 | tf_op jit(solution)/shard_map/all_gather | solution.py:815
  58.1 6.7 %feed_body.1 = (bf16[256,576]{1,0:T(8,128)(2,1)}, bf16[256,576]{1,0:T(8,128)(2,1)}, bf16[256,576]{1,0:T(8,128)(2,1)}, bf16[256,576]{1,0:T(8,128)(2,1)}, bf16[4,1...) custom-call(s32[1]{0:T(128)} %bitcast.refs_0_, ...), custom_call_target="tpu_custom_call" | custom-call | bytes 1024 | tf_op jit(solution)/shard_map/feed_body/pallas_call | solution.py:60
  64.8 4.4 %all-to-all-start.1 = ((bf16[4,136,576]{2,1,0:T(8,128)(2,1)}), bf16[4,136,576]{2,1,0:T(8,128)(2,1)}, u32[]{:S(2)}, u32[]{:S(2)}) async-start(bf16[4,136,576]{2,1,0:T(8,128)(2,1)} %get-tuple-element.102), calls=%async_computation.1 | async-start | bytes 1392640 | tf_op jit(solution)/shard_map/all_to_all | solution.py:713
  71.1 2.2 collective-permute-start.15
  74.9 5.3 %all-to-all-done.1.refs_1_ = bf16[4,136,576]{2,1,0:T(8,128)(2,1)} async-done(((bf16[4,136,576]{2,1,0:T(8,128)(2,1)}), bf16[4,136,576]{2,1,0:T(8,128)(2,1)}, u32[]{:S(2)}, u32[]{:S(2)}) %all-to-all-start.1) | async-done | bytes 626720 | tf_op jit(solution)/shard_map/all_to_all | solution.py:713
  80.2 6.9 %back_body.1 = (f32[128,576]{1,0:T(8,128)}, bf16[128,576]{1,0:T(8,128)(2,1)}, bf16[128,576]{1,0:T(8,128)(2,1)}, bf16[8,128,384]{2,1,0:T(8,128)(2,1)}, f32[1,576]{1,0:T(1,128)}) custom-call(s32[5]{0:T(128)} %stack.20.refs_1_.refs_0_, bf16[4,136,576]{2,1,0:T(8,128)(2,1)} %all-to-all-done.1.refs_1_, bf16[136,576]{1,0:T(8,128)(2,1)} %collective-permute-done.refs_1_.refs_2_, ...), custom_call_target="tpu_custom_call" | custom-call | bytes 1024 | tf_op jit(solution)/shard_map/back_body/pallas_call | solution.py:60
  87.2 2.9 %collective-permute-done.17.refs_3_ = bf16[144,1152]{1,0:T(8,128)(2,1)} collective-permute-done((bf16[144,1152]{1,0:T(8,128)(2,1)}, bf16[144,1152]{1,0:T(8,128)(2,1)}, u32[]{:S(2)}, u32[]{:S(2)}) %collective-permute-start.17) | collective-permute-done | bytes 331808 | tf_op jit(solution)/shard_map/ppermute | solution.py:705
  90.1 4.2 %all-to-all-start.2 = ((bf16[8,128,384]{2,1,0:T(8,128)(2,1)}), bf16[8,128,384]{2,1,0:T(8,128)(2,1)}, u32[]{:S(2)}, u32[]{:S(2)}) async-start(bf16[8,128,384]{2,1,0:T(8,128)(2,1)} %after.17), calls=%async_computation.2 | async-start | bytes 1572864 | tf_op jit(solution)/shard_map/all_to_all | solution.py:713
  94.3 2.2 add_pieces_body.3.refs_0_
  96.5 2.4 collective-permute-start.35
  100.8 9.0 %collective-permute-done.24.refs_12_.refs_4_.refs_8_ = bf16[256,576]{1,0:T(8,128)(2,1)} collective-permute-done((bf16[256,576]{1,0:T(8,128)(2,1)}, bf16[256,576]{1,0:T(8,128)(2,1)}, u32[]{:S(2)}, u32[]{:S(2)}) %collective-permute-start.24) | collective-permute-done | bytes 294944 | tf_op jit(solution)/shard_map/ppermute | solution.py:705
  109.9 5.9 %collective-permute-done.25.refs_13_.refs_5_.refs_9_ = bf16[256,576]{1,0:T(8,128)(2,1)} collective-permute-done((bf16[256,576]{1,0:T(8,128)(2,1)}, bf16[256,576]{1,0:T(8,128)(2,1)}, u32[]{:S(2)}, u32[]{:S(2)}) %collective-permute-start.25) | collective-permute-done | bytes 294944 | tf_op jit(solution)/shard_map/ppermute | solution.py:705
  115.7 3.5 %input_body.1 = (f32[128,576]{1,0:T(8,128)}, bf16[136,576]{1,0:T(8,128)(2,1)}, bf16[136,576]{1,0:T(8,128)(2,1)}, bf16[136,576]{1,0:T(8,128)(2,1)}, bf16[136,576]{1,0:T(8,128)(2,1)}) custom-call(s32[1]{0:T(128)} %bitcast.refs_0_, bf16[8,128,384]{2,1,0:T(8,128)(2,1)} %all-to-all-done.2.refs_1_, bf16[136,576]{1,0:T(8,128)(2,1)} %collective-permute-done.refs_1_.refs_2_, ...), custom_call_target="tpu_custom_call" | custom-call | bytes 1024 | tf_op jit(solution)/shard_map/input_body/pallas_call | solution.py:60
  119.2 2.1 add_slots_body.1
  121.3 4.4 %all-to-all-start.4 = ((bf16[8,144,384]{2,1,0:T(8,128)(2,1)}), bf16[8,144,384]{2,1,0:T(8,128)(2,1)}, u32[]{:S(2)}, u32[]{:S(2)}) async-start(bf16[8,144,384]{2,1,0:T(8,128)(2,1)} %bitcast.24), calls=%async_computation.4 | async-start | bytes 1769472 | tf_op jit(solution)/shard_map/all_to_all | solution.py:713
  127.7 5.9 %collective-permute-done.28.refs_4_ = bf16[136,576]{1,0:T(8,128)(2,1)} collective-permute-done((bf16[136,576]{1,0:T(8,128)(2,1)S(1)}, bf16[136,576]{1,0:T(8,128)(2,1)}, u32[]{:S(2)}, u32[]{:S(2)}) %collective-permute-start.28) | collective-permute-done | bytes 156704 | tf_op jit(solution)/shard_map/ppermute | solution.py:705
  133.6 2.0 collective-permute-done.29.refs_5_
  135.6 3.1 %attn_grad_body.1 = (bf16[152,576]{1,0:T(8,128)(2,1)}, bf16[152,576]{1,0:T(8,128)(2,1)}, bf16[152,576]{1,0:T(8,128)(2,1)}, bf16[152,576]{1,0:T(8,128)(2,1)}) custom-call(s32[1]{0:T(128)} %bitcast.refs_0_, s32[1]{0:T(128)} %bitcast.11.refs_1_, bf16[136,576]{1,0:T(8,128)(2,1)} %get-tuple-element.124.refs_2_, bf16[136,576]{1,0:T(8,128)(2,1)} %collective-permute-done.27.refs_3_, ...), custom_call_target="tpu_custom_call" | custom-call | bytes 1024 | tf_op jit(solution)/shard_map/attn_grad_body/pallas_call | solution.py:60
  138.7 2.2 collective-permute-start.30
  143.3 2.4 finish_body.1.refs_4_
  145.7 3.8 %collective-permute-start.26 = (bf16[2,576,128]{2,1,0:T(8,128)(2,1)}, bf16[2,576,128]{2,1,0:T(8,128)(2,1)}, u32[]{:S(2)}, u32[]{:S(2)}) collective-permute-start(bf16[2,576,128]{2,1,0:T(8,128)(2,1)} %finish_body.1.refs_4_), channel_id=1, source_target_pairs={{0,0},{1,16},{2,2},{3,18},{4,4},{5,20},{6,6},{7,22},{8,8},{9,24},{... | collective-permute-start | bytes 884744 | tf_op jit(solution)/shard_map/ppermute | solution.py:890
  151.0 1.7 collective-permute-done.32.refs_3_
  152.8 2.0 add_pieces_body.2.refs_0_
  156.4 9.8 %collective-permute-done.33.refs_1_ = bf16[152,576]{1,0:T(8,128)(2,1)} collective-permute-done((bf16[152,576]{1,0:T(8,128)(2,1)}, bf16[152,576]{1,0:T(8,128)(2,1)}, u32[]{:S(2)}, u32[]{:S(2)}) %collective-permute-start.33) | collective-permute-done | bytes 175136 | tf_op jit(solution)/shard_map/ppermute | solution.py:701
  166.2 1.9 add_second_body.1
  168.1 4.2 %all-to-all-start.3 = ((bf16[4,144,576]{2,1,0:T(8,128)(2,1)}), bf16[4,144,576]{2,1,0:T(8,128)(2,1)}, u32[]{:S(2)}, u32[]{:S(2)}) async-start(bf16[4,144,576]{2,1,0:T(8,128)(2,1)} %get-tuple-element.133.refs_7_), calls=%async_computation.3 | async-start | bytes 1474560 | tf_op jit(solution)/shard_map/all_to_all | solution.py:713
  172.7 25.5 %feed_ns_body.1 = (bf16[1160,384]{1,0:T(8,128)(2,1)}, bf16[1160,384]{1,0:T(8,128)(2,1)}) custom-call(s32[5]{0:T(128)} %stack.20.refs_1_.refs_0_, bf16[4,2,144,384]{3,2,1,0:T(8,128)(2,1)} %after.18.refs_1_, bf16[4,2,144,384]{3,2,1,0:T(8,128)(2,1)} %collective-permute-done.36.refs_2_, bf16[576,384]{1,0:T(8,128)(2,1)} %after.13.refs_3_, ...), custom_call_target="tpu_custom_call" | custom-call | bytes 1024 | tf_op jit(solution)/shard_map/feed_ns_body/pallas_call | solution.py:60
  198.2 4.0 %collective-permute-start.37 = (bf16[1160,384]{1,0:T(8,128)(2,1)}, bf16[1160,384]{1,0:T(8,128)(2,1)}, u32[]{:S(2)}, u32[]{:S(2)}) collective-permute-start(bf16[1160,384]{1,0:T(8,128)(2,1)} %get-tuple-element.136.refs_6_.refs_1_), channel_id=1, source_target_pairs={{0,4},{4,0},{2,6},{6,2},{8,12},{12,8},{10,14},{14,10},{16,20},{20,... | collective-permute-start | bytes 2672648 | tf_op jit(solution)/shard_map/ppermute | solution.py:910
  202.2 4.2 %all-to-all-start.6 = ((bf16[4,144,576]{2,1,0:T(8,128)(2,1)}), bf16[4,144,576]{2,1,0:T(8,128)(2,1)}, u32[]{:S(2)}, u32[]{:S(2)}) async-start(bf16[4,144,576]{2,1,0:T(8,128)(2,1)} %all-to-all-done.3.refs_1_), calls=%async_computation.6 | async-start | bytes 1474560 | tf_op jit(solution)/shard_map/all_to_all | solution.py:713
  206.9 2.6 %collective-permute-start.39 = (bf16[1160,384]{1,0:T(8,128)(2,1)}, bf16[1160,384]{1,0:T(8,128)(2,1)}, u32[]{:S(2)}, u32[]{:S(2)}) collective-permute-start(bf16[1160,384]{1,0:T(8,128)(2,1)} %get-tuple-element.137), channel_id=1, source_target_pairs={{0,5},{4,1},{2,7},{6,3},{8,13},{12,9},{10,15},{14,11},{16,21},{20,... | collective-permute-start | bytes 2672648 | tf_op jit(solution)/shard_map/ppermute | solution.py:911
  209.5 15.3 %attn_ns_body.1.refs_0_ = bf16[4,152,576]{2,1,0:T(8,128)(2,1)} custom-call(s32[1]{0:T(128)} %bitcast.refs_0_, bf16[4,144,576]{2,1,0:T(8,128)(2,1)} %all-to-all-done.3.refs_1_, bf16[144,576]{1,0:T(8,128)(2,1)} %get-tuple-element.134.refs_2_, bf16[144,576]{1,0:T(8,128)(2,1)} %collective-permute-done.20.refs_6_.refs_3_, ...), custom_call_target="tpu_custom_call" | custom-call | bytes 1024 | tf_op jit(solution)/shard_map/attn_ns_body/pallas_call | solution.py:60
  224.8 4.3 %all-to-all-start.5 = ((bf16[4,152,576]{2,1,0:T(8,128)(2,1)}), bf16[4,152,576]{2,1,0:T(8,128)(2,1)}, u32[]{:S(2)}, u32[]{:S(2)}) async-start(bf16[4,152,576]{2,1,0:T(8,128)(2,1)} %after.19.refs_9_), calls=%async_computation.5 | async-start | bytes 1556480 | tf_op jit(solution)/shard_map/all_to_all | solution.py:713
  232.3 6.5 %feed_new_body.1 = (f32[2,144,1536]{2,1,0:T(8,128)}, f32[576,384]{1,0:T(8,128)}, f32[2,144,1536]{2,1,0:T(8,128)}, f32[576,384]{1,0:T(8,128)}, f32[2,144,1536]{2,...) custom-call(s32[5]{0:T(128)} %stack.20.refs_1_.refs_0_, bf16[1160,384]{1,0:T(8,128)(2,1)} %get-tuple-element.136.refs_6_.refs_1_, ...), custom_call_target="tpu_custom_call" | custom-call | bytes 1024 | tf_op jit(solution)/shard_map/feed_new_body/pallas_call | solution.py:60
  238.8 1.9 all-to-all-done.5.refs_0_
  240.8 3.7 %attn_new_body.1 = (f32[144,576]{1,0:T(8,128)}, f32[2,144,192]{2,1,0:T(8,128)}, f32[144,576]{1,0:T(8,128)}, f32[144,576]{1,0:T(8,128)}, f32[2,144,192]{2,1,0:T(8...) custom-call(bf16[4,152,576]{2,1,0:T(8,128)(2,1)} %all-to-all-done.5., ...), custom_call_target="tpu_custom_call" | custom-call | bytes 1024 | tf_op jit(solution)/shard_map/attn_new_body/pallas_call | solution.py:60
  (93 shorter events, 26.6 us)
Async XLA Ops:
  2.7 12.7 %collective-permute-start.2 = (bf16[152,960]{1,0:T(8,128)(2,1)}, bf16[152,960]{1,0:T(8,128)(2,1)}, u32[]{:S(2)}, u32[]{:S(2)}) collective-permute-start(bf16[152,960]{1,0:T(8,128)(2,1)} %get-tuple-element.89.refs_2_), channel_id=1, source_target_pairs={{0,2},{2,0},{1,3},{3,1},{4,6},{6,4},{5,7},{7,5},{8,10},{10,8},{9,1... | collective-permute-start | bytes 875528 | tf_op jit(solution)/shard_map/ppermute | solution.py:701
  5.6 7.9 %collective-permute-start = (bf16[136,576]{1,0:T(8,128)(2,1)}, bf16[136,576]{1,0:T(8,128)(2,1)}, u32[]{:S(2)}, u32[]{:S(2)}) collective-permute-start(bf16[136,576]{1,0:T(8,128)(2,1)} %get-tuple-element.88), channel_id=1, source_target_pairs={{0,0},{1,16},{2,2},{3,18},{4,4},{5,20},{6,6},{7,22},{8,8},{9,24},{... | collective-permute-start | bytes 470024 | tf_op jit(solution)/shard_map/ppermute | solution.py:753
  8.5 10.6 %collective-permute-start.1 = (bf16[152,960]{1,0:T(8,128)(2,1)}, bf16[152,960]{1,0:T(8,128)(2,1)}, u32[]{:S(2)}, u32[]{:S(2)}) collective-permute-start(bf16[152,960]{1,0:T(8,128)(2,1)} %get-tuple-element.89.refs_2_), channel_id=1, source_target_pairs={{0,1},{1,0},{2,3},{3,2},{4,5},{5,4},{6,7},{7,6},{8,9},{9,8},{10,11... | collective-permute-start | bytes 875528 | tf_op jit(solution)/shard_map/ppermute | solution.py:701
  10.3 7.1 %collective-permute-start.5 = (bf16[144,576]{1,0:T(8,128)(2,1)}, bf16[144,576]{1,0:T(8,128)(2,1)}, u32[]{:S(2)}, u32[]{:S(2)}) collective-permute-start(bf16[144,576]{1,0:T(8,128)(2,1)} %refs_5_.7), channel_id=1, source_target_pairs={{0,2},{2,0},{1,3},{3,1},{4,6},{6,4},{5,7},{7,5},{8,10},{10,8},{9,1... | collective-permute-start | bytes 497672 | tf_op jit(solution)/shard_map/ppermute | solution.py:701
  10.8 8.4 %collective-permute-start.4 = (bf16[144,576]{1,0:T(8,128)(2,1)}, bf16[144,576]{1,0:T(8,128)(2,1)}, u32[]{:S(2)}, u32[]{:S(2)}) collective-permute-start(bf16[144,576]{1,0:T(8,128)(2,1)} %refs_5_.7), channel_id=1, source_target_pairs={{0,1},{1,0},{2,3},{3,2},{4,5},{5,4},{6,7},{7,6},{8,9},{9,8},{10,11... | collective-permute-start | bytes 497672 | tf_op jit(solution)/shard_map/ppermute | solution.py:701
  15.3 3.9 %collective-permute-start.3 = (bf16[152,960]{1,0:T(8,128)(2,1)}, bf16[152,960]{1,0:T(8,128)(2,1)}, u32[]{:S(2)}, u32[]{:S(2)}) collective-permute-start(bf16[152,960]{1,0:T(8,128)(2,1)} %collective-permute-done.2.refs_4_), channel_id=1, source_target_pairs={{0,1},{1,0},{2,3},{3,2},{4,5},{5,4},{6,7},{7,6},{8,9},{9,8},{10,11... | collective-permute-start | bytes 875528 | tf_op jit(solution)/shard_map/ppermute | solution.py:701
  17.4 1.8 collective-permute-start.6
  22.2 13.0 %all-to-all-start = ((bf16[4,136,384]{2,1,0:T(8,128)(2,1)}), bf16[4,136,384]{2,1,0:T(8,128)(2,1)}, u32[]{:S(2)}, u32[]{:S(2)}) async-start(bf16[4,136,384]{2,1,0:T(8,128)(2,1)} %get-tuple-element.92), calls=%async_computation | async-start | bytes 835584 | tf_op jit(solution)/shard_map/all_to_all | solution.py:713
  26.3 8.9 %collective-permute-start.8 = (bf16[144,768]{1,0:T(8,128)(2,1)}, bf16[144,768]{1,0:T(8,128)(2,1)}, u32[]{:S(2)}, u32[]{:S(2)}) collective-permute-start(bf16[144,768]{1,0:T(8,128)(2,1)} %get-tuple-element.94), channel_id=1, source_target_pairs={{0,1},{1,0},{2,3},{3,2},{4,5},{5,4},{6,7},{7,6},{8,9},{9,8},{10,11... | collective-permute-start | bytes 663560 | tf_op jit(solution)/shard_map/ppermute | solution.py:705
  26.8 8.4 %collective-permute-start.9 = (bf16[144,768]{1,0:T(8,128)(2,1)}, bf16[144,768]{1,0:T(8,128)(2,1)}, u32[]{:S(2)}, u32[]{:S(2)}) collective-permute-start(bf16[144,768]{1,0:T(8,128)(2,1)} %get-tuple-element.95), channel_id=1, source_target_pairs={{0,2},{1,3},{2,0},{3,1},{4,6},{5,7},{6,4},{7,5},{8,10},{9,11},{10,... | collective-permute-start | bytes 663560 | tf_op jit(solution)/shard_map/ppermute | solution.py:705
  28.3 6.9 %collective-permute-start.7 = (bf16[576,128]{1,0:T(8,128)(2,1)}, bf16[576,128]{1,0:T(8,128)(2,1)}, u32[]{:S(2)}, u32[]{:S(2)}) collective-permute-start(bf16[576,128]{1,0:T(8,128)(2,1)} %bitcast.31), channel_id=1, source_target_pairs={{0,0},{1,16},{2,2},{3,18},{4,4},{5,20},{6,6},{7,22},{8,8},{9,24},{... | collective-permute-start | bytes 442376 | tf_op jit(solution)/shard_map/ppermute | solution.py:768
  35.2 4.0 %collective-permute-start.10 = (bf16[4,136,384]{2,1,0:T(8,128)(2,1)}, bf16[4,136,384]{2,1,0:T(8,128)(2,1)}, u32[]{:S(2)}, u32[]{:S(2)}) collective-permute-start(bf16[4,136,384]{2,1,0:T(8,128)(2,1)} %after.10.refs_3_.refs_9_), channel_id=1, source_target_pairs={{0,1},{1,0},{2,3},{3,2},{4,5},{5,4},{6,7},{7,6},{8,9},{9,8},{10,11... | collective-permute-start | bytes 1253384 | tf_op jit(solution)/shard_map/ppermute | solution.py:701
  37.1 7.8 %collective-permute-start.11 = (bf16[144,768]{1,0:T(8,128)(2,1)}, bf16[144,768]{1,0:T(8,128)(2,1)}, u32[]{:S(2)}, u32[]{:S(2)}) collective-permute-start(bf16[144,768]{1,0:T(8,128)(2,1)} %get-tuple-element.99), channel_id=1, source_target_pairs={{0,3},{1,2},{2,1},{3,0},{4,7},{5,6},{6,5},{7,4},{8,11},{9,10},{10,... | collective-permute-start | bytes 663560 | tf_op jit(solution)/shard_map/ppermute | solution.py:705
  37.3 19.7 %collective-permute-start.12 = (bf16[576,128]{1,0:T(8,128)(2,1)}, bf16[576,128]{1,0:T(8,128)(2,1)}, u32[]{:S(2)}, u32[]{:S(2)}) collective-permute-start(bf16[576,128]{1,0:T(8,128)(2,1)} %collective-permute-done.7.refs_2_.refs_3_), channel_id=1, source_target_pairs={{0,1},{1,0},{2,3},{3,2},{4,5},{5,4},{6,7},{7,6},{8,9},{9,8},{10,11... | collective-permute-start | bytes 442376 | tf_op jit(solution)/shard_map/ppermute | solution.py:705
  37.7 20.3 %collective-permute-start.13 = (bf16[576,128]{1,0:T(8,128)(2,1)}, bf16[576,128]{1,0:T(8,128)(2,1)}, u32[]{:S(2)}, u32[]{:S(2)}) collective-permute-start(bf16[576,128]{1,0:T(8,128)(2,1)} %collective-permute-done.7.refs_2_.refs_3_), channel_id=1, source_target_pairs={{0,2},{1,3},{2,0},{3,1},{4,6},{5,7},{6,4},{7,5},{8,10},{9,11},{10,... | collective-permute-start | bytes 442376 | tf_op jit(solution)/shard_map/ppermute | solution.py:705
  39.2 18.8 %collective-permute-start.14 = (bf16[576,128]{1,0:T(8,128)(2,1)}, bf16[576,128]{1,0:T(8,128)(2,1)}, u32[]{:S(2)}, u32[]{:S(2)}) collective-permute-start(bf16[576,128]{1,0:T(8,128)(2,1)} %collective-permute-done.7.refs_2_.refs_3_), channel_id=1, source_target_pairs={{0,3},{1,2},{2,1},{3,0},{4,7},{5,6},{6,5},{7,4},{8,11},{9,10},{10,... | collective-permute-start | bytes 442376 | tf_op jit(solution)/shard_map/ppermute | solution.py:705
  56.2 14.9 %collective-permute-start.20 = (bf16[144,576]{1,0:T(8,128)(2,1)}, bf16[144,576]{1,0:T(8,128)(2,1)}, u32[]{:S(2)}, u32[]{:S(2)}) collective-permute-start(bf16[144,576]{1,0:T(8,128)(2,1)} %after.14), channel_id=1, source_target_pairs={{0,1},{1,0},{2,3},{3,2},{4,5},{5,4},{6,7},{7,6},{8,9},{9,8},{10,11... | collective-permute-start | bytes 497672 | tf_op jit(solution)/shard_map/ppermute | solution.py:705
  56.5 16.8 %collective-permute-start.21 = (bf16[144,576]{1,0:T(8,128)(2,1)}, bf16[144,576]{1,0:T(8,128)(2,1)}, u32[]{:S(2)}, u32[]{:S(2)}) collective-permute-start(bf16[144,576]{1,0:T(8,128)(2,1)} %after.15), channel_id=1, source_target_pairs={{0,2},{1,3},{2,0},{3,1},{4,6},{5,7},{6,4},{7,5},{8,10},{9,11},{10,... | collective-permute-start | bytes 497672 | tf_op jit(solution)/shard_map/ppermute | solution.py:705
  57.0 17.2 %collective-permute-start.22 = (bf16[144,576]{1,0:T(8,128)(2,1)}, bf16[144,576]{1,0:T(8,128)(2,1)}, u32[]{:S(2)}, u32[]{:S(2)}) collective-permute-start(bf16[144,576]{1,0:T(8,128)(2,1)} %after.16), channel_id=1, source_target_pairs={{0,3},{1,2},{2,1},{3,0},{4,7},{5,6},{6,5},{7,4},{8,11},{9,10},{10,... | collective-permute-start | bytes 497672 | tf_op jit(solution)/shard_map/ppermute | solution.py:705
  64.8 15.4 %all-to-all-start.1 = ((bf16[4,136,576]{2,1,0:T(8,128)(2,1)}), bf16[4,136,576]{2,1,0:T(8,128)(2,1)}, u32[]{:S(2)}, u32[]{:S(2)}) async-start(bf16[4,136,576]{2,1,0:T(8,128)(2,1)} %get-tuple-element.102), calls=%async_computation.1 | async-start | bytes 1392640 | tf_op jit(solution)/shard_map/all_to_all | solution.py:713
  69.2 20.9 %collective-permute-start.18 = (bf16[576,384]{1,0:T(8,128)(2,1)}, bf16[576,384]{1,0:T(8,128)(2,1)}, u32[]{:S(2)}, u32[]{:S(2)}) collective-permute-start(bf16[576,384]{1,0:T(8,128)(2,1)} %after.12), channel_id=1, source_target_pairs={{0,1},{1,0},{2,3},{3,2},{4,5},{5,4},{6,7},{7,6},{8,9},{9,8},{10,11... | collective-permute-start | bytes 1327112 | tf_op jit(solution)/shard_map/ppermute | solution.py:705
  69.9 20.2 %collective-permute-start.19 = (bf16[576,384]{1,0:T(8,128)(2,1)}, bf16[576,384]{1,0:T(8,128)(2,1)}, u32[]{:S(2)}, u32[]{:S(2)}) collective-permute-start(bf16[576,384]{1,0:T(8,128)(2,1)} %after.13.refs_3_), channel_id=1, source_target_pairs={{0,2},{1,3},{2,0},{3,1},{4,6},{5,7},{6,4},{7,5},{8,10},{9,11},{10,... | collective-permute-start | bytes 1327112 | tf_op jit(solution)/shard_map/ppermute | solution.py:705
  71.1 16.0 %collective-permute-start.15 = (bf16[144,1152]{1,0:T(8,128)(2,1)}, bf16[144,1152]{1,0:T(8,128)(2,1)}, u32[]{:S(2)}, u32[]{:S(2)}) collective-permute-start(bf16[144,1152]{1,0:T(8,128)(2,1)} %get-tuple-element.107), channel_id=1, source_target_pairs={{0,4},{4,0},{8,12},{12,8},{1,5},{5,1},{9,13},{13,9},{2,6},{6,2},{1... | collective-permute-start | bytes 995336 | tf_op jit(solution)/shard_map/ppermute | solution.py:705
  73.4 13.8 %collective-permute-start.16 = (bf16[144,1152]{1,0:T(8,128)(2,1)}, bf16[144,1152]{1,0:T(8,128)(2,1)}, u32[]{:S(2)}, u32[]{:S(2)}) collective-permute-start(bf16[144,1152]{1,0:T(8,128)(2,1)} %get-tuple-element.108), channel_id=1, source_target_pairs={{0,8},{4,12},{8,0},{12,4},{1,9},{5,13},{9,1},{13,5},{2,10},{6,14},... | collective-permute-start | bytes 995336 | tf_op jit(solution)/shard_map/ppermute | solution.py:705
  74.3 15.8 %collective-permute-start.17 = (bf16[144,1152]{1,0:T(8,128)(2,1)}, bf16[144,1152]{1,0:T(8,128)(2,1)}, u32[]{:S(2)}, u32[]{:S(2)}) collective-permute-start(bf16[144,1152]{1,0:T(8,128)(2,1)} %get-tuple-element.109), channel_id=1, source_target_pairs={{0,12},{4,8},{8,4},{12,0},{1,13},{5,9},{9,5},{13,1},{2,14},{6,10},... | collective-permute-start | bytes 995336 | tf_op jit(solution)/shard_map/ppermute | solution.py:705
  90.1 25.7 %all-to-all-start.2 = ((bf16[8,128,384]{2,1,0:T(8,128)(2,1)}), bf16[8,128,384]{2,1,0:T(8,128)(2,1)}, u32[]{:S(2)}, u32[]{:S(2)}) async-start(bf16[8,128,384]{2,1,0:T(8,128)(2,1)} %after.17), calls=%async_computation.2 | async-start | bytes 1572864 | tf_op jit(solution)/shard_map/all_to_all | solution.py:713
  96.5 22.7 %collective-permute-start.35 = (bf16[144,1152]{1,0:T(8,128)(2,1)}, bf16[144,1152]{1,0:T(8,128)(2,1)}, u32[]{:S(2)}, u32[]{:S(2)}) collective-permute-start(bf16[144,1152]{1,0:T(8,128)(2,1)} %add_pieces_body.3.refs_0_), channel_id=1, source_target_pairs={{0,16},{16,0},{1,17},{17,1},{2,18},{18,2},{3,19},{19,3},{4,20},{20... | collective-permute-start | bytes 995336 | tf_op jit(solution)/shard_map/ppermute | solution.py:701
  98.8 2.0 collective-permute-start.23
  99.0 10.9 %collective-permute-start.24 = (bf16[256,576]{1,0:T(8,128)(2,1)}, bf16[256,576]{1,0:T(8,128)(2,1)}, u32[]{:S(2)}, u32[]{:S(2)}) collective-permute-start(bf16[256,576]{1,0:T(8,128)(2,1)} %get-tuple-element.120), channel_id=1, source_target_pairs={{0,2},{1,3},{2,0},{3,1},{4,6},{5,7},{6,4},{7,5},{8,10},{9,11},{10,... | collective-permute-start | bytes 884744 | tf_op jit(solution)/shard_map/ppermute | solution.py:705
  99.5 16.2 %collective-permute-start.25 = (bf16[256,576]{1,0:T(8,128)(2,1)}, bf16[256,576]{1,0:T(8,128)(2,1)}, u32[]{:S(2)}, u32[]{:S(2)}) collective-permute-start(bf16[256,576]{1,0:T(8,128)(2,1)} %get-tuple-element.121), channel_id=1, source_target_pairs={{0,3},{1,2},{2,1},{3,0},{4,7},{5,6},{6,5},{7,4},{8,11},{9,10},{10,... | collective-permute-start | bytes 884744 | tf_op jit(solution)/shard_map/ppermute | solution.py:705
  121.3 28.2 %all-to-all-start.4 = ((bf16[8,144,384]{2,1,0:T(8,128)(2,1)}), bf16[8,144,384]{2,1,0:T(8,128)(2,1)}, u32[]{:S(2)}, u32[]{:S(2)}) async-start(bf16[8,144,384]{2,1,0:T(8,128)(2,1)} %bitcast.24), calls=%async_computation.4 | async-start | bytes 1769472 | tf_op jit(solution)/shard_map/all_to_all | solution.py:713
  125.7 1.9 collective-permute-start.27
  126.2 7.4 %collective-permute-start.28 = (bf16[136,576]{1,0:T(8,128)(2,1)S(1)}, bf16[136,576]{1,0:T(8,128)(2,1)}, u32[]{:S(2)}, u32[]{:S(2)}) collective-permute-start(bf16[136,576]{1,0:T(8,128)(2,1)S(1)} %copy-done.3), channel_id=1, source_target_pairs={{0,2},{1,3},{2,0},{3,1},{4,6},{5,7},{6,4},{7,5},{8,10},{9,11},{10,... | collective-permute-start | bytes 470024 | tf_op jit(solution)/shard_map/ppermute | solution.py:705
  126.8 8.8 %collective-permute-start.29 = (bf16[136,576]{1,0:T(8,128)(2,1)S(1)}, bf16[136,576]{1,0:T(8,128)(2,1)}, u32[]{:S(2)}, u32[]{:S(2)}) collective-permute-start(bf16[136,576]{1,0:T(8,128)(2,1)S(1)} %copy-done.2), channel_id=1, source_target_pairs={{0,3},{1,2},{2,1},{3,0},{4,7},{5,6},{6,5},{7,4},{8,11},{9,10},{10,... | collective-permute-start | bytes 470024 | tf_op jit(solution)/shard_map/ppermute | solution.py:705
  138.7 10.8 %collective-permute-start.30 = (bf16[152,576]{1,0:T(8,128)(2,1)}, bf16[152,576]{1,0:T(8,128)(2,1)}, u32[]{:S(2)}, u32[]{:S(2)}) collective-permute-start(bf16[152,576]{1,0:T(8,128)(2,1)} %get-tuple-element.129), channel_id=1, source_target_pairs={{0,4},{4,0},{8,12},{12,8},{1,5},{5,1},{9,13},{13,9},{2,6},{6,2},{1... | collective-permute-start | bytes 525320 | tf_op jit(solution)/shard_map/ppermute | solution.py:705
  140.9 15.4 %collective-permute-start.34 = (bf16[576,384]{1,0:T(8,128)(2,1)}, bf16[576,384]{1,0:T(8,128)(2,1)}, u32[]{:S(2)}, u32[]{:S(2)}) collective-permute-start(bf16[576,384]{1,0:T(8,128)(2,1)} %after.12), channel_id=1, source_target_pairs={{0,3},{1,2},{2,1},{3,0},{4,7},{5,6},{6,5},{7,4},{8,11},{9,10},{10,... | collective-permute-start | bytes 1327112 | tf_op jit(solution)/shard_map/ppermute | solution.py:705
  141.6 9.5 %collective-permute-start.31 = (bf16[152,576]{1,0:T(8,128)(2,1)}, bf16[152,576]{1,0:T(8,128)(2,1)}, u32[]{:S(2)}, u32[]{:S(2)}) collective-permute-start(bf16[152,576]{1,0:T(8,128)(2,1)} %get-tuple-element.130), channel_id=1, source_target_pairs={{0,8},{4,12},{8,0},{12,4},{1,9},{5,13},{9,1},{13,5},{2,10},{6,14},... | collective-permute-start | bytes 525320 | tf_op jit(solution)/shard_map/ppermute | solution.py:705
  143.0 9.7 %collective-permute-start.32 = (bf16[152,576]{1,0:T(8,128)(2,1)}, bf16[152,576]{1,0:T(8,128)(2,1)}, u32[]{:S(2)}, u32[]{:S(2)}) collective-permute-start(bf16[152,576]{1,0:T(8,128)(2,1)} %get-tuple-element.131), channel_id=1, source_target_pairs={{0,12},{4,8},{8,4},{12,0},{1,13},{5,9},{9,5},{13,1},{2,14},{6,10},... | collective-permute-start | bytes 525320 | tf_op jit(solution)/shard_map/ppermute | solution.py:705
  145.7 10.7 %collective-permute-start.26 = (bf16[2,576,128]{2,1,0:T(8,128)(2,1)}, bf16[2,576,128]{2,1,0:T(8,128)(2,1)}, u32[]{:S(2)}, u32[]{:S(2)}) collective-permute-start(bf16[2,576,128]{2,1,0:T(8,128)(2,1)} %finish_body.1.refs_4_), channel_id=1, source_target_pairs={{0,0},{1,16},{2,2},{3,18},{4,4},{5,20},{6,6},{7,22},{8,8},{9,24},{... | collective-permute-start | bytes 884744 | tf_op jit(solution)/shard_map/ppermute | solution.py:890
  149.5 23.2 %collective-permute-start.36 = (bf16[4,2,144,384]{3,2,1,0:T(8,128)(2,1)}, bf16[4,2,144,384]{3,2,1,0:T(8,128)(2,1)}, u32[]{:S(2)}, u32[]{:S(2)}) collective-permute-start(bf16[4,2,144,384]{3,2,1,0:T(8,128)(2,1)} %after.18.refs_1_), channel_id=1, source_target_pairs={{0,2},{2,0},{1,3},{3,1},{4,6},{6,4},{5,7},{7,5},{8,10},{10,8},{9,1... | collective-permute-start | bytes 2654216 | tf_op jit(solution)/shard_map/ppermute | solution.py:701
  154.7 11.4 %collective-permute-start.33 = (bf16[152,576]{1,0:T(8,128)(2,1)}, bf16[152,576]{1,0:T(8,128)(2,1)}, u32[]{:S(2)}, u32[]{:S(2)}) collective-permute-start(bf16[152,576]{1,0:T(8,128)(2,1)} %add_pieces_body.2.refs_0_), channel_id=1, source_target_pairs={{0,16},{16,0},{1,17},{17,1},{2,18},{18,2},{3,19},{19,3},{4,20},{20... | collective-permute-start | bytes 525320 | tf_op jit(solution)/shard_map/ppermute | solution.py:701
  168.1 34.1 %all-to-all-start.3 = ((bf16[4,144,576]{2,1,0:T(8,128)(2,1)}), bf16[4,144,576]{2,1,0:T(8,128)(2,1)}, u32[]{:S(2)}, u32[]{:S(2)}) async-start(bf16[4,144,576]{2,1,0:T(8,128)(2,1)} %get-tuple-element.133.refs_7_), calls=%async_computation.3 | async-start | bytes 1474560 | tf_op jit(solution)/shard_map/all_to_all | solution.py:713
  198.2 26.5 %collective-permute-start.37 = (bf16[1160,384]{1,0:T(8,128)(2,1)}, bf16[1160,384]{1,0:T(8,128)(2,1)}, u32[]{:S(2)}, u32[]{:S(2)}) collective-permute-start(bf16[1160,384]{1,0:T(8,128)(2,1)} %get-tuple-element.136.refs_6_.refs_1_), channel_id=1, source_target_pairs={{0,4},{4,0},{2,6},{6,2},{8,12},{12,8},{10,14},{14,10},{16,20},{20,... | collective-permute-start | bytes 2672648 | tf_op jit(solution)/shard_map/ppermute | solution.py:910
  202.2 22.6 %all-to-all-start.6 = ((bf16[4,144,576]{2,1,0:T(8,128)(2,1)}), bf16[4,144,576]{2,1,0:T(8,128)(2,1)}, u32[]{:S(2)}, u32[]{:S(2)}) async-start(bf16[4,144,576]{2,1,0:T(8,128)(2,1)} %all-to-all-done.3.refs_1_), calls=%async_computation.6 | async-start | bytes 1474560 | tf_op jit(solution)/shard_map/all_to_all | solution.py:713
  206.4 25.9 %collective-permute-start.38 = (bf16[1160,384]{1,0:T(8,128)(2,1)}, bf16[1160,384]{1,0:T(8,128)(2,1)}, u32[]{:S(2)}, u32[]{:S(2)}) collective-permute-start(bf16[1160,384]{1,0:T(8,128)(2,1)} %get-tuple-element.137), channel_id=1, source_target_pairs={{0,1},{1,0},{2,3},{3,2},{4,5},{5,4},{6,7},{7,6},{8,9},{9,8},{10,11... | collective-permute-start | bytes 2672648 | tf_op jit(solution)/shard_map/ppermute | solution.py:701
  206.9 25.4 %collective-permute-start.39 = (bf16[1160,384]{1,0:T(8,128)(2,1)}, bf16[1160,384]{1,0:T(8,128)(2,1)}, u32[]{:S(2)}, u32[]{:S(2)}) collective-permute-start(bf16[1160,384]{1,0:T(8,128)(2,1)} %get-tuple-element.137), channel_id=1, source_target_pairs={{0,5},{4,1},{2,7},{6,3},{8,13},{12,9},{10,15},{14,11},{16,21},{20,... | collective-permute-start | bytes 2672648 | tf_op jit(solution)/shard_map/ppermute | solution.py:911
  224.8 6.2 %copy-start.1 = (f32[2,144]{1,0:T(2,128)S(1)}, f32[2,144]{1,0:T(2,128)}, u32[]{:S(2)}) copy-start(f32[2,144]{1,0:T(2,128)} %param.24) | copy-start | bytes 3460
  224.8 16.0 %all-to-all-start.5 = ((bf16[4,152,576]{2,1,0:T(8,128)(2,1)}), bf16[4,152,576]{2,1,0:T(8,128)(2,1)}, u32[]{:S(2)}, u32[]{:S(2)}) async-start(bf16[4,152,576]{2,1,0:T(8,128)(2,1)} %after.19.refs_9_), calls=%async_computation.5 | async-start | bytes 1556480 | tf_op jit(solution)/shard_map/all_to_all | solution.py:713
  (4 other events, 21.0 us)

commit v2 on v1

--- a/solution.py
+++ b/solution.py
@@ -271,7 +271,7 @@
         out_ref[s] = out[s * tok : (s + 1) * tok, :]
     for j, send in enumerate((m0, m1, m2, m3)):
         send[0:tok, :] = out_ref[me ^ j]
-        send[tok:, :] = jnp.where((me ^ j) == 2, rows_ref[...], in_ref[...])
+        send[tok : 2 * tok, :] = jnp.where((me ^ j) == 2, rows_ref[...], in_ref[...])
     gu_grad = dot_rows(ffn_in, both).astype(bf16)
     down_grad = dot(cotangent, hidden).astype(bf16)
     height = whole_ref.shape[1]
@@ -453,7 +453,7 @@
     me, lo = me_ref[0], lo_ref[0]
     gain = jnp.zeros((8, D), f32)
     for j, (cols, piece) in enumerate(((r0, m0), (r1, m1), (r2, m2), (r3, m3))):
-        rows_ref[j * tok : (j + 1) * tok, :] = piece[tok:, :]
+        rows_ref[j * tok : (j + 1) * tok, :] = piece[tok : 2 * tok, :]
         cols_ref[j * tok : (j + 1) * tok, :] = cols[0:tok, :]
         gain = gain + cols[tok:, :].astype(f32)
     grad = dot_rows(rows_ref[...], cols_ref[...]).astype(bf16)
@@ -487,7 +487,7 @@
     return jnp.sum(jnp.sum(rows, axis=0, keepdims=True), axis=1, keepdims=True)
 
 
-def sweeps(z_ref, zb_ref, rest_ref, rest_b_ref, poly_ref, squares, block, steps):
+def sweeps(z_ref, zb_ref, rest_ref, rest_b_ref, poly_ref, squares, block, steps, unroll=1):
     n = z_ref.shape[0]
     row = lax.broadcasted_iota(jnp.int32, (block, n), 0)
     col = lax.broadcasted_iota(jnp.int32, (block, n), 1)
@@ -522,7 +522,7 @@
         zb_ref[...] = z_ref[...].astype(bf16)
         return total
 
-    return lax.fori_loop(0, steps, sweep, squares)
+    return lax.fori_loop(0, steps, sweep, squares, unroll=unroll)
 
 
 def normalize(z_ref, zb_ref):
@@ -634,7 +634,7 @@
 
     @pl.when(jnp.logical_not(narrow))
     def _():
-        sweeps(z_ref, zb_ref, rest_ref, rest_b_ref, poly_ref, squares, D, NS_STEPS)
+        sweeps(z_ref, zb_ref, rest_ref, rest_b_ref, poly_ref, squares, D, NS_STEPS, NS_STEPS)
 
     count = jnp.where(narrow, float(KV_WIDTH), float(D))
     norm = norm_rows(total, count * D, (8, D))
@@ -675,22 +675,39 @@
         norm_ref[number] = pick(number, slice(D, D + 8))
 
 
+def widen_body(results_ref, output_ref, dx_ref):
+    output_ref[...] = results_ref[0].astype(f32)
+    dx_ref[...] = results_ref[1].astype(f32)
+
+
+def attn_moment_body(
+    tokens, grad_ref, mq_ref, mkv_ref, mo_ref, rows_ref, mg_ref, gains_ref,
+    gq, gkv, go, nq, nkv, no, gg, ng, ug,
+):
+    grad = rows_ref[0:2, 0 : mg_ref.shape[1]]
+    moment = MOMENTUM * mg_ref[...] + grad
+    gg[...] = grad
+    ng[...] = moment
+    ug[...] = gains_ref[...].astype(f32) + -GAIN_RATE / math.sqrt(tokens) * moment
+    for number, old_ref, grad_out, new_out in ((0, mq_ref, gq, nq), (2, mo_ref, go, no)):
+        grad = grad_ref[number].astype(f32)
+        grad_out[...] = grad
+        new_out[...] = MOMENTUM * old_ref[...] + grad
+    for i, number in enumerate((1, 3)):
+        grad = grad_ref[number, :, 0:KV_WIDTH].astype(f32)
+        gkv[i] = grad
+        nkv[i] = MOMENTUM * mkv_ref[i] + grad
+
+
 def attn_new_body(
-    back_ref, grad_ref, feed_norm_ref, wq_ref, wkv_ref, wo_ref, mq_ref, mkv_ref, mo_ref,
-    gq, gkv, go, nq, nkv, no, uq, ukv, uo, norm_ref,
+    back_ref, feed_norm_ref, wq_ref, wkv_ref, wo_ref, uq, ukv, uo, norm_ref
 ):
     rate = -RATE * SHAPE_SCALE * math.sqrt(D)
     rows = wq_ref.shape[0]
-
-    def update(number, width, weight, old):
-        ortho = back_ref[number, 0:rows, 0:width].astype(f32)
-        grad = grad_ref[number, :, 0:width].astype(f32)
-        return grad, MOMENTUM * old + grad, weight.astype(f32) + rate * ortho
-
-    gq[...], nq[...], uq[...] = update(0, D, wq_ref[...], mq_ref[...])
-    go[...], no[...], uo[...] = update(2, D, wo_ref[...], mo_ref[...])
+    uq[...] = wq_ref[...].astype(f32) + rate * back_ref[0, 0:rows, :].astype(f32)
+    uo[...] = wo_ref[...].astype(f32) + rate * back_ref[2, 0:rows, :].astype(f32)
     for i, number in enumerate((1, 3)):
-        gkv[i], nkv[i], ukv[i] = update(number, KV_WIDTH, wkv_ref[i], mkv_ref[i])
+        ukv[i] = wkv_ref[i].astype(f32) + rate * back_ref[number, 0:rows, 0:KV_WIDTH].astype(f32)
     for i, number in enumerate((0, 1, 3, 2)):
         norm_ref[i] = jnp.sum(back_ref[number, rows : rows + 2, 0:1].astype(f32))
     for i in range(3):
@@ -818,7 +835,7 @@
     olds = pass_shard((old_same, old_other, old_same, old_other))
     misc_0, misc_1, misc_2, misc_3, dffn_part, *feed_grads = call(
         feed_body,
-        [((2 * tok, D), bf16)] * n_shard + [((n_shard, tok + 8, D), bf16)]
+        [((2 * tok + 48, D), bf16)] * n_shard + [((n_shard, tok + 8, D), bf16)]
         + [((height, 3 * part), bf16)] * n_lo,
         (me, lo, ffn_all) + cots + wide_pieces + (w_down.T, attn_in, attn_rows),
         scratch=(
@@ -888,11 +905,12 @@
     )
     attn_other = trade(attn_sum, "hi")
     results = lax.ppermute(finished, ALL, moves)
+    output, input_grad = call(widen_body, [((D, tok), f32)] * 2, (results,), hold=(attn_sum,))
     attn_slots, gain_rows = call(
         add_second_body,
         [((n_lo, height, D), bf16), ((8, D), f32)],
         (attn_sum, attn_other),
-        hold=(results, olds[3]),
+        hold=(output, olds[3]),
     )
     feed_same, feed_other = call(
         feed_ns_body,
@@ -934,19 +952,20 @@
     three = [((rows, D), f32), ((2, rows, KV_WIDTH), f32), ((rows, D), f32)]
     (
         grad_query, grad_kv, grad_out, moment_query, moment_kv, moment_out,
-        new_query, new_kv, new_out, momentum_norms,
+        grad_gains, moment_gains, new_gains,
     ) = call(
+        functools.partial(attn_moment_body, tok * n_ctx * n_shard),
+        three * 2 + [((2, rows), f32)] * 3,
+        (attn_rows_back, mom_query, mom_kv, mom_out, gain_rows, mom_gains, norm_gains),
+        hold=(attn_ortho,),
+    )
+    new_query, new_kv, new_out, momentum_norms = call(
         attn_new_body,
-        three * 3 + [((7,), f32)],
-        (attn_back, attn_rows_back, feed_norm, w_query, w_kv, w_out, mom_query, mom_kv, mom_out),
-    )
-    grad_gains = gain_rows[:2, :rows]
-    moment_gains = MOMENTUM * mom_gains + grad_gains
-    all_tokens = tok * n_ctx * n_shard
-    new_gains = norm_gains.astype(f32) + -GAIN_RATE / math.sqrt(all_tokens) * moment_gains
-    results = jnp.transpose(results, (0, 2, 1)).astype(f32)
+        three + [((7,), f32)],
+        (attn_back, feed_norm, w_query, w_kv, w_out),
+    )
     return (
-        results[0][None], results[1][None],
+        output.T[None], input_grad.T[None],
         grad_gains, grad_query, grad_kv, grad_out, grad_gate_up, grad_down.T,
         moment_gains, moment_query, moment_kv, moment_out, moment_gate_up, moment_down.T,
         momentum_norms,

time: 246 us -> 242 us (0.984)
  waiting for transfers between devices: 45.8 us -> 41.4 us
  Pallas kernels: 97.5 us -> 100 us
    pallas_call x18 -> x20, Pallas kernels: 97.5 us -> 100 us  [call(): pl.pallas_call(run, name=getattr(body, 'func', body).__name__, out_shape=...]
  transfers between devices with their start and end apart: 47 -> 47, of which waited for: 13 -> 11; matrix products, arithmetic and copies ran while one was open for 3% -> 2% of each run, Pallas kernels for 35% -> 38%
where the time goes in v2:
time: 242 us; the launch traced here: 241 us
  Pallas kernels  100 us (41%)
  starting transfers between devices  82 us (34%)
  waiting for transfers between devices  41.4 us (17%)
  blocking collectives  11.3 us (5%)
    pallas_call x20, Pallas kernels, call(): pl.pallas_call(run, name=getattr(body, 'func', body).__name__, out_shape=...  100 us
    all_to_all x7, starting transfers between devices, deal(): return lax.all_to_all(x, axis, 0, 0, tiled=True)  29.7 us
    ppermute x24, waiting for transfers between devices, pass_on(): return lax.ppermute(x, axis, [(i, i ^ j) for i in range(size)])  25.8 us
    ppermute x24, starting transfers between devices, pass_on(): return lax.ppermute(x, axis, [(i, i ^ j) for i in range(size)])  20.4 us
    ppermute x11, starting transfers between devices, trade(): return lax.ppermute(x, axis, TRADE)  16 us
    all_gather x1, blocking collectives, on_device(): lax.all_gather(after(ffn_in, wide_pieces[3]), SHARD, axis=0, tiled=True)  11.3 us
    ppermute x11, waiting for transfers between devices, trade(): return lax.ppermute(x, axis, TRADE)  8.07 us
    all_to_all x7, waiting for transfers between devices, deal(): return lax.all_to_all(x, axis, 0, 0, tiled=True)  7.54 us
  transfers between devices with their start and end apart: 47, of which 11 were waited for; matrix products, arithmetic and copies ran while one was open for 2% of the time, Pallas kernels for 38%

profile of v2, /device:TPU:0, one launch (start us, length us, event | category | flops | bytes accessed | tf_op | source)
XLA Modules:
  0.0 240.5 jit_solution(6254974935379190064)
XLA Ops:
  0.7 2.0 pack_body.1
  2.7 3.0 %collective-permute-start.2 = (bf16[152,960]{1,0:T(8,128)(2,1)}, bf16[152,960]{1,0:T(8,128)(2,1)}, u32[]{:S(2)}, u32[]{:S(2)}) collective-permute-start(bf16[152,960]{1,0:T(8,128)(2,1)} %get-tuple-element.94.refs_2_), channel_id=1, source_target_pairs={{0,2},{2,0},{1,3},{3,1},{4,6},{6,4},{5,7},{7,5},{8,10},{10,8},{9,1... | collective-permute-start | bytes 875528 | tf_op jit(solution)/shard_map/ppermute | solution.py:718
  5.6 2.9 %collective-permute-start = (bf16[136,576]{1,0:T(8,128)(2,1)}, bf16[136,576]{1,0:T(8,128)(2,1)}, u32[]{:S(2)}, u32[]{:S(2)}) collective-permute-start(bf16[136,576]{1,0:T(8,128)(2,1)} %get-tuple-element.93), channel_id=1, source_target_pairs={{0,0},{1,16},{2,2},{3,18},{4,4},{5,20},{6,6},{7,22},{8,8},{9,24},{... | collective-permute-start | bytes 470024 | tf_op jit(solution)/shard_map/ppermute | solution.py:770
  11.3 2.1 pack_wide_body.1
  15.3 2.1 collective-permute-start.3
  19.3 2.9 %project_body.1 = (bf16[128,576]{1,0:T(8,128)(2,1)}, bf16[128,576]{1,0:T(8,128)(2,1)}, bf16[4,136,384]{2,1,0:T(8,128)(2,1)}, bf16[576,960]{1,0:T(8,128)(2,1)}, f32[8,576]{1,0:T(8,128)}) custom-call(s32[1]{0:T(128)} %bitcast.refs_0_, bf16[136,576]{1,0:T(8,128)(2,1)} %collective-permute-done.refs_1_.refs_2_, bf16[152,960]{1,0:T(8,128)(2,1)} %get-tuple-element.94.refs_2_, ...), custom_call_target="tpu_custom_call" | custom-call | bytes 1024 | tf_op jit(solution)/shard_map/project_body/pallas_call | solution.py:60
  22.2 4.1 %all-to-all-start = ((bf16[4,136,384]{2,1,0:T(8,128)(2,1)}), bf16[4,136,384]{2,1,0:T(8,128)(2,1)}, u32[]{:S(2)}, u32[]{:S(2)}) async-start(bf16[4,136,384]{2,1,0:T(8,128)(2,1)} %get-tuple-element.97), calls=%async_computation | async-start | bytes 835584 | tf_op jit(solution)/shard_map/all_to_all | solution.py:730
  28.3 2.8 %collective-permute-start.7 = (bf16[576,128]{1,0:T(8,128)(2,1)}, bf16[576,128]{1,0:T(8,128)(2,1)}, u32[]{:S(2)}, u32[]{:S(2)}) collective-permute-start(bf16[576,128]{1,0:T(8,128)(2,1)} %bitcast.37), channel_id=1, source_target_pairs={{0,0},{1,16},{2,2},{3,18},{4,4},{5,20},{6,6},{7,22},{8,8},{9,24},{... | collective-permute-start | bytes 442376 | tf_op jit(solution)/shard_map/ppermute | solution.py:785
  31.7 3.4 %old_body.1 = (bf16[144,576]{1,0:T(8,128)(2,1)}, bf16[144,576]{1,0:T(8,128)(2,1)}, bf16[144,576]{1,0:T(8,128)(2,1)}, bf16[144,576]{1,0:T(8,128)(2,1)}, bf16[576,...) custom-call(s32[1]{0:T(128)} %bitcast.refs_0_, s32[5]{0:T(128)} %stack.20.refs_1_.refs_0_, f32[144,576]{1,0:T(8,128)} %refs_1_.3, ...), custom_call_target="tpu_custom_call" | custom-call | bytes 1024 | tf_op jit(solution)/shard_map/old_body/pallas_call | solution.py:60
  35.2 1.9 collective-permute-start.10
  39.2 5.1 %attend_body.1 = (bf16[576,576]{1,0:T(8,128)(2,1)}, f32[128,576]{1,0:T(8,128)}, bf16[128,576]{1,0:T(8,128)(2,1)}, bf16[128,576]{1,0:T(8,128)(2,1)}, f32[128,576]{1,0:T(8,128)}, /*index=5*/f32[3,384]{1,0:T(4,128)}) custom-call(s32[1]{0:T(128)} %bitcast.refs_0_, bf16[136,576]{1,0:T(8,128)(2,1)} %collective-permute-done.refs_1_.refs_2_, ...), custom_call_target="tpu_custom_call" | custom-call | bytes 1024 | tf_op jit(solution)/shard_map/attend_body/pallas_call | solution.py:60
  44.9 11.3 %all_gather.3.refs_2_.refs_1_ = bf16[512,576]{1,0:T(8,128)(2,1)} all-gather(bf16[128,576]{1,0:T(8,128)(2,1)} %after.11), channel_id=1, replica_groups=mesh['hi'=2,'lh'=2,'lx'=2,'y'=2,'core'=2] {'y','core'}, dimensions={0}, use_global_device_ids=true | all-gather | bytes 737280 | tf_op jit(solution)/shard_map/all_gather | solution.py:832
  58.1 6.8 %feed_body.1 = (bf16[304,576]{1,0:T(8,128)(2,1)}, bf16[304,576]{1,0:T(8,128)(2,1)}, bf16[304,576]{1,0:T(8,128)(2,1)}, bf16[304,576]{1,0:T(8,128)(2,1)}, bf16[4,1...) custom-call(s32[1]{0:T(128)} %bitcast.refs_0_, ...), custom_call_target="tpu_custom_call" | custom-call | bytes 1024 | tf_op jit(solution)/shard_map/feed_body/pallas_call | solution.py:60
  64.9 4.3 %all-to-all-start.1 = ((bf16[4,136,576]{2,1,0:T(8,128)(2,1)}), bf16[4,136,576]{2,1,0:T(8,128)(2,1)}, u32[]{:S(2)}, u32[]{:S(2)}) async-start(bf16[4,136,576]{2,1,0:T(8,128)(2,1)} %get-tuple-element.107), calls=%async_computation.1 | async-start | bytes 1392640 | tf_op jit(solution)/shard_map/all_to_all | solution.py:730
  71.2 2.2 collective-permute-start.15
  75.0 5.3 %all-to-all-done.1.refs_1_ = bf16[4,136,576]{2,1,0:T(8,128)(2,1)} async-done(((bf16[4,136,576]{2,1,0:T(8,128)(2,1)}), bf16[4,136,576]{2,1,0:T(8,128)(2,1)}, u32[]{:S(2)}, u32[]{:S(2)}) %all-to-all-start.1) | async-done | bytes 626720 | tf_op jit(solution)/shard_map/all_to_all | solution.py:730
  80.3 6.9 %back_body.1 = (f32[128,576]{1,0:T(8,128)}, bf16[128,576]{1,0:T(8,128)(2,1)}, bf16[128,576]{1,0:T(8,128)(2,1)}, bf16[8,128,384]{2,1,0:T(8,128)(2,1)}, f32[1,576]{1,0:T(1,128)}) custom-call(s32[5]{0:T(128)} %stack.20.refs_1_.refs_0_, bf16[4,136,576]{2,1,0:T(8,128)(2,1)} %all-to-all-done.1.refs_1_, bf16[136,576]{1,0:T(8,128)(2,1)} %collective-permute-done.refs_1_.refs_2_, ...), custom_call_target="tpu_custom_call" | custom-call | bytes 1024 | tf_op jit(solution)/shard_map/back_body/pallas_call | solution.py:60
  87.2 2.9 %collective-permute-done.17.refs_3_ = bf16[144,1152]{1,0:T(8,128)(2,1)} collective-permute-done((bf16[144,1152]{1,0:T(8,128)(2,1)}, bf16[144,1152]{1,0:T(8,128)(2,1)}, u32[]{:S(2)}, u32[]{:S(2)}) %collective-permute-start.17) | collective-permute-done | bytes 331808 | tf_op jit(solution)/shard_map/ppermute | solution.py:722
  90.2 4.2 %all-to-all-start.2 = ((bf16[8,128,384]{2,1,0:T(8,128)(2,1)}), bf16[8,128,384]{2,1,0:T(8,128)(2,1)}, u32[]{:S(2)}, u32[]{:S(2)}) async-start(bf16[8,128,384]{2,1,0:T(8,128)(2,1)} %after.17), calls=%async_computation.2 | async-start | bytes 1572864 | tf_op jit(solution)/shard_map/all_to_all | solution.py:730
  96.3 2.2 add_pieces_body.3.refs_0_
  98.5 2.3 collective-permute-start.35
  100.8 6.1 %collective-permute-done.24.refs_12_.refs_4_.refs_8_ = bf16[304,576]{1,0:T(8,128)(2,1)} collective-permute-done((bf16[304,576]{1,0:T(8,128)(2,1)}, bf16[304,576]{1,0:T(8,128)(2,1)}, u32[]{:S(2)}, u32[]{:S(2)}) %collective-permute-start.24) | collective-permute-done | bytes 350240 | tf_op jit(solution)/shard_map/ppermute | solution.py:722
  107.0 6.8 %collective-permute-done.25.refs_13_.refs_5_.refs_9_ = bf16[304,576]{1,0:T(8,128)(2,1)} collective-permute-done((bf16[304,576]{1,0:T(8,128)(2,1)}, bf16[304,576]{1,0:T(8,128)(2,1)}, u32[]{:S(2)}, u32[]{:S(2)}) %collective-permute-start.25) | collective-permute-done | bytes 350240 | tf_op jit(solution)/shard_map/ppermute | solution.py:722
  113.8 3.5 %input_body.1 = (f32[128,576]{1,0:T(8,128)}, bf16[136,576]{1,0:T(8,128)(2,1)}, bf16[136,576]{1,0:T(8,128)(2,1)}, bf16[136,576]{1,0:T(8,128)(2,1)}, bf16[136,576]{1,0:T(8,128)(2,1)}) custom-call(s32[1]{0:T(128)} %bitcast.refs_0_, bf16[8,128,384]{2,1,0:T(8,128)(2,1)} %all-to-all-done.2.refs_1_, bf16[136,576]{1,0:T(8,128)(2,1)} %collective-permute-done.refs_1_.refs_2_, ...), custom_call_target="tpu_custom_call" | custom-call | bytes 1024 | tf_op jit(solution)/shard_map/input_body/pallas_call | solution.py:60
  117.3 2.1 add_slots_body.1
  119.4 4.4 %all-to-all-start.5 = ((bf16[8,144,384]{2,1,0:T(8,128)(2,1)}), bf16[8,144,384]{2,1,0:T(8,128)(2,1)}, u32[]{:S(2)}, u32[]{:S(2)}) async-start(bf16[8,144,384]{2,1,0:T(8,128)(2,1)} %bitcast.28), calls=%async_computation.5 | async-start | bytes 1769472 | tf_op jit(solution)/shard_map/all_to_all | solution.py:730
  126.1 5.9 %collective-permute-done.28.refs_4_ = bf16[136,576]{1,0:T(8,128)(2,1)} collective-permute-done((bf16[136,576]{1,0:T(8,128)(2,1)S(1)}, bf16[136,576]{1,0:T(8,128)(2,1)}, u32[]{:S(2)}, u32[]{:S(2)}) %collective-permute-start.28) | collective-permute-done | bytes 156704 | tf_op jit(solution)/shard_map/ppermute | solution.py:722
  132.0 2.0 collective-permute-done.29.refs_5_
  134.0 3.2 %attn_grad_body.1 = (bf16[152,576]{1,0:T(8,128)(2,1)}, bf16[152,576]{1,0:T(8,128)(2,1)}, bf16[152,576]{1,0:T(8,128)(2,1)}, bf16[152,576]{1,0:T(8,128)(2,1)}) custom-call(s32[1]{0:T(128)} %bitcast.refs_0_, s32[1]{0:T(128)} %bitcast.11.refs_1_, bf16[136,576]{1,0:T(8,128)(2,1)} %get-tuple-element.129.refs_2_, bf16[136,576]{1,0:T(8,128)(2,1)} %collective-permute-done.27.refs_3_, ...), custom_call_target="tpu_custom_call" | custom-call | bytes 1024 | tf_op jit(solution)/shard_map/attn_grad_body/pallas_call | solution.py:60
  137.2 1.8 collective-permute-start.30
  141.6 2.5 %finish_body.1.refs_4_ = bf16[2,576,128]{2,1,0:T(8,128)(2,1)} custom-call(f32[128,576]{1,0:T(8,128)} %get-tuple-element.102.refs_4_.refs_0_, f32[128,576]{1,0:T(8,128)} %get-tuple-element.127.refs_1_.refs_2_, bf16[304,576]{1,0:T(8,128)(2,1)} %get-tuple-element.128.refs_2_.refs_6_, bf16[304,576]{1,0:T(8,128)(2,1)} %collective-permute-done.23.refs_11_.refs_3_.refs_7_, ...), custom_call_target="tpu_custom_call" | custom-call | bytes 1024 | tf_op jit(solution)/shard_map/finish_body/pallas_call | solution.py:60
  144.1 3.8 %collective-permute-start.26 = (bf16[2,576,128]{2,1,0:T(8,128)(2,1)}, bf16[2,576,128]{2,1,0:T(8,128)(2,1)}, u32[]{:S(2)}, u32[]{:S(2)}) collective-permute-start(bf16[2,576,128]{2,1,0:T(8,128)(2,1)} %finish_body.1.refs_4_), channel_id=1, source_target_pairs={{0,0},{1,16},{2,2},{3,18},{4,4},{5,20},{6,6},{7,22},{8,8},{9,24},{... | collective-permute-start | bytes 884744 | tf_op jit(solution)/shard_map/ppermute | solution.py:907
  150.8 2.0 add_pieces_body.2.refs_1_.refs_0_
  152.8 2.4 collective-permute-start.33
  155.2 1.8 widen_body.1
  157.0 8.0 %collective-permute-done.33.refs_1_ = bf16[152,576]{1,0:T(8,128)(2,1)} collective-permute-done((bf16[152,576]{1,0:T(8,128)(2,1)}, bf16[152,576]{1,0:T(8,128)(2,1)}, u32[]{:S(2)}, u32[]{:S(2)}) %collective-permute-start.33) | collective-permute-done | bytes 175136 | tf_op jit(solution)/shard_map/ppermute | solution.py:718
  164.9 1.9 add_second_body.1
  166.9 4.2 %all-to-all-start.3 = ((bf16[4,144,576]{2,1,0:T(8,128)(2,1)}), bf16[4,144,576]{2,1,0:T(8,128)(2,1)}, u32[]{:S(2)}, u32[]{:S(2)}) async-start(bf16[4,144,576]{2,1,0:T(8,128)(2,1)} %get-tuple-element.139.refs_7_), calls=%async_computation.3 | async-start | bytes 1474560 | tf_op jit(solution)/shard_map/all_to_all | solution.py:730
  171.1 25.4 %feed_ns_body.1 = (bf16[1160,384]{1,0:T(8,128)(2,1)}, bf16[1160,384]{1,0:T(8,128)(2,1)}) custom-call(s32[5]{0:T(128)} %stack.20.refs_1_.refs_0_, bf16[4,2,144,384]{3,2,1,0:T(8,128)(2,1)} %after.18.refs_1_, bf16[4,2,144,384]{3,2,1,0:T(8,128)(2,1)} %collective-permute-done.36.refs_2_, bf16[576,384]{1,0:T(8,128)(2,1)} %after.13.refs_3_, ...), custom_call_target="tpu_custom_call" | custom-call | bytes 1024 | tf_op jit(solution)/shard_map/feed_ns_body/pallas_call | solution.py:60
  196.5 3.9 %collective-permute-start.37 = (bf16[1160,384]{1,0:T(8,128)(2,1)}, bf16[1160,384]{1,0:T(8,128)(2,1)}, u32[]{:S(2)}, u32[]{:S(2)}) collective-permute-start(bf16[1160,384]{1,0:T(8,128)(2,1)} %get-tuple-element.143.refs_6_.refs_1_), channel_id=1, source_target_pairs={{0,4},{4,0},{2,6},{6,2},{8,12},{12,8},{10,14},{14,10},{16,20},{20,... | collective-permute-start | bytes 2672648 | tf_op jit(solution)/shard_map/ppermute | solution.py:928
  200.3 4.2 %all-to-all-start.4 = ((bf16[4,144,576]{2,1,0:T(8,128)(2,1)}), bf16[4,144,576]{2,1,0:T(8,128)(2,1)}, u32[]{:S(2)}, u32[]{:S(2)}) async-start(bf16[4,144,576]{2,1,0:T(8,128)(2,1)} %all-to-all-done.3.refs_1_), calls=%async_computation.4 | async-start | bytes 1474560 | tf_op jit(solution)/shard_map/all_to_all | solution.py:730
  205.0 2.6 %collective-permute-start.39 = (bf16[1160,384]{1,0:T(8,128)(2,1)}, bf16[1160,384]{1,0:T(8,128)(2,1)}, u32[]{:S(2)}, u32[]{:S(2)}) collective-permute-start(bf16[1160,384]{1,0:T(8,128)(2,1)} %get-tuple-element.148), channel_id=1, source_target_pairs={{0,5},{4,1},{2,7},{6,3},{8,13},{12,9},{10,15},{14,11},{16,21},{20,... | collective-permute-start | bytes 2672648 | tf_op jit(solution)/shard_map/ppermute | solution.py:929
  207.6 14.5 %attn_ns_body.1.refs_0_ = bf16[4,152,576]{2,1,0:T(8,128)(2,1)} custom-call(s32[1]{0:T(128)} %bitcast.refs_0_, bf16[4,144,576]{2,1,0:T(8,128)(2,1)} %all-to-all-done.3.refs_1_, bf16[144,576]{1,0:T(8,128)(2,1)} %get-tuple-element.141.refs_2_, bf16[144,576]{1,0:T(8,128)(2,1)} %collective-permute-done.20.refs_6_.refs_3_, ...), custom_call_target="tpu_custom_call" | custom-call | bytes 1024 | tf_op jit(solution)/shard_map/attn_ns_body/pallas_call | solution.py:60
  222.2 4.2 %all-to-all-start.6 = ((bf16[4,152,576]{2,1,0:T(8,128)(2,1)}), bf16[4,152,576]{2,1,0:T(8,128)(2,1)}, u32[]{:S(2)}, u32[]{:S(2)}) async-start(bf16[4,152,576]{2,1,0:T(8,128)(2,1)} %after.19.refs_7_.refs_9_), calls=%async_computation.6 | async-start | bytes 1556480 | tf_op jit(solution)/shard_map/all_to_all | solution.py:730
  226.4 6.5 %feed_new_body.1 = (f32[2,144,1536]{2,1,0:T(8,128)}, f32[576,384]{1,0:T(8,128)}, f32[2,144,1536]{2,1,0:T(8,128)}, f32[576,384]{1,0:T(8,128)}, f32[2,144,1536]{2,...) custom-call(s32[5]{0:T(128)} %stack.20.refs_1_.refs_0_, bf16[1160,384]{1,0:T(8,128)(2,1)} %get-tuple-element.143.refs_6_.refs_1_, ...), custom_call_target="tpu_custom_call" | custom-call | bytes 1024 | tf_op jit(solution)/shard_map/feed_new_body/pallas_call | solution.py:60
  232.9 2.8 %attn_moment_body.1 = (f32[144,576]{1,0:T(8,128)}, f32[2,144,192]{2,1,0:T(8,128)}, f32[144,576]{1,0:T(8,128)}, f32[144,576]{1,0:T(8,128)}, f32[2,144,192]{2,1,0:...) custom-call(bf16[4,144,576]{2,1,0:T(8,128)(2,1)} %all-to-all-done.4.refs_0_, ...), custom_call_target="tpu_custom_call" | custom-call | bytes 1024 | tf_op jit(solution)/shard_map/attn_moment_body/pallas_call | solution.py:60
  235.8 2.2 all-to-all-done.6.refs_0_
  238.0 2.4 attn_new_body.1
  (88 shorter events, 26.8 us)
Async XLA Ops:
  2.7 12.7 %collective-permute-start.2 = (bf16[152,960]{1,0:T(8,128)(2,1)}, bf16[152,960]{1,0:T(8,128)(2,1)}, u32[]{:S(2)}, u32[]{:S(2)}) collective-permute-start(bf16[152,960]{1,0:T(8,128)(2,1)} %get-tuple-element.94.refs_2_), channel_id=1, source_target_pairs={{0,2},{2,0},{1,3},{3,1},{4,6},{6,4},{5,7},{7,5},{8,10},{10,8},{9,1... | collective-permute-start | bytes 875528 | tf_op jit(solution)/shard_map/ppermute | solution.py:718
  5.6 7.9 %collective-permute-start = (bf16[136,576]{1,0:T(8,128)(2,1)}, bf16[136,576]{1,0:T(8,128)(2,1)}, u32[]{:S(2)}, u32[]{:S(2)}) collective-permute-start(bf16[136,576]{1,0:T(8,128)(2,1)} %get-tuple-element.93), channel_id=1, source_target_pairs={{0,0},{1,16},{2,2},{3,18},{4,4},{5,20},{6,6},{7,22},{8,8},{9,24},{... | collective-permute-start | bytes 470024 | tf_op jit(solution)/shard_map/ppermute | solution.py:770
  8.5 10.6 %collective-permute-start.1 = (bf16[152,960]{1,0:T(8,128)(2,1)}, bf16[152,960]{1,0:T(8,128)(2,1)}, u32[]{:S(2)}, u32[]{:S(2)}) collective-permute-start(bf16[152,960]{1,0:T(8,128)(2,1)} %get-tuple-element.94.refs_2_), channel_id=1, source_target_pairs={{0,1},{1,0},{2,3},{3,2},{4,5},{5,4},{6,7},{7,6},{8,9},{9,8},{10,11... | collective-permute-start | bytes 875528 | tf_op jit(solution)/shard_map/ppermute | solution.py:718
  10.3 7.1 %collective-permute-start.5 = (bf16[144,576]{1,0:T(8,128)(2,1)}, bf16[144,576]{1,0:T(8,128)(2,1)}, u32[]{:S(2)}, u32[]{:S(2)}) collective-permute-start(bf16[144,576]{1,0:T(8,128)(2,1)} %refs_4_.5), channel_id=1, source_target_pairs={{0,2},{2,0},{1,3},{3,1},{4,6},{6,4},{5,7},{7,5},{8,10},{10,8},{9,1... | collective-permute-start | bytes 497672 | tf_op jit(solution)/shard_map/ppermute | solution.py:718
  10.8 8.4 %collective-permute-start.4 = (bf16[144,576]{1,0:T(8,128)(2,1)}, bf16[144,576]{1,0:T(8,128)(2,1)}, u32[]{:S(2)}, u32[]{:S(2)}) collective-permute-start(bf16[144,576]{1,0:T(8,128)(2,1)} %refs_4_.5), channel_id=1, source_target_pairs={{0,1},{1,0},{2,3},{3,2},{4,5},{5,4},{6,7},{7,6},{8,9},{9,8},{10,11... | collective-permute-start | bytes 497672 | tf_op jit(solution)/shard_map/ppermute | solution.py:718
  15.3 3.9 %collective-permute-start.3 = (bf16[152,960]{1,0:T(8,128)(2,1)}, bf16[152,960]{1,0:T(8,128)(2,1)}, u32[]{:S(2)}, u32[]{:S(2)}) collective-permute-start(bf16[152,960]{1,0:T(8,128)(2,1)} %collective-permute-done.2.refs_4_), channel_id=1, source_target_pairs={{0,1},{1,0},{2,3},{3,2},{4,5},{5,4},{6,7},{7,6},{8,9},{9,8},{10,11... | collective-permute-start | bytes 875528 | tf_op jit(solution)/shard_map/ppermute | solution.py:718
  17.4 1.8 collective-permute-start.6
  22.2 13.0 %all-to-all-start = ((bf16[4,136,384]{2,1,0:T(8,128)(2,1)}), bf16[4,136,384]{2,1,0:T(8,128)(2,1)}, u32[]{:S(2)}, u32[]{:S(2)}) async-start(bf16[4,136,384]{2,1,0:T(8,128)(2,1)} %get-tuple-element.97), calls=%async_computation | async-start | bytes 835584 | tf_op jit(solution)/shard_map/all_to_all | solution.py:730
  26.3 8.9 %collective-permute-start.8 = (bf16[144,768]{1,0:T(8,128)(2,1)}, bf16[144,768]{1,0:T(8,128)(2,1)}, u32[]{:S(2)}, u32[]{:S(2)}) collective-permute-start(bf16[144,768]{1,0:T(8,128)(2,1)} %get-tuple-element.99), channel_id=1, source_target_pairs={{0,1},{1,0},{2,3},{3,2},{4,5},{5,4},{6,7},{7,6},{8,9},{9,8},{10,11... | collective-permute-start | bytes 663560 | tf_op jit(solution)/shard_map/ppermute | solution.py:722
  26.8 8.4 %collective-permute-start.9 = (bf16[144,768]{1,0:T(8,128)(2,1)}, bf16[144,768]{1,0:T(8,128)(2,1)}, u32[]{:S(2)}, u32[]{:S(2)}) collective-permute-start(bf16[144,768]{1,0:T(8,128)(2,1)} %get-tuple-element.100), channel_id=1, source_target_pairs={{0,2},{1,3},{2,0},{3,1},{4,6},{5,7},{6,4},{7,5},{8,10},{9,11},{10,... | collective-permute-start | bytes 663560 | tf_op jit(solution)/shard_map/ppermute | solution.py:722
  28.3 6.9 %collective-permute-start.7 = (bf16[576,128]{1,0:T(8,128)(2,1)}, bf16[576,128]{1,0:T(8,128)(2,1)}, u32[]{:S(2)}, u32[]{:S(2)}) collective-permute-start(bf16[576,128]{1,0:T(8,128)(2,1)} %bitcast.37), channel_id=1, source_target_pairs={{0,0},{1,16},{2,2},{3,18},{4,4},{5,20},{6,6},{7,22},{8,8},{9,24},{... | collective-permute-start | bytes 442376 | tf_op jit(solution)/shard_map/ppermute | solution.py:785
  35.2 4.0 %collective-permute-start.10 = (bf16[4,136,384]{2,1,0:T(8,128)(2,1)}, bf16[4,136,384]{2,1,0:T(8,128)(2,1)}, u32[]{:S(2)}, u32[]{:S(2)}) collective-permute-start(bf16[4,136,384]{2,1,0:T(8,128)(2,1)} %after.10.refs_3_.refs_9_), channel_id=1, source_target_pairs={{0,1},{1,0},{2,3},{3,2},{4,5},{5,4},{6,7},{7,6},{8,9},{9,8},{10,11... | collective-permute-start | bytes 1253384 | tf_op jit(solution)/shard_map/ppermute | solution.py:718
  37.1 7.8 %collective-permute-start.11 = (bf16[144,768]{1,0:T(8,128)(2,1)}, bf16[144,768]{1,0:T(8,128)(2,1)}, u32[]{:S(2)}, u32[]{:S(2)}) collective-permute-start(bf16[144,768]{1,0:T(8,128)(2,1)} %get-tuple-element.104), channel_id=1, source_target_pairs={{0,3},{1,2},{2,1},{3,0},{4,7},{5,6},{6,5},{7,4},{8,11},{9,10},{10,... | collective-permute-start | bytes 663560 | tf_op jit(solution)/shard_map/ppermute | solution.py:722
  37.3 19.7 %collective-permute-start.12 = (bf16[576,128]{1,0:T(8,128)(2,1)}, bf16[576,128]{1,0:T(8,128)(2,1)}, u32[]{:S(2)}, u32[]{:S(2)}) collective-permute-start(bf16[576,128]{1,0:T(8,128)(2,1)} %collective-permute-done.7.refs_2_.refs_3_), channel_id=1, source_target_pairs={{0,1},{1,0},{2,3},{3,2},{4,5},{5,4},{6,7},{7,6},{8,9},{9,8},{10,11... | collective-permute-start | bytes 442376 | tf_op jit(solution)/shard_map/ppermute | solution.py:722
  37.7 20.3 %collective-permute-start.13 = (bf16[576,128]{1,0:T(8,128)(2,1)}, bf16[576,128]{1,0:T(8,128)(2,1)}, u32[]{:S(2)}, u32[]{:S(2)}) collective-permute-start(bf16[576,128]{1,0:T(8,128)(2,1)} %collective-permute-done.7.refs_2_.refs_3_), channel_id=1, source_target_pairs={{0,2},{1,3},{2,0},{3,1},{4,6},{5,7},{6,4},{7,5},{8,10},{9,11},{10,... | collective-permute-start | bytes 442376 | tf_op jit(solution)/shard_map/ppermute | solution.py:722
  39.2 18.8 %collective-permute-start.14 = (bf16[576,128]{1,0:T(8,128)(2,1)}, bf16[576,128]{1,0:T(8,128)(2,1)}, u32[]{:S(2)}, u32[]{:S(2)}) collective-permute-start(bf16[576,128]{1,0:T(8,128)(2,1)} %collective-permute-done.7.refs_2_.refs_3_), channel_id=1, source_target_pairs={{0,3},{1,2},{2,1},{3,0},{4,7},{5,6},{6,5},{7,4},{8,11},{9,10},{10,... | collective-permute-start | bytes 442376 | tf_op jit(solution)/shard_map/ppermute | solution.py:722
  56.2 15.0 %collective-permute-start.20 = (bf16[144,576]{1,0:T(8,128)(2,1)}, bf16[144,576]{1,0:T(8,128)(2,1)}, u32[]{:S(2)}, u32[]{:S(2)}) collective-permute-start(bf16[144,576]{1,0:T(8,128)(2,1)} %after.14), channel_id=1, source_target_pairs={{0,1},{1,0},{2,3},{3,2},{4,5},{5,4},{6,7},{7,6},{8,9},{9,8},{10,11... | collective-permute-start | bytes 497672 | tf_op jit(solution)/shard_map/ppermute | solution.py:722
  56.5 16.9 %collective-permute-start.21 = (bf16[144,576]{1,0:T(8,128)(2,1)}, bf16[144,576]{1,0:T(8,128)(2,1)}, u32[]{:S(2)}, u32[]{:S(2)}) collective-permute-start(bf16[144,576]{1,0:T(8,128)(2,1)} %after.15), channel_id=1, source_target_pairs={{0,2},{1,3},{2,0},{3,1},{4,6},{5,7},{6,4},{7,5},{8,10},{9,11},{10,... | collective-permute-start | bytes 497672 | tf_op jit(solution)/shard_map/ppermute | solution.py:722
  57.0 17.3 %collective-permute-start.22 = (bf16[144,576]{1,0:T(8,128)(2,1)}, bf16[144,576]{1,0:T(8,128)(2,1)}, u32[]{:S(2)}, u32[]{:S(2)}) collective-permute-start(bf16[144,576]{1,0:T(8,128)(2,1)} %after.16), channel_id=1, source_target_pairs={{0,3},{1,2},{2,1},{3,0},{4,7},{5,6},{6,5},{7,4},{8,11},{9,10},{10,... | collective-permute-start | bytes 497672 | tf_op jit(solution)/shard_map/ppermute | solution.py:722
  64.9 15.4 %all-to-all-start.1 = ((bf16[4,136,576]{2,1,0:T(8,128)(2,1)}), bf16[4,136,576]{2,1,0:T(8,128)(2,1)}, u32[]{:S(2)}, u32[]{:S(2)}) async-start(bf16[4,136,576]{2,1,0:T(8,128)(2,1)} %get-tuple-element.107), calls=%async_computation.1 | async-start | bytes 1392640 | tf_op jit(solution)/shard_map/all_to_all | solution.py:730
  69.3 20.9 %collective-permute-start.18 = (bf16[576,384]{1,0:T(8,128)(2,1)}, bf16[576,384]{1,0:T(8,128)(2,1)}, u32[]{:S(2)}, u32[]{:S(2)}) collective-permute-start(bf16[576,384]{1,0:T(8,128)(2,1)} %after.12), channel_id=1, source_target_pairs={{0,1},{1,0},{2,3},{3,2},{4,5},{5,4},{6,7},{7,6},{8,9},{9,8},{10,11... | collective-permute-start | bytes 1327112 | tf_op jit(solution)/shard_map/ppermute | solution.py:722
  70.0 20.2 %collective-permute-start.19 = (bf16[576,384]{1,0:T(8,128)(2,1)}, bf16[576,384]{1,0:T(8,128)(2,1)}, u32[]{:S(2)}, u32[]{:S(2)}) collective-permute-start(bf16[576,384]{1,0:T(8,128)(2,1)} %after.13.refs_3_), channel_id=1, source_target_pairs={{0,2},{1,3},{2,0},{3,1},{4,6},{5,7},{6,4},{7,5},{8,10},{9,11},{10,... | collective-permute-start | bytes 1327112 | tf_op jit(solution)/shard_map/ppermute | solution.py:722
  71.2 16.0 %collective-permute-start.15 = (bf16[144,1152]{1,0:T(8,128)(2,1)}, bf16[144,1152]{1,0:T(8,128)(2,1)}, u32[]{:S(2)}, u32[]{:S(2)}) collective-permute-start(bf16[144,1152]{1,0:T(8,128)(2,1)} %get-tuple-element.112), channel_id=1, source_target_pairs={{0,4},{4,0},{8,12},{12,8},{1,5},{5,1},{9,13},{13,9},{2,6},{6,2},{1... | collective-permute-start | bytes 995336 | tf_op jit(solution)/shard_map/ppermute | solution.py:722
  73.4 13.8 %collective-permute-start.16 = (bf16[144,1152]{1,0:T(8,128)(2,1)}, bf16[144,1152]{1,0:T(8,128)(2,1)}, u32[]{:S(2)}, u32[]{:S(2)}) collective-permute-start(bf16[144,1152]{1,0:T(8,128)(2,1)} %get-tuple-element.113), channel_id=1, source_target_pairs={{0,8},{4,12},{8,0},{12,4},{1,9},{5,13},{9,1},{13,5},{2,10},{6,14},... | collective-permute-start | bytes 995336 | tf_op jit(solution)/shard_map/ppermute | solution.py:722
  74.3 15.8 %collective-permute-start.17 = (bf16[144,1152]{1,0:T(8,128)(2,1)}, bf16[144,1152]{1,0:T(8,128)(2,1)}, u32[]{:S(2)}, u32[]{:S(2)}) collective-permute-start(bf16[144,1152]{1,0:T(8,128)(2,1)} %get-tuple-element.114), channel_id=1, source_target_pairs={{0,12},{4,8},{8,4},{12,0},{1,13},{5,9},{9,5},{13,1},{2,14},{6,10},... | collective-permute-start | bytes 995336 | tf_op jit(solution)/shard_map/ppermute | solution.py:722
  90.2 23.6 %all-to-all-start.2 = ((bf16[8,128,384]{2,1,0:T(8,128)(2,1)}), bf16[8,128,384]{2,1,0:T(8,128)(2,1)}, u32[]{:S(2)}, u32[]{:S(2)}) async-start(bf16[8,128,384]{2,1,0:T(8,128)(2,1)} %after.17), calls=%async_computation.2 | async-start | bytes 1572864 | tf_op jit(solution)/shard_map/all_to_all | solution.py:730
  94.4 6.4 %collective-permute-start.23 = (bf16[304,576]{1,0:T(8,128)(2,1)}, bf16[304,576]{1,0:T(8,128)(2,1)}, u32[]{:S(2)}, u32[]{:S(2)}) collective-permute-start(bf16[304,576]{1,0:T(8,128)(2,1)} %get-tuple-element.124), channel_id=1, source_target_pairs={{0,1},{1,0},{2,3},{3,2},{4,5},{5,4},{6,7},{7,6},{8,9},{9,8},{10,11... | collective-permute-start | bytes 1050632 | tf_op jit(solution)/shard_map/ppermute | solution.py:722
  94.8 12.2 %collective-permute-start.24 = (bf16[304,576]{1,0:T(8,128)(2,1)}, bf16[304,576]{1,0:T(8,128)(2,1)}, u32[]{:S(2)}, u32[]{:S(2)}) collective-permute-start(bf16[304,576]{1,0:T(8,128)(2,1)} %get-tuple-element.125), channel_id=1, source_target_pairs={{0,2},{1,3},{2,0},{3,1},{4,6},{5,7},{6,4},{7,5},{8,10},{9,11},{10,... | collective-permute-start | bytes 1050632 | tf_op jit(solution)/shard_map/ppermute | solution.py:722
  95.3 18.5 %collective-permute-start.25 = (bf16[304,576]{1,0:T(8,128)(2,1)}, bf16[304,576]{1,0:T(8,128)(2,1)}, u32[]{:S(2)}, u32[]{:S(2)}) collective-permute-start(bf16[304,576]{1,0:T(8,128)(2,1)} %get-tuple-element.126), channel_id=1, source_target_pairs={{0,3},{1,2},{2,1},{3,0},{4,7},{5,6},{6,5},{7,4},{8,11},{9,10},{10,... | collective-permute-start | bytes 1050632 | tf_op jit(solution)/shard_map/ppermute | solution.py:722
  98.5 18.8 %collective-permute-start.35 = (bf16[144,1152]{1,0:T(8,128)(2,1)}, bf16[144,1152]{1,0:T(8,128)(2,1)}, u32[]{:S(2)}, u32[]{:S(2)}) collective-permute-start(bf16[144,1152]{1,0:T(8,128)(2,1)} %add_pieces_body.3.refs_0_), channel_id=1, source_target_pairs={{0,16},{16,0},{1,17},{17,1},{2,18},{18,2},{3,19},{19,3},{4,20},{20... | collective-permute-start | bytes 995336 | tf_op jit(solution)/shard_map/ppermute | solution.py:718
  119.4 5.8 %copy-start = (bf16[136,576]{1,0:T(8,128)(2,1)S(1)}, bf16[136,576]{1,0:T(8,128)(2,1)}, u32[]{:S(2)}) copy-start(bf16[136,576]{1,0:T(8,128)(2,1)} %get-tuple-element.132) | copy-start | bytes 470020
  119.4 28.5 %all-to-all-start.5 = ((bf16[8,144,384]{2,1,0:T(8,128)(2,1)}), bf16[8,144,384]{2,1,0:T(8,128)(2,1)}, u32[]{:S(2)}, u32[]{:S(2)}) async-start(bf16[8,144,384]{2,1,0:T(8,128)(2,1)} %bitcast.28), calls=%async_computation.5 | async-start | bytes 1769472 | tf_op jit(solution)/shard_map/all_to_all | solution.py:730
  123.7 2.3 collective-permute-start.27
  124.6 7.4 %collective-permute-start.28 = (bf16[136,576]{1,0:T(8,128)(2,1)S(1)}, bf16[136,576]{1,0:T(8,128)(2,1)}, u32[]{:S(2)}, u32[]{:S(2)}) collective-permute-start(bf16[136,576]{1,0:T(8,128)(2,1)S(1)} %copy-done.1), channel_id=1, source_target_pairs={{0,2},{1,3},{2,0},{3,1},{4,6},{5,7},{6,4},{7,5},{8,10},{9,11},{10,... | collective-permute-start | bytes 470024 | tf_op jit(solution)/shard_map/ppermute | solution.py:722
  125.2 8.8 %collective-permute-start.29 = (bf16[136,576]{1,0:T(8,128)(2,1)S(1)}, bf16[136,576]{1,0:T(8,128)(2,1)}, u32[]{:S(2)}, u32[]{:S(2)}) collective-permute-start(bf16[136,576]{1,0:T(8,128)(2,1)S(1)} %copy-done), channel_id=1, source_target_pairs={{0,3},{1,2},{2,1},{3,0},{4,7},{5,6},{6,5},{7,4},{8,11},{9,10},{10,... | collective-permute-start | bytes 470024 | tf_op jit(solution)/shard_map/ppermute | solution.py:722
  137.2 10.7 %collective-permute-start.30 = (bf16[152,576]{1,0:T(8,128)(2,1)}, bf16[152,576]{1,0:T(8,128)(2,1)}, u32[]{:S(2)}, u32[]{:S(2)}) collective-permute-start(bf16[152,576]{1,0:T(8,128)(2,1)} %get-tuple-element.134), channel_id=1, source_target_pairs={{0,4},{4,0},{8,12},{12,8},{1,5},{5,1},{9,13},{13,9},{2,6},{6,2},{1... | collective-permute-start | bytes 525320 | tf_op jit(solution)/shard_map/ppermute | solution.py:722
  139.0 17.9 %collective-permute-start.34 = (bf16[576,384]{1,0:T(8,128)(2,1)}, bf16[576,384]{1,0:T(8,128)(2,1)}, u32[]{:S(2)}, u32[]{:S(2)}) collective-permute-start(bf16[576,384]{1,0:T(8,128)(2,1)} %after.12), channel_id=1, source_target_pairs={{0,3},{1,2},{2,1},{3,0},{4,7},{5,6},{6,5},{7,4},{8,11},{9,10},{10,... | collective-permute-start | bytes 1327112 | tf_op jit(solution)/shard_map/ppermute | solution.py:722
  139.9 9.6 %collective-permute-start.31 = (bf16[152,576]{1,0:T(8,128)(2,1)}, bf16[152,576]{1,0:T(8,128)(2,1)}, u32[]{:S(2)}, u32[]{:S(2)}) collective-permute-start(bf16[152,576]{1,0:T(8,128)(2,1)} %get-tuple-element.135), channel_id=1, source_target_pairs={{0,8},{4,12},{8,0},{12,4},{1,9},{5,13},{9,1},{13,5},{2,10},{6,14},... | collective-permute-start | bytes 525320 | tf_op jit(solution)/shard_map/ppermute | solution.py:722
  141.1 9.7 %collective-permute-start.32 = (bf16[152,576]{1,0:T(8,128)(2,1)}, bf16[152,576]{1,0:T(8,128)(2,1)}, u32[]{:S(2)}, u32[]{:S(2)}) collective-permute-start(bf16[152,576]{1,0:T(8,128)(2,1)} %get-tuple-element.136), channel_id=1, source_target_pairs={{0,12},{4,8},{8,4},{12,0},{1,13},{5,9},{9,5},{13,1},{2,14},{6,10},... | collective-permute-start | bytes 525320 | tf_op jit(solution)/shard_map/ppermute | solution.py:722
  144.1 11.1 %collective-permute-start.26 = (bf16[2,576,128]{2,1,0:T(8,128)(2,1)}, bf16[2,576,128]{2,1,0:T(8,128)(2,1)}, u32[]{:S(2)}, u32[]{:S(2)}) collective-permute-start(bf16[2,576,128]{2,1,0:T(8,128)(2,1)} %finish_body.1.refs_4_), channel_id=1, source_target_pairs={{0,0},{1,16},{2,2},{3,18},{4,4},{5,20},{6,6},{7,22},{8,8},{9,24},{... | collective-permute-start | bytes 884744 | tf_op jit(solution)/shard_map/ppermute | solution.py:907
  147.9 23.2 %collective-permute-start.36 = (bf16[4,2,144,384]{3,2,1,0:T(8,128)(2,1)}, bf16[4,2,144,384]{3,2,1,0:T(8,128)(2,1)}, u32[]{:S(2)}, u32[]{:S(2)}) collective-permute-start(bf16[4,2,144,384]{3,2,1,0:T(8,128)(2,1)} %after.18.refs_1_), channel_id=1, source_target_pairs={{0,2},{2,0},{1,3},{3,1},{4,6},{6,4},{5,7},{7,5},{8,10},{10,8},{9,1... | collective-permute-start | bytes 2654216 | tf_op jit(solution)/shard_map/ppermute | solution.py:718
  152.8 12.1 %collective-permute-start.33 = (bf16[152,576]{1,0:T(8,128)(2,1)}, bf16[152,576]{1,0:T(8,128)(2,1)}, u32[]{:S(2)}, u32[]{:S(2)}) collective-permute-start(bf16[152,576]{1,0:T(8,128)(2,1)} %add_pieces_body.2.refs_1_.refs_0_), channel_id=1, source_target_pairs={{0,16},{16,0},{1,17},{17,1},{2,18},{18,2},{3,19},{19,3},{4,20},{20... | collective-permute-start | bytes 525320 | tf_op jit(solution)/shard_map/ppermute | solution.py:718
  166.9 33.5 %all-to-all-start.3 = ((bf16[4,144,576]{2,1,0:T(8,128)(2,1)}), bf16[4,144,576]{2,1,0:T(8,128)(2,1)}, u32[]{:S(2)}, u32[]{:S(2)}) async-start(bf16[4,144,576]{2,1,0:T(8,128)(2,1)} %get-tuple-element.139.refs_7_), calls=%async_computation.3 | async-start | bytes 1474560 | tf_op jit(solution)/shard_map/all_to_all | solution.py:730
  196.5 25.7 %collective-permute-start.37 = (bf16[1160,384]{1,0:T(8,128)(2,1)}, bf16[1160,384]{1,0:T(8,128)(2,1)}, u32[]{:S(2)}, u32[]{:S(2)}) collective-permute-start(bf16[1160,384]{1,0:T(8,128)(2,1)} %get-tuple-element.143.refs_6_.refs_1_), channel_id=1, source_target_pairs={{0,4},{4,0},{2,6},{6,2},{8,12},{12,8},{10,14},{14,10},{16,20},{20,... | collective-permute-start | bytes 2672648 | tf_op jit(solution)/shard_map/ppermute | solution.py:928
  200.3 21.8 %all-to-all-start.4 = ((bf16[4,144,576]{2,1,0:T(8,128)(2,1)}), bf16[4,144,576]{2,1,0:T(8,128)(2,1)}, u32[]{:S(2)}, u32[]{:S(2)}) async-start(bf16[4,144,576]{2,1,0:T(8,128)(2,1)} %all-to-all-done.3.refs_1_), calls=%async_computation.4 | async-start | bytes 1474560 | tf_op jit(solution)/shard_map/all_to_all | solution.py:730
  204.6 21.8 %collective-permute-start.38 = (bf16[1160,384]{1,0:T(8,128)(2,1)}, bf16[1160,384]{1,0:T(8,128)(2,1)}, u32[]{:S(2)}, u32[]{:S(2)}) collective-permute-start(bf16[1160,384]{1,0:T(8,128)(2,1)} %get-tuple-element.148), channel_id=1, source_target_pairs={{0,1},{1,0},{2,3},{3,2},{4,5},{5,4},{6,7},{7,6},{8,9},{9,8},{10,11... | collective-permute-start | bytes 2672648 | tf_op jit(solution)/shard_map/ppermute | solution.py:718
  205.0 21.4 %collective-permute-start.39 = (bf16[1160,384]{1,0:T(8,128)(2,1)}, bf16[1160,384]{1,0:T(8,128)(2,1)}, u32[]{:S(2)}, u32[]{:S(2)}) collective-permute-start(bf16[1160,384]{1,0:T(8,128)(2,1)} %get-tuple-element.148), channel_id=1, source_target_pairs={{0,5},{4,1},{2,7},{6,3},{8,13},{12,9},{10,15},{14,11},{16,21},{20,... | collective-permute-start | bytes 2672648 | tf_op jit(solution)/shard_map/ppermute | solution.py:929
  222.2 15.8 %all-to-all-start.6 = ((bf16[4,152,576]{2,1,0:T(8,128)(2,1)}), bf16[4,152,576]{2,1,0:T(8,128)(2,1)}, u32[]{:S(2)}, u32[]{:S(2)}) async-start(bf16[4,152,576]{2,1,0:T(8,128)(2,1)} %after.19.refs_7_.refs_9_), calls=%async_computation.6 | async-start | bytes 1556480 | tf_op jit(solution)/shard_map/all_to_all | solution.py:730
  (2 other events, 9.7 us)
